TPU v7x, 512 devices: a whole 4x4x16 slice. The times are simulated.
512 devices in a mesh: gx: 32 (over z, core), gy: 16 (over x, y).
Axes of the slice: x: 4, y: 4, z: 16, core: 2. Of those that a mesh axis runs over, the one named last changes fastest.
Arguments:
- leaf_moments: bfloat16 [131072, 256], P(('gx', 'gy')), may hold values from -6 to 6
- leaf_src: int32 [131072, 32], P(('gx', 'gy')), may hold values from -1 to 4223, as said below
- leaf_cls: int32 [131072, 32], P(('gx', 'gy')), may hold values from -1 to 7
- send_rows: int32 [32, 16, 16, 8], P('gx'), may hold values from 0 to 255, as said below
- send_count: int32 [32, 16, 16], P('gx'), may hold values from 0 to 8, as said below
- par_src: int32 [16384, 32], P(('gx', 'gy')), may hold values from -1 to 16383, as said below
- par_cls: int32 [16384, 32], P(('gx', 'gy')), may hold values from -1 to 7
- top_src: int32 [2048, 32], P('gx'), may hold values from -1 to 63, as said below
- top_cls: int32 [2048, 32], P('gx'), may hold values from -1 to 7
- points: float32 [4096, 3, 128], P(('gx', 'gy')), may hold values from 0 to 1
- charges: float32 [4096, 128], P(('gx', 'gy')), may hold values from -0.18 to 0.18
- near_src: int32 [4096, 8], P(('gx', 'gy')), may hold values from -1 to 4095, as said below
- m2m_ops: bfloat16 [8, 256, 256], replicated, may hold values from -0.125 to 0.125
- m2l_ops: bfloat16 [8, 256, 256], replicated, may hold values from -0.0625 to 0.0625
- l2l_ops: bfloat16 [8, 256, 256], replicated, may hold values from -0.375 to 0.375
Outputs:
- leaf_local: bfloat16 [131072, 256], P(('gx', 'gy'))
- near_potential: float32 [4096, 128], P(('gx', 'gy'))
Inputs may be any that keep to these rules, and one draw needn't show every extreme that they name: leaf_src and leaf_cls are -1 in the same slots; a list's used slots come first, at least 16 of them. A value below 4096 names a leaf of the target's own device; a larger one names a sender other than the target's own device. The first send_count[g, s, p] entries of send_rows[g, s, p] are distinct. send_count[g, s, s] = 0; for each device some sender fills all 8 slots. par_src and par_cls are -1 in the same slots; a source parent lies on a device with the same gy index whose gx index differs by at most one. top_src and top_cls are -1 in the same slots. `near_src`: a tile of device d (linear index over gx then gy) lists tiles of global numbers d * 8 - 4 to (d + 1) * 8 + 3, its own tile in slot 0.
All inputs are finite; a program needn't handle non-finite values.
Results may differ from a plain program's by a relative error of at most 0.015.
Values may be sent and summed in bfloat16 or wider, within the bound.
No kernel may reach another device: no remote copies, remote signals or barrier semaphores. Data moves between devices by JAX's collectives and lax.ppermute only.
A program may use at most 64 MiB of HBM per device.

v0:
```python
import jax
import jax.numpy as jnp
from jax import lax
from jax.sharding import PartitionSpec as P

HALO_T = 4


SOFTENING = 0.05


def extended(shard, sides, width):
    for axis, dim in sides:
        size, length = (lax.axis_size(axis), shard.shape[dim])
        up = [(i, (i + 1) % size) for i in range(size - 1)]
        down = [(j, i) for i, j in up]
        last = lax.slice_in_dim(shard, length - width, length, axis=dim)
        first = lax.slice_in_dim(shard, 0, width, axis=dim)
        before = lax.ppermute(last, axis, up)
        after = lax.ppermute(first, axis, down)
        shard = jnp.concatenate([before, shard, after], axis=dim)
    return shard


def passed_along(block, axis, distance):
    devices = range(lax.axis_size(axis))
    route = [(i - distance, i) for i in devices if i - distance in devices]
    return lax.ppermute(block, axis, route)


def upward(moments, m2m_ops):
    grouped = moments.reshape(-1, 8, moments.shape[1])
    return jnp.einsum("ncp,cpq->nq", grouped, m2m_ops, preferred_element_type=jnp.float32).astype(
        jnp.bfloat16
    )


def downward(locals_in, l2l_ops):
    spread = jnp.einsum("np,cpq->ncq", locals_in, l2l_ops, preferred_element_type=jnp.float32)
    return spread.reshape(-1, locals_in.shape[1])


def translate(source_bank, row_ids, classes, m2l_ops):
    usable = row_ids >= 0
    picked = jnp.take(source_bank, jnp.clip(row_ids, 0, source_bank.shape[0] - 1), axis=0)
    onehot = ((classes[..., None] == jnp.arange(m2l_ops.shape[0])) & usable[..., None]).astype(
        jnp.bfloat16
    )
    buckets = jnp.einsum("ljk,ljp->klp", onehot, picked, preferred_element_type=jnp.float32).astype(
        jnp.bfloat16
    )
    return jnp.einsum("klp,kpq->lq", buckets, m2l_ops, preferred_element_type=jnp.float32)


def tile_potential(targets, sources):
    differ_x = targets[:, 0, :, None] - sources[:, 0, None, :]
    differ_y = targets[:, 1, :, None] - sources[:, 1, None, :]
    differ_z = targets[:, 2, :, None] - sources[:, 2, None, :]
    distance_sq = differ_x * differ_x + differ_y * differ_y + differ_z * differ_z
    return jnp.sum(sources[:, 3, None, :] * lax.rsqrt(distance_sq + SOFTENING * SOFTENING), axis=-1)


def per_device(
    leaf_moments,
    leaf_src,
    leaf_cls,
    send_rows,
    send_count,
    par_src,
    par_cls,
    top_src,
    top_cls,
    points,
    charges,
    near_src,
    m2m_ops,
    m2l_ops,
    l2l_ops,
):
    groups = lax.axis_size("gy")
    own_index = lax.axis_index("gy")
    row_index = lax.axis_index("gx")
    device = row_index * groups + own_index
    leaf_dev, breadth = leaf_moments.shape
    parents = upward(leaf_moments, m2m_ops)
    top_moments = upward(parents, m2m_ops)
    top_dev = top_moments.shape[0]
    par_dev = parents.shape[0]
    top_bank = lax.all_gather(top_moments, "gy", axis=0, tiled=True)
    own_rows = lax.dynamic_slice_in_dim(top_src, own_index * top_dev, top_dev, 0)
    own_classes = lax.dynamic_slice_in_dim(top_cls, own_index * top_dev, top_dev, 0)
    top_field = translate(top_bank, own_rows, own_classes, m2l_ops)
    top_local = top_field.astype(jnp.bfloat16)
    rim_bank = extended(parents, (("gx", 0),), par_dev)
    source_device = par_src // par_dev
    placed = (source_device - device) // groups + 1
    par_rows = jnp.where(par_src >= 0, placed * par_dev + par_src % par_dev, -1)
    parent_field = translate(rim_bank, par_rows, par_cls, m2l_ops)
    parent_local = (parent_field + downward(top_local, l2l_ops)).astype(jnp.bfloat16)
    send_table = send_rows[0]
    counts = send_count[0]
    slot_count = send_table.shape[2]
    row_group = groups * leaf_dev
    remote = leaf_src >= row_group
    offset = jnp.clip(leaf_src - row_group, 0, groups * slot_count - 1)
    sender = offset // slot_count
    slot = offset % slot_count
    live = slot < counts[sender, own_index]
    leaf_bank = lax.all_gather(leaf_moments, "gy", axis=0, tiled=True)
    remote_rows = sender * leaf_dev + send_table[sender, own_index, slot]
    chosen = jnp.where(remote, jnp.where(live, remote_rows, -1), leaf_src)
    leaf_rows = jnp.where(leaf_src < 0, -1, chosen)
    leaf_field = translate(leaf_bank, leaf_rows, leaf_cls, m2l_ops)
    leaf_local = (leaf_field + downward(parent_local, l2l_ops)).astype(jnp.bfloat16)
    packed = jnp.concatenate([points, charges[:, None, :]], axis=1)
    tile_dev = packed.shape[0]
    from_below = passed_along(packed[tile_dev - HALO_T :], ("gx", "gy"), 1)
    from_above = passed_along(packed[:HALO_T], ("gx", "gy"), -1)
    tile_bank = jnp.concatenate([from_below, packed, from_above], axis=0)
    bank_tiles = tile_bank.shape[0]
    tile_rows = jnp.where(near_src >= 0, near_src - (device * tile_dev - HALO_T), -1)
    weights = jnp.sum(
        (tile_rows[:, :, None] == jnp.arange(bank_tiles)[None, None, :]).astype(jnp.float32), axis=1
    )

    def accumulate(source_index, total):
        source_tile = lax.dynamic_index_in_dim(tile_bank, source_index, 0, keepdims=True)
        factor = lax.dynamic_index_in_dim(weights, source_index, 1, keepdims=False)
        return total + factor[:, None] * tile_potential(points, source_tile)

    near_total = lax.fori_loop(0, bank_tiles, accumulate, jnp.zeros(charges.shape, jnp.float32))
    return (leaf_local, near_total)


def solution(mesh):
    return jax.shard_map(
        per_device,
        mesh=mesh,
        in_specs=(
            P(("gx", "gy"), None),
            P(("gx", "gy"), None),
            P(("gx", "gy"), None),
            P("gx", None, None, None),
            P("gx", None, None),
            P(("gx", "gy"), None),
            P(("gx", "gy"), None),
            P("gx", None),
            P("gx", None),
            P(("gx", "gy"), None, None),
            P(("gx", "gy"), None),
            P(("gx", "gy"), None),
            P(),
            P(),
            P(),
        ),
        out_specs=(P(("gx", "gy"), None), P(("gx", "gy"), None)),
        check_vma=False,
    )
```

profile of v0, /device:TPU:390, one launch (start us, length us, event | category | flops | bytes accessed | tf_op | source)
XLA Modules:
  0.0 226.0 jit_solution(5764973480112348560)
XLA Ops:
  7.2 0.7 all-gather.3.cloned.1.call-update
  7.9 1.6 fusion.14
  9.5 3.6 %collective-permute-start.1 = (bf16[32,256]{1,0:T(8,128)(2,1)S(1)}, bf16[32,256]{1,0:T(8,128)(2,1)}, u32[]{:S(2)}, u32[]{:S(2)}) collective-permute-start(bf16[32,256]{1,0:T(8,128)(2,1)S(1)} %fusion.14), channel_id=1, source_target_pairs={{16,0},{32,16},{48,32},{64,48},{80,64},{96,80},{112,96},{128,112},... | collective-permute-start | bytes 49160 | tf_op jit(solution)/shard_map/ppermute | solution.py:20
  13.1 1.9 collective-permute-start
  15.0 0.7 copy.75
  15.7 1.3 fusion.67
  17.0 5.2 %collective-permute-start.3 = (f32[4,4,128]{2,1,0:T(4,128)}, f32[4,4,128]{2,1,0:T(4,128)}, u32[]{:S(2)}, u32[]{:S(2)}) collective-permute-start(f32[4,4,128]{2,1,0:T(4,128)} %get-tuple-element.146), channel_id=1, source_target_pairs={{1,0},{2,1},{3,2},{4,3},{5,4},{6,5},{7,6},{8,7},{9,8},{10,9},{11,1... | collective-permute-start | bytes 24584 | tf_op jit(solution)/shard_map/ppermute | solution.py:28
  22.2 1.9 collective-permute-start.2
  24.1 0.9 copy.59
  25.0 0.2 fusion.38
  25.2 0.1 reshape.51
  25.3 50.4 %gather_fusion.1 = s32[8192]{0:T(1024)S(1)} fusion(s32[16,16,8]{1,2,0:T(8,128)S(1)} %bitcast.95, s32[8192]{0:T(1024)S(1)} %reshape.51), kind=kCustom, calls=%fused_computation.1 | custom fusion | bytes 163840 | tf_op jit(solution)/shard_map/gather | solution.py:110
  75.7 0.1 reshape.54
  75.8 0.1 reshape.45
  75.9 0.5 copy-done.1
  76.4 52.9 %gather_fusion = s32[8192]{0:T(1024)S(1)} fusion(s32[16,16]{1,0:T(8,128)S(1)} %bitcast.94, s32[8192]{0:T(1024)S(1)} %reshape.45), kind=kCustom, calls=%fused_computation | custom fusion | bytes 131072 | tf_op jit(solution)/shard_map/gather | solution.py:108
  129.3 0.7 reshape.48
  130.1 1.1 broadcast_compare_fusion
  131.3 0.8 broadcast_compare_fusion.1
  132.1 0.1 reshape.59
  132.3 0.2 fusion.21
  132.5 25.0 %all-gather = bf16[16,4,256]{2,1,0:T(4,128)(2,1)S(1)} all-gather(bf16[1,4,256]{2,1,0:T(4,128)(2,1)S(1)} %fusion.21), channel_id=1, replica_groups=mesh['gx'=32,'gy'=16] {'gy'}, dimensions={0}, use_global_device_ids=true | all-gather | bytes 34816 | tf_op jit(solution)/shard_map/all_gather | solution.py:89
  157.6 0.8 compare_and_fusion.1
  158.4 0.1 copy.69
  158.5 0.1 reshape.75
  158.6 0.1 copy.67
  158.7 0.8 constant_dynamic-slice_fusion.1
  159.5 0.1 copy.70
  159.5 0.1 copy.71
  159.6 0.9 gather_fusion.4
  160.5 0.7 subtract_select_fusion
  161.2 0.2 fusion.16
  161.4 0.7 fusion.26
  162.1 0.1 convert_reduce_fusion
  162.3 0.1 copy.63
  162.4 0.7 pad_maximum_fusion.1
  163.2 12.1 %while.14 = (s32[]{:T(128)}, f32[8,128]{1,0:T(8,128)S(1)}, f32[8,16]{0,1:T(8,128)S(1)}, f32[16,4,128]{2,1,0:T(4,128)S(1)}, f32[8,3,128]{2,0,1:T(8,128)S(1)}, /*index=5*/s32[]{:T(128)}, s32[]{:T(128)}) while((s32[]{:T(128)}, f32[8,128]{1,0:T(8,128)S(1)}, f32[8,16]{0,1:T(8,128)S(1)}, f32[16,4,128]{2,1,0:T(4,128)S(1)}, ...), condition=%wide.region_3.4_spmd.clone, body=%wide.region_1.3_spmd.clone.sunk | while | flops 1443843 | bytes 63687 | solution.py:131
  163.2 0.6 multiply_reduce_fusion.2
  163.9 0.1 select_add_fusion.2
  164.0 0.6 multiply_reduce_fusion.2
  164.7 0.1 select_add_fusion.2
  164.8 0.6 multiply_reduce_fusion.2
  165.5 0.6 multiply_reduce_fusion.2
  166.3 0.6 multiply_reduce_fusion.2
  167.0 0.6 multiply_reduce_fusion.2
  167.7 0.1 select_add_fusion.2
  167.8 0.6 multiply_reduce_fusion.2
  168.4 0.1 select_add_fusion.2
  168.5 0.6 multiply_reduce_fusion.2
  169.3 0.6 multiply_reduce_fusion.2
  170.0 0.6 multiply_reduce_fusion.2
  170.8 0.6 multiply_reduce_fusion.2
  171.5 0.6 multiply_reduce_fusion.2
  172.3 0.6 multiply_reduce_fusion.2
  173.1 0.6 multiply_reduce_fusion.2
  173.8 0.6 multiply_reduce_fusion.2
  174.6 0.6 multiply_reduce_fusion.2
  175.3 0.7 pad_maximum_fusion
  176.1 3.9 %gather_fusion.3 = bf16[1024,256]{1,0:T(8,128)(2,1)S(1)} fusion(bf16[96,256]{1,0:T(8,128)(2,1)S(1)} %pad_maximum_fusion, s32[1024]{0:T(1024)S(1)} %broadcast_clamp_fusion.1), kind=kCustom, calls=%fused_computation.3 | custom fusion | bytes 1052672 | tf_op jit(solution)/shard_map/jit(_take)/gather | solution.py:45
  180.0 0.3 fusion.12
  180.3 0.7 fusion.25
  181.1 32.9 %gather_fusion.2 = bf16[8192,256]{1,0:T(8,128)(2,1)} fusion(bf16[4096,256]{1,0:T(8,128)(2,1)} %all-gather.3.cloned.1.call-done, s32[8192]{0:T(1024)S(1)} %broadcast_clamp_fusion), kind=kCustom, calls=%fused_computation.2 | custom fusion | bytes 8421376 | tf_op jit(solution)/shard_map/jit(_take)/gather | solution.py:45
  214.0 3.9 %fusion.7 = bf16[8,256,256]{2,0,1:T(8,128)(2,1)S(1)} fusion(bf16[256,32,256]{2,1,0:T(8,128)(2,1)} %bitcast.96, pred[256,32]{1,0:T(8,128)(4,1)S(1)} %compare_and_fusion, s32[256,32]{1,0:T(8,128)S(1)} %copy.63, pred[256,32]{1,0:T(8,128)(4,1)S(1)} %get-tuple-element.134), kind=kOutput, calls=%fused_computation.21 | convolution fusion | flops 36306944 | bytes 5292032 | tf_op jit(solution)/shard_map/ljk,ljp->klp/dot_general | solution.py:49
  217.9 1.2 fusion.11
  (110 shorter events, 1.7 us)
Async XLA Ops:
  7.2 154.2 %copy-start = (bf16[8,256,256]{2,1,0:T(8,128)(2,1)S(1)}, bf16[8,256,256]{2,1,0:T(8,128)(2,1)}, u32[]{:S(2)}) copy-start(bf16[8,256,256]{2,1,0:T(8,128)(2,1)} %param.30) | copy-start | bytes 3145732
  7.2 18.1 %copy-start.2 = (s32[1,16,16,8]{2,3,1,0:T(8,128)S(1)}, s32[1,16,16,8]{2,3,1,0:T(8,128)}, u32[]{:S(2)}) copy-start(s32[1,16,16,8]{2,3,1,0:T(8,128)} %param.20) | copy-start | bytes 24580
  7.2 173.9 %all-gather.3.cloned.1.call-start = ((), (), s32[]{:S(2)}) async-start(), calls=%async_computation | async-start | bytes 2228224 | tf_op jit(solution)/shard_map/all_gather | solution.py:109
  9.5 165.8 %collective-permute-start.1 = (bf16[32,256]{1,0:T(8,128)(2,1)S(1)}, bf16[32,256]{1,0:T(8,128)(2,1)}, u32[]{:S(2)}, u32[]{:S(2)}) collective-permute-start(bf16[32,256]{1,0:T(8,128)(2,1)S(1)} %fusion.14), channel_id=1, source_target_pairs={{16,0},{32,16},{48,32},{64,48},{80,64},{96,80},{112,96},{128,112},... | collective-permute-start | bytes 49160 | tf_op jit(solution)/shard_map/ppermute | solution.py:20
  13.1 162.3 %collective-permute-start = (bf16[32,256]{1,0:T(8,128)(2,1)S(1)}, bf16[32,256]{1,0:T(8,128)(2,1)}, u32[]{:S(2)}, u32[]{:S(2)}) collective-permute-start(bf16[32,256]{1,0:T(8,128)(2,1)S(1)} %fusion.14), channel_id=1, source_target_pairs={{0,16},{16,32},{32,48},{48,64},{64,80},{80,96},{96,112},{112,128},... | collective-permute-start | bytes 49160 | tf_op jit(solution)/shard_map/ppermute | solution.py:19
  17.0 145.4 %collective-permute-start.3 = (f32[4,4,128]{2,1,0:T(4,128)}, f32[4,4,128]{2,1,0:T(4,128)}, u32[]{:S(2)}, u32[]{:S(2)}) collective-permute-start(f32[4,4,128]{2,1,0:T(4,128)} %get-tuple-element.146), channel_id=1, source_target_pairs={{1,0},{2,1},{3,2},{4,3},{5,4},{6,5},{7,6},{8,7},{9,8},{10,9},{11,1... | collective-permute-start | bytes 24584 | tf_op jit(solution)/shard_map/ppermute | solution.py:28
  22.2 140.2 %collective-permute-start.2 = (f32[4,4,128]{2,1,0:T(4,128)}, f32[4,4,128]{2,1,0:T(4,128)}, u32[]{:S(2)}, u32[]{:S(2)}) collective-permute-start(f32[4,4,128]{2,1,0:T(4,128)} %get-tuple-element.145), channel_id=1, source_target_pairs={{0,1},{1,2},{2,3},{3,4},{4,5},{5,6},{6,7},{7,8},{8,9},{9,10},{10,1... | collective-permute-start | bytes 24584 | tf_op jit(solution)/shard_map/ppermute | solution.py:28
  75.7 0.7 copy-start.1
  76.4 55.9 %copy-start.3 = (bf16[8,256,256]{2,1,0:T(8,128)(2,1)S(1)}, bf16[8,256,256]{2,1,0:T(8,128)(2,1)}, u32[]{:S(2)}) copy-start(bf16[8,256,256]{2,1,0:T(8,128)(2,1)} %param.29) | copy-start | bytes 3145732
  76.4 85.0 %copy-start.4 = (bf16[8,256,256]{2,1,0:T(8,128)(2,1)S(1)}, bf16[8,256,256]{2,1,0:T(8,128)(2,1)}, u32[]{:S(2)}) copy-start(bf16[8,256,256]{2,1,0:T(8,128)(2,1)} %param.31) | copy-start | bytes 3145732
  129.3 32.9 %copy-start.7 = (s32[256,32]{0,1:T(8,128)S(1)}, s32[256,32]{0,1:T(8,128)}, u32[]{:S(2)}) copy-start(s32[256,32]{0,1:T(8,128)} %param.19) | copy-start | bytes 98308
  129.3 33.9 %copy-start.5 = (f32[8,3,128]{2,0,1:T(8,128)S(1)}, f32[8,3,128]{2,0,1:T(8,128)}, u32[]{:S(2)}) copy-start(f32[8,3,128]{2,0,1:T(8,128)} %param.26) | copy-start | bytes 36868
  161.4 18.6 %copy-start.8 = (s32[32,32]{1,0:T(8,128)S(1)}, s32[32,32]{1,0:T(8,128)}, u32[]{:S(2)}) copy-start(s32[32,32]{1,0:T(8,128)} %param.23) | copy-start | bytes 12292
  175.3 5.8 %copy-start.6 = (f32[8,128]{1,0:T(8,128)}, f32[8,128]{1,0:T(8,128)S(1)}, u32[]{:S(2)}) copy-start(f32[8,128]{1,0:T(8,128)S(1)} %get-tuple-element.95) | copy-start | bytes 12292
Sparse Core Ops, SparseCore 0:
  11.0 59.9 all-gather.2
where the time goes:
time: 227 us; the launch traced here: 226 us
  local copies, waits for them, and re-layouts  146 us (64%)
  blocking collectives  25 us (11%)
  other arithmetic  18 us (8%)
  between operations  14.3 us (6%)
  starting transfers between devices  12.6 us (6%)
  matrix products  8.87 us (4%)
    gather x2, local copies, waits for them, and re-layouts, per_device(): live = slot < counts[sender, own_index]  53.6 us
    gather x2, local copies, waits for them, and re-layouts, per_device(): remote_rows = sender * leaf_dev + send_table[sender, own_index, slot]  50.5 us
    gather x3, local copies, waits for them, and re-layouts, translate(): jnp.take(source_bank, jnp.clip(row_ids, 0, source_bank.shape[0] - 1), axi...  37.7 us
    all_gather x1, blocking collectives, per_device(): top_bank = lax.all_gather(top_moments, 'gy', axis=0, tiled=True)  25 us
    reduce_sum x16, other arithmetic, tile_potential(): jnp.sum(sources[:, 3, None, :] * lax.rsqrt(distance_sq + SOFTENING * SOFT...  10.3 us
    ppermute x2, starting transfers between devices, passed_along(): return lax.ppermute(block, axis, route)  7.1 us
  transfers between devices with their start and end apart: 5, of which 0 were waited for; matrix products, arithmetic and copies ran while one was open for 59% of the time, Pallas kernels for 0%

commit v1 on v0

v1 whole, which is shorter than its diff:
```python
import functools

import jax
import jax.numpy as jnp
from jax import lax
from jax.experimental import pallas as pl
from jax.experimental.pallas import tpu as pltpu
from jax.sharding import PartitionSpec as P

F32 = jnp.float32
BF16 = jnp.bfloat16
I32 = jnp.int32

HALO_T = 4
SOFTENING = 0.05
VMEM_LIMIT = 24 * 1024 * 1024


def iota(shape, dim):
    return lax.broadcasted_iota(I32, shape, dim)


def dot(a, b):
    return jnp.dot(a, b, preferred_element_type=F32)


def dot_tn(a, b):
    return lax.dot_general(a, b, (((0,), (0,)), ((), ())), preferred_element_type=F32)


def pack_kernel(leaf_ref, m2m_ref, rows_ref, count_ref, send_ref, parents_ref):
    me = lax.axis_index("gy")
    leaf = leaf_ref[...]
    counts = jnp.broadcast_to(count_ref[pl.ds(me, 1), :].astype(F32), (16, 16))
    counts = jnp.sum(jnp.where(iota((16, 16), 0) == iota((16, 16), 1), counts, 0.0), axis=1, keepdims=True)
    table = rows_ref[me].astype(F32)
    table = jnp.where(iota((16, 8), 1).astype(F32) < counts, table, -1.0).astype(BF16)
    repeat = (iota((128, 16), 0) // 8 == iota((128, 16), 1)).astype(F32).astype(BF16)
    spread = dot(repeat, table)
    column = jnp.sum(
        jnp.where(iota((128, 8), 0) % 8 == iota((128, 8), 1), spread, 0.0), axis=1, keepdims=True
    )
    pick = (iota((128, 256), 1).astype(F32) == column).astype(F32).astype(BF16)
    sent = dot(pick, leaf)
    order = (iota((256, 256), 1) == 8 * (iota((256, 256), 0) % 32) + iota((256, 256), 0) // 32)
    by_child = dot(order.astype(F32).astype(BF16), leaf).astype(BF16)
    parents = dot(by_child[0:32], m2m_ref[0])
    for c in range(1, 8):
        parents += dot(by_child[32 * c : 32 * c + 32], m2m_ref[c])
    parents = parents.astype(BF16)
    parents_ref[...] = parents
    row = iota((64, 32), 0)
    order = (iota((64, 32), 1) == 8 * (row % 8) + row // 8) & (row % 8 < 4)
    by_child = dot(order.astype(F32).astype(BF16), parents)
    top = dot(by_child[0:8].astype(BF16), m2m_ref[0])
    for c in range(1, 8):
        top += dot(by_child[8 * c : 8 * c + 8].astype(BF16), m2m_ref[c])
    for p in range(16):
        send_ref[p] = jnp.concatenate([sent[8 * p : 8 * p + 8], top], axis=0).astype(BF16)


def pack(leaf, m2m, rows, count):
    return pl.pallas_call(
        pack_kernel,
        out_shape=(
            jax.ShapeDtypeStruct((16, 16, 256), BF16),
            jax.ShapeDtypeStruct((32, 256), BF16),
        ),
        compiler_params=pltpu.CompilerParams(vmem_limit_bytes=VMEM_LIMIT),
        cost_estimate=pl.CostEstimate(flops=200_000_000, bytes_accessed=1_500_000, transcendentals=0),
        name="pack",
    )(leaf, m2m, rows, count)


def fields(src_ref, val_ref, lanes, base, rows):
    at = iota((rows, 128), 0)
    even = jnp.zeros((rows, 128), I32)
    odd = jnp.zeros((rows, 128), I32)
    for first, last in ((0, 15), (15, 30), (30, 32)):
        word = jnp.zeros((rows, 128), I32)
        for j in range(first, last):
            hit = at == (src_ref[j : j + 1, lanes] - base)
            word += jnp.where(hit, val_ref[j : j + 1, lanes], 0)
        even += word & 0x0F0F0F0F
        odd += (word >> 4) & 0x0F0F0F0F
    return even, odd


def counts_of(even, odd, k):
    word = odd if k % 2 else even
    return ((word >> (8 * (k // 2))) & 0xFF).astype(F32).astype(BF16)


def lists_kernel(
    leaf_ref, src_ref, cls_ref, par_src_ref, par_cls_ref, top_src_ref, top_cls_ref, m2l_ref,
    partial_ref, far_ref, small_ref,
    src_t, val_t, low_src, low_val, near_w, far_w, z_ref,
):
    me = lax.axis_index("gy")
    device = lax.axis_index("gx") * 16 + me
    src = src_ref[...]
    src = jnp.where(src >= 4096, src - (4096 - 256), src - 256 * me)
    src_t[...] = src.T
    cls = cls_ref[...]
    val_t[...] = jnp.where(cls >= 0, jnp.left_shift(1, 4 * jnp.maximum(cls, 0)), 0).T
    psrc = par_src_ref[...]
    place = (psrc // 32 - device + 16) // 16
    psrc = jnp.where(psrc >= 0, place * 32 + psrc % 32, -1)
    tsrc = top_src_ref[pl.ds(4 * me, 4), :]
    tsrc = jnp.where(tsrc >= 0, (tsrc // 4) * 8 + tsrc % 4, -1)
    tcls = top_cls_ref[pl.ds(4 * me, 4), :]
    both = jnp.concatenate([psrc, tsrc, jnp.full((92, 32), -1, I32)], axis=0)
    low_src[...] = both.T
    both = jnp.concatenate([par_cls_ref[...], tcls, jnp.full((92, 32), -1, I32)], axis=0)
    low_val[...] = jnp.where(both >= 0, jnp.left_shift(1, 4 * jnp.maximum(both, 0)), 0).T

    rows = 64

    def near_block(i, _):
        for half in range(2):
            lanes = slice(128 * half, 128 * half + 128)
            even, odd = fields(src_t, val_t, lanes, i * rows, rows)
            for k in range(8):
                near_w[pl.ds(pl.multiple_of(256 * k + i * rows, rows), rows), lanes] = counts_of(even, odd, k)
        return 0

    def far_block(i, _):
        for half in range(2):
            lanes = slice(128 * half, 128 * half + 128)
            even, odd = fields(src_t, val_t, lanes, 256 + i * rows, rows)
            for k in range(8):
                far_w[pl.ds(pl.multiple_of(128 * k + i * rows, rows), rows), lanes] = counts_of(even, odd, k)
        return 0

    def small_block(i, _):
        even, odd = fields(low_src, low_val, slice(0, 128), i * rows, rows)
        for k in range(8):
            small_ref[k, pl.ds(pl.multiple_of(i * rows, rows), rows), :] = counts_of(even, odd, k)
        return 0

    lax.fori_loop(0, 4, near_block, 0)
    lax.fori_loop(0, 2, far_block, 0)
    lax.fori_loop(0, 2, small_block, 0)

    leaf = leaf_ref[...]
    for k in range(8):
        z_ref[256 * k : 256 * k + 256, :] = dot(leaf, m2l_ref[k]).astype(BF16)
    partial_ref[...] = dot_tn(near_w[...], z_ref[...])
    for k in range(8):
        far_ref[:, 128 * k : 128 * k + 128] = far_w[128 * k : 128 * k + 128, :].T


def lists(leaf, src, cls, par_src, par_cls, top_src, top_cls, m2l):
    return pl.pallas_call(
        lists_kernel,
        out_shape=(
            jax.ShapeDtypeStruct((256, 256), F32),
            jax.ShapeDtypeStruct((256, 1024), BF16),
            jax.ShapeDtypeStruct((8, 128, 128), BF16),
        ),
        scratch_shapes=[
            pltpu.VMEM((32, 256), I32),
            pltpu.VMEM((32, 256), I32),
            pltpu.VMEM((32, 128), I32),
            pltpu.VMEM((32, 128), I32),
            pltpu.VMEM((2048, 256), BF16),
            pltpu.VMEM((1024, 256), BF16),
            pltpu.VMEM((2048, 256), BF16),
        ],
        compiler_params=pltpu.CompilerParams(vmem_limit_bytes=VMEM_LIMIT),
        cost_estimate=pl.CostEstimate(flops=3_000_000_000, bytes_accessed=2_500_000, transcendentals=0),
        name="lists",
    )(leaf, src, cls, par_src, par_cls, top_src, top_cls, m2l)


def pieces(x):
    high = x.astype(BF16).astype(F32)
    rest = x - high
    middle = rest.astype(BF16).astype(F32)
    return high, middle, rest - middle


def near_kernel(list_ref, points_ref, charges_ref, below_ref, above_ref, out_ref, source_s, target_s, q_s):
    device = lax.axis_index("gx") * 16 + lax.axis_index("gy")
    ones = jnp.ones((3, 128), F32)
    pad = jnp.zeros((5, 128), F32)
    for s in range(16):
        if s < 4:
            xyz, q = below_ref[s, 0:3, :], below_ref[s, 3:4, :]
        elif s < 12:
            xyz, q = points_ref[s - 4], charges_ref[s - 4 : s - 3, :]
        else:
            xyz, q = above_ref[s - 12, 0:3, :], above_ref[s - 12, 3:4, :]
        q_s[s] = jnp.broadcast_to(q, (8, 128))
        high, middle, low = pieces(xyz)
        norm = jnp.sum(xyz * xyz, axis=0, keepdims=True)
        n = jnp.concatenate(pieces(norm), axis=0)
        source_s[s] = jnp.concatenate(
            [high, high, middle, high, low, middle, ones, n, jnp.zeros((8, 128), F32)], axis=0
        ).astype(BF16)
        if 4 <= s < 12:
            n = jnp.concatenate(pieces(norm + SOFTENING * SOFTENING), axis=0)
            target_s[s - 4] = jnp.concatenate(
                [-2.0 * high, -2.0 * middle, -2.0 * high, -2.0 * low, -2.0 * high, -2.0 * middle, n, ones,
                 jnp.zeros((8, 128), F32)],
                axis=0,
            ).astype(BF16)

    def tile(t, _):
        target = target_s[t]
        total = jnp.zeros((128, 128), F32)
        for j in range(8):
            number = list_ref[t, j]
            place = jnp.clip(number - (device * 8 - HALO_T), 0, 15)
            q = q_s[place][0:1, :] * jnp.where(number >= 0, 1.0, 0.0)
            total += q * lax.rsqrt(dot_tn(target, source_s[place]))
        out_ref[pl.ds(t, 1), :] = jnp.sum(total.T, axis=0, keepdims=True)
        return 0

    lax.fori_loop(0, 8, tile, 0)


def near(near_src, points, charges, below, above):
    vmem = pl.BlockSpec(memory_space=pltpu.VMEM)
    return pl.pallas_call(
        near_kernel,
        out_shape=jax.ShapeDtypeStruct((8, 128), F32),
        in_specs=[pl.BlockSpec(memory_space=pltpu.SMEM), vmem, vmem, vmem, vmem],
        scratch_shapes=[
            pltpu.VMEM((16, 32, 128), BF16),
            pltpu.VMEM((8, 32, 128), BF16),
            pltpu.VMEM((16, 8, 128), F32),
        ],
        compiler_params=pltpu.CompilerParams(vmem_limit_bytes=VMEM_LIMIT),
        cost_estimate=pl.CostEstimate(flops=1_500_000_000, bytes_accessed=100_000, transcendentals=1_000_000),
        name="near",
    )(near_src, points, charges, below, above)


def down_kernel(
    recv_ref, before_ref, parents_ref, after_ref, partial_ref, far_ref, small_ref, m2l_ref, l2l_ref,
    out_ref, far_z, top_z, par_z,
):
    recv = recv_ref[...].reshape(256, 256)
    bank = jnp.concatenate([before_ref[...], parents_ref[...], after_ref[...]], axis=0)
    for k in range(8):
        z = dot(recv, m2l_ref[k]).reshape(16, 16, 256)
        far_z[128 * k : 128 * k + 128, :] = z[:, :8].reshape(128, 256).astype(BF16)
        top_z[128 * k : 128 * k + 128, :] = z[:, 8:].reshape(128, 256).astype(BF16)
        z = dot(bank, m2l_ref[k])
        par_z[128 * k : 128 * k + 128, :] = jnp.concatenate([z, jnp.zeros((32, 256), F32)], axis=0).astype(BF16)
    weights = small_ref[...].reshape(1024, 128)
    top_field = dot_tn(weights, top_z[...])
    top_local = top_field.astype(BF16)
    par_field = dot_tn(weights, par_z[...])[0:32]
    row = iota((32, 128), 0)
    lane = iota((32, 128), 1)
    for c in range(8):
        spread = ((lane == 32 + row // 8) & (row % 8 == c)).astype(F32).astype(BF16)
        par_field += dot(dot(spread, top_local).astype(BF16), l2l_ref[c])
    parent_local = par_field.astype(BF16)
    total = partial_ref[...] + dot(far_ref[...], far_z[...])
    row = iota((256, 32), 0)
    lane = iota((256, 32), 1)
    for c in range(8):
        spread = ((lane == row // 8) & (row % 8 == c)).astype(F32).astype(BF16)
        total += dot(dot(spread, parent_local).astype(BF16), l2l_ref[c])
    out_ref[...] = total.astype(BF16)


def down(recv, before, parents, after, partial, far, small, m2l, l2l):
    return pl.pallas_call(
        down_kernel,
        out_shape=jax.ShapeDtypeStruct((256, 256), BF16),
        scratch_shapes=[
            pltpu.VMEM((1024, 256), BF16),
            pltpu.VMEM((1024, 256), BF16),
            pltpu.VMEM((1024, 256), BF16),
        ],
        compiler_params=pltpu.CompilerParams(vmem_limit_bytes=VMEM_LIMIT),
        cost_estimate=pl.CostEstimate(flops=1_500_000_000, bytes_accessed=3_500_000, transcendentals=0),
        name="down",
    )(recv, before, parents, after, partial, far, small, m2l, l2l)


def shifted(block, axes, distance):
    size = lax.axis_size(axes)
    route = [(i, i + distance) for i in range(size) if 0 <= i + distance < size]
    return lax.ppermute(block, axes, route)


def per_device(
    leaf_moments, leaf_src, leaf_cls, send_rows, send_count, par_src, par_cls, top_src, top_cls,
    points, charges, near_src, m2m_ops, m2l_ops, l2l_ops,
):
    packed = jnp.concatenate([points, charges[:, None, :]], axis=1)
    below = shifted(packed[-HALO_T:], ("gx", "gy"), 1)
    above = shifted(packed[:HALO_T], ("gx", "gy"), -1)
    sent, parents = pack(leaf_moments, m2m_ops, send_rows[0], send_count[0])
    recv = lax.all_to_all(sent, "gy", 0, 0, tiled=True)
    before = shifted(parents, "gx", 1)
    after = shifted(parents, "gx", -1)
    partial, far, small = lists(leaf_moments, leaf_src, leaf_cls, par_src, par_cls, top_src, top_cls, m2l_ops)
    near_total = near(near_src, points, charges, below, above)
    leaf_local = down(recv, before, parents, after, partial, far, small, m2l_ops, l2l_ops)
    return leaf_local, near_total


def solution(mesh):
    both = P(("gx", "gy"))
    return jax.shard_map(
        per_device,
        mesh=mesh,
        in_specs=(both, both, both, P("gx"), P("gx"), both, both, P("gx"), P("gx"), both, both, both, P(), P(), P()),
        out_specs=(both, both),
        check_vma=False,
    )
```

time: 227 us -> 46.3 us (0.20)
  the two profiles are of different devices: /device:TPU:390 before, /device:TPU:384 now
where the time goes in v1:
time: 46.3 us; the launch traced here: 45.6 us
  starting transfers between devices  24.8 us (54%)
  Pallas kernels  12.4 us (27%)
  local copies, waits for them, and re-layouts  7.47 us (16%)
  between operations  0.85 us (2%)
    ppermute x4, starting transfers between devices, shifted(): return lax.ppermute(block, axes, route)  17.8 us
    unnamed x42, local copies, waits for them, and re-layouts  7.47 us
    all_to_all x1, starting transfers between devices, per_device(): recv = lax.all_to_all(sent, 'gy', 0, 0, tiled=True)  7.05 us
    pallas_call x1, Pallas kernels, near(): pl.pallas_call(near_kernel, out_shape=jax.ShapeDtypeStruct((8, 128), F32)...  4.14 us
    pallas_call x1, Pallas kernels, lists(): pl.pallas_call(lists_kernel, out_shape=(jax.ShapeDtypeStruct((256, 256),...  3.57 us
    pallas_call x1, Pallas kernels, down(): pl.pallas_call(down_kernel, out_shape=jax.ShapeDtypeStruct((256, 256), BF...  2.9 us
    pallas_call x1, Pallas kernels, pack(): pl.pallas_call(pack_kernel, out_shape=(jax.ShapeDtypeStruct((16, 16, 256)...  1.81 us
  transfers between devices with their start and end apart: 5, of which 0 were waited for; matrix products, arithmetic and copies ran while one was open for 1% of the time, Pallas kernels for 17%

profile of v1, /device:TPU:384, one launch (start us, length us, event | category | flops | bytes accessed | tf_op | source)
XLA Modules:
  0.0 45.6 jit_solution(18074181724545627852)
XLA Ops:
  0.6 0.0 copy-start.1
  0.6 0.0 copy-start.2
  0.6 1.0 %copy.17 = s32[1,16,16,8]{3,2,1,0:T(8,128)S(1)} copy(s32[1,16,16,8]{2,3,1,0:T(8,128)} %param.18) | data formatting | bytes 16384 | tf_op args[3]
  1.6 0.0 copy-done.1
  1.6 0.0 copy-done.2
  1.6 0.0 copy-start
  1.7 1.2 %copy-done = bf16[8,256,256]{2,1,0:T(8,128)(2,1)S(1)} copy-done((bf16[8,256,256]{2,1,0:T(8,128)(2,1)S(1)}, bf16[8,256,256]{2,1,0:T(8,128)(2,1)}, u32[]{:S(2)}) %copy-start) | copy-done | bytes 1048600
  2.9 0.0 copy-start.4
  2.9 1.8 %pack.1 = (bf16[16,16,256]{2,1,0:T(8,128)(2,1)}, bf16[32,256]{1,0:T(8,128)(2,1)S(1)}) custom-call(bf16[256,256]{1,0:T(8,128)(2,1)S(1)} %copy-done.1, bf16[8,256,256]{2,1,0:T(8,128)(2,1)S(1)} %copy-done, s32[16,16,8]{2,1,0:T(8,128)S(1)} %bitcast.3, s32[16,16]{1,0:T(8,128)S(1)} %bitcast.4), custom_call_target="tpu_custom_call" | custom-call | flops 200000000 | bytes 1500000 | tf_op jit(solution)/shard_map/pack/pallas_call | solution.py:63
  4.7 1.9 %collective-permute-start = (bf16[32,256]{1,0:T(8,128)(2,1)S(1)}, bf16[32,256]{1,0:T(8,128)(2,1)S(1)}, u32[]{:S(2)}, u32[]{:S(2)}) collective-permute-start(bf16[32,256]{1,0:T(8,128)(2,1)S(1)} %get-tuple-element.8.parents_ref), channel_id=1, source_target_pairs={{0,16},{16,32},{32,48},{48,64},{64,80},{80,96},{96,112},{112,128},... | collective-permute-start | bytes 49160 | tf_op jit(solution)/shard_map/ppermute | solution.py:289
  6.6 4.9 %collective-permute-start.1 = (bf16[32,256]{1,0:T(8,128)(2,1)S(1)}, bf16[32,256]{1,0:T(8,128)(2,1)S(1)}, u32[]{:S(2)}, u32[]{:S(2)}) collective-permute-start(bf16[32,256]{1,0:T(8,128)(2,1)S(1)} %get-tuple-element.8.parents_ref), channel_id=1, source_target_pairs={{16,0},{32,16},{48,32},{64,48},{80,64},{96,80},{112,96},{128,112},... | collective-permute-start | bytes 49160 | tf_op jit(solution)/shard_map/ppermute | solution.py:289
  11.5 0.0 copy-start.17
  11.5 7.0 %all-to-all-start = ((bf16[16,16,256]{2,1,0:T(8,128)(2,1)}), bf16[16,16,256]{2,1,0:T(8,128)(2,1)S(1)}, u32[]{:S(2)}, u32[]{:S(2)}) async-start(bf16[16,16,256]{2,1,0:T(8,128)(2,1)} %get-tuple-element.7), calls=%async_computation | async-start | bytes 262144 | tf_op jit(solution)/shard_map/all_to_all | solution.py:300
  18.5 0.0 copy-done.17
  18.5 0.0 copy-start.3
  18.5 0.0 copy-start.13
  18.6 0.7 %copy-done.3 = f32[8,128]{1,0:T(8,128)S(1)} copy-done((f32[8,128]{1,0:T(8,128)S(1)}, f32[8,128]{1,0:T(8,128)}, u32[]{:S(2)}) %copy-start.3) | copy-done | bytes 4120
  19.2 3.8 %collective-permute-start.2 = (f32[4,4,128]{2,1,0:T(4,128)S(1)}, f32[4,4,128]{2,1,0:T(4,128)S(1)}, u32[]{:S(2)}, u32[]{:S(2)}) collective-permute-start(f32[4,4,128]{2,1,0:T(4,128)S(1)} %get-tuple-element.13), channel_id=1, source_target_pairs={{0,1},{1,2},{2,3},{3,4},{4,5},{5,6},{6,7},{7,8},{8,9},{9,10},{10,1... | collective-permute-start | bytes 24584 | tf_op jit(solution)/shard_map/ppermute | solution.py:289
  23.1 0.0 copy-start.14
  23.1 7.2 %collective-permute-start.3 = (f32[4,4,128]{2,1,0:T(4,128)S(1)}, f32[4,4,128]{2,1,0:T(4,128)S(1)}, u32[]{:S(2)}, u32[]{:S(2)}) collective-permute-start(f32[4,4,128]{2,1,0:T(4,128)S(1)} %get-tuple-element.12), channel_id=1, source_target_pairs={{1,0},{2,1},{3,2},{4,3},{5,4},{6,5},{7,6},{8,7},{9,8},{10,9},{11,1... | collective-permute-start | bytes 24584 | tf_op jit(solution)/shard_map/ppermute | solution.py:289
  30.3 0.0 copy-done.13
  30.3 0.1 copy.18.src_ref
  30.4 0.0 copy-done.14
  30.4 0.0 copy-start.15
  30.4 0.1 copy.19.cls_ref
  30.5 0.6 %copy-done.15 = s32[64,32]{0,1:T(8,128)S(1)} copy-done((s32[64,32]{0,1:T(8,128)S(1)}, s32[64,32]{0,1:T(8,128)}, u32[]{:S(2)}) %copy-start.15) | copy-done | bytes 8216
  31.1 0.0 copy-start.16
  31.1 0.1 copy.20.top_src_ref
  31.2 0.6 %copy-done.16 = s32[64,32]{0,1:T(8,128)S(1)} copy-done((s32[64,32]{0,1:T(8,128)S(1)}, s32[64,32]{0,1:T(8,128)}, u32[]{:S(2)}) %copy-start.16) | copy-done | bytes 8216
  31.8 0.0 copy-start.6
  31.8 0.0 copy-start.7
  31.8 0.1 copy.21.top_cls_ref
  31.9 0.0 copy-done.4
  31.9 0.6 %copy-done.6 = s32[32,32]{1,0:T(8,128)S(1)} copy-done((s32[32,32]{1,0:T(8,128)S(1)}, s32[32,32]{1,0:T(8,128)}, u32[]{:S(2)}) %copy-start.6) | copy-done | bytes 4120
  32.5 0.0 copy-done.7
  32.5 0.0 copy-start.8
  32.6 3.6 %lists.1 = (f32[256,256]{1,0:T(8,128)S(1)}, bf16[256,1024]{1,0:T(8,128)(2,1)S(1)}, bf16[8,128,128]{2,1,0:T(8,128)(2,1)S(1)}) custom-call(bf16[256,256]{1,0:T(8,128)(2,1)S(1)} %copy-done.1, s32[256,32]{1,0:T(8,128)S(1)} %copy.18.src_ref, s32[256,32]{1,0:T(8,128)S(1)} %copy.19.cls_ref, s32[32,32]{1,0:T(8,128)S(1)} %copy-done.6, s32[32,32]{1,0:T(8,128)S(1)} %copy-done.7, ...), custom_call_target="tpu_custom_call" | custom-call | flops 3000000000 | bytes 2500000 | tf_op jit(solution)/shard_map/lists/pallas_call | solution.py:154
  36.1 0.0 copy-start.9
  36.1 0.7 %copy-done.9 = f32[256,256]{1,0:T(8,128)} copy-done((f32[256,256]{1,0:T(8,128)}, f32[256,256]{1,0:T(8,128)S(1)}, u32[]{:S(2)}) %copy-start.9) | copy-done | bytes 262168
  36.8 0.0 copy-start.11
  36.8 0.7 %copy-done.11 = bf16[8,128,128]{2,1,0:T(8,128)(2,1)} copy-done((bf16[8,128,128]{2,1,0:T(8,128)(2,1)}, bf16[8,128,128]{2,1,0:T(8,128)(2,1)S(1)}, u32[]{:S(2)}) %copy-start.11) | copy-done | bytes 262168
  37.5 0.0 copy-start.5
  37.5 0.0 collective-permute-done.2.below_ref
  37.5 0.0 copy-start.10
  37.5 0.0 collective-permute-done.3.above_ref
  37.5 0.0 copy-done.8
  37.5 4.1 %near.1 = f32[8,128]{1,0:T(8,128)} custom-call(s32[8,8]{1,0:T(8,128)S(1)} %copy-done.8, f32[8,3,128]{2,1,0:T(4,128)S(1)} %copy.23.points_ref, f32[8,128]{1,0:T(8,128)S(1)} %copy-done.3, f32[4,4,128]{2,1,0:T(4,128)S(1)} %collective-permute-done.2.below_ref, f32[4,4,128]{2,1,0:T(4,128)S(1)} %collective-permute-done.3.above_ref), custom_call_target="tpu_custom_call" | custom-call | flops 1500000000 | bytes 100000 | tf_op jit(solution)/shard_map/near/pallas_call | solution.py:225
  41.7 0.0 collective-permute-done.before_ref
  41.7 0.0 collective-permute-done.1.after_ref
  41.7 0.0 all-to-all-done.recv_ref
  41.7 0.0 copy-done.5
  41.7 0.0 copy-done.10
  41.7 0.0 copy-start.12
  41.7 0.9 %copy-done.12 = bf16[8,128,128]{2,1,0:T(8,128)(2,1)S(1)} copy-done((bf16[8,128,128]{2,1,0:T(8,128)(2,1)S(1)}, bf16[8,128,128]{2,1,0:T(8,128)(2,1)}, u32[]{:S(2)}) %copy-start.12) | copy-done | bytes 262168
  42.7 2.9 %down.1 = bf16[256,256]{1,0:T(8,128)(2,1)} custom-call(bf16[16,16,256]{2,1,0:T(8,128)(2,1)S(1)} %all-to-all-done.recv_ref, bf16[32,256]{1,0:T(8,128)(2,1)S(1)} %collective-permute-done.before_ref, bf16[32,256]{1,0:T(8,128)(2,1)S(1)} %get-tuple-element.8.parents_ref, bf16[32,256]{1,0:T(8,128)(2,1)S(1)} %collective-permute-done.1.after_ref, ...), custom_call_target="tpu_custom_call" | custom-call | flops 1500000000 | bytes 3500000 | tf_op jit(solution)/shard_map/down/pallas_call | solution.py:272
  (2 shorter events, 0.0 us)
Async XLA Ops:
  0.6 1.0 %copy-start.1 = (bf16[256,256]{1,0:T(8,128)(2,1)S(1)}, bf16[256,256]{1,0:T(8,128)(2,1)}, u32[]{:S(2)}) copy-start(bf16[256,256]{1,0:T(8,128)(2,1)} %leaf_ref.3) | copy-start | bytes 393220
  0.6 1.0 %copy-start.2 = (s32[1,16,16]{2,1,0:T(8,128)S(1)}, s32[1,16,16]{2,1,0:T(8,128)}, u32[]{:S(2)}) copy-start(s32[1,16,16]{2,1,0:T(8,128)} %param.19) | copy-start | bytes 3076
  1.6 1.2 %copy-start = (bf16[8,256,256]{2,1,0:T(8,128)(2,1)S(1)}, bf16[8,256,256]{2,1,0:T(8,128)(2,1)}, u32[]{:S(2)}) copy-start(bf16[8,256,256]{2,1,0:T(8,128)(2,1)} %m2m_ref.1) | copy-start | bytes 3145732
  2.9 29.0 %copy-start.4 = (bf16[8,256,256]{2,1,0:T(8,128)(2,1)S(1)}, bf16[8,256,256]{2,1,0:T(8,128)(2,1)}, u32[]{:S(2)}) copy-start(bf16[8,256,256]{2,1,0:T(8,128)(2,1)} %m2l_ref.3) | copy-start | bytes 3145732
  4.7 37.0 %collective-permute-start = (bf16[32,256]{1,0:T(8,128)(2,1)S(1)}, bf16[32,256]{1,0:T(8,128)(2,1)S(1)}, u32[]{:S(2)}, u32[]{:S(2)}) collective-permute-start(bf16[32,256]{1,0:T(8,128)(2,1)S(1)} %get-tuple-element.8.parents_ref), channel_id=1, source_target_pairs={{0,16},{16,32},{32,48},{48,64},{64,80},{80,96},{96,112},{112,128},... | collective-permute-start | bytes 49160 | tf_op jit(solution)/shard_map/ppermute | solution.py:289
  6.6 35.1 %collective-permute-start.1 = (bf16[32,256]{1,0:T(8,128)(2,1)S(1)}, bf16[32,256]{1,0:T(8,128)(2,1)S(1)}, u32[]{:S(2)}, u32[]{:S(2)}) collective-permute-start(bf16[32,256]{1,0:T(8,128)(2,1)S(1)} %get-tuple-element.8.parents_ref), channel_id=1, source_target_pairs={{16,0},{32,16},{48,32},{64,48},{80,64},{96,80},{112,96},{128,112},... | collective-permute-start | bytes 49160 | tf_op jit(solution)/shard_map/ppermute | solution.py:289
  11.5 7.1 %copy-start.17 = (f32[8,3,128]{2,0,1:T(8,128)S(1)}, f32[8,3,128]{2,0,1:T(8,128)}, u32[]{:S(2)}) copy-start(f32[8,3,128]{2,0,1:T(8,128)} %param.24) | copy-start | bytes 36868
  11.5 30.2 %all-to-all-start = ((bf16[16,16,256]{2,1,0:T(8,128)(2,1)}), bf16[16,16,256]{2,1,0:T(8,128)(2,1)S(1)}, u32[]{:S(2)}, u32[]{:S(2)}) async-start(bf16[16,16,256]{2,1,0:T(8,128)(2,1)} %get-tuple-element.7), calls=%async_computation | async-start | bytes 262144 | tf_op jit(solution)/shard_map/all_to_all | solution.py:300
  18.5 0.7 %copy-start.3 = (f32[8,128]{1,0:T(8,128)S(1)}, f32[8,128]{1,0:T(8,128)}, u32[]{:S(2)}) copy-start(f32[8,128]{1,0:T(8,128)} %charges_ref.1) | copy-start | bytes 12292
  18.5 11.7 %copy-start.13 = (s32[256,32]{0,1:T(8,128)S(1)}, s32[256,32]{0,1:T(8,128)}, u32[]{:S(2)}) copy-start(s32[256,32]{0,1:T(8,128)} %param.16) | copy-start | bytes 98308
  19.2 18.3 %collective-permute-start.2 = (f32[4,4,128]{2,1,0:T(4,128)S(1)}, f32[4,4,128]{2,1,0:T(4,128)S(1)}, u32[]{:S(2)}, u32[]{:S(2)}) collective-permute-start(f32[4,4,128]{2,1,0:T(4,128)S(1)} %get-tuple-element.13), channel_id=1, source_target_pairs={{0,1},{1,2},{2,3},{3,4},{4,5},{5,6},{6,7},{7,8},{8,9},{9,10},{10,1... | collective-permute-start | bytes 24584 | tf_op jit(solution)/shard_map/ppermute | solution.py:289
  23.1 7.3 %copy-start.14 = (s32[256,32]{0,1:T(8,128)S(1)}, s32[256,32]{0,1:T(8,128)}, u32[]{:S(2)}) copy-start(s32[256,32]{0,1:T(8,128)} %param.17) | copy-start | bytes 98308
  23.1 14.4 %collective-permute-start.3 = (f32[4,4,128]{2,1,0:T(4,128)S(1)}, f32[4,4,128]{2,1,0:T(4,128)S(1)}, u32[]{:S(2)}, u32[]{:S(2)}) collective-permute-start(f32[4,4,128]{2,1,0:T(4,128)S(1)} %get-tuple-element.12), channel_id=1, source_target_pairs={{1,0},{2,1},{3,2},{4,3},{5,4},{6,5},{7,6},{8,7},{9,8},{10,9},{11,1... | collective-permute-start | bytes 24584 | tf_op jit(solution)/shard_map/ppermute | solution.py:289
  30.4 0.7 %copy-start.15 = (s32[64,32]{0,1:T(8,128)S(1)}, s32[64,32]{0,1:T(8,128)}, u32[]{:S(2)}) copy-start(s32[64,32]{0,1:T(8,128)} %param.22) | copy-start | bytes 24580
  31.1 0.7 %copy-start.16 = (s32[64,32]{0,1:T(8,128)S(1)}, s32[64,32]{0,1:T(8,128)}, u32[]{:S(2)}) copy-start(s32[64,32]{0,1:T(8,128)} %param.23) | copy-start | bytes 24580
  31.8 0.7 %copy-start.6 = (s32[32,32]{1,0:T(8,128)S(1)}, s32[32,32]{1,0:T(8,128)}, u32[]{:S(2)}) copy-start(s32[32,32]{1,0:T(8,128)} %par_src_ref.1) | copy-start | bytes 12292
  31.8 0.7 %copy-start.7 = (s32[32,32]{1,0:T(8,128)S(1)}, s32[32,32]{1,0:T(8,128)}, u32[]{:S(2)}) copy-start(s32[32,32]{1,0:T(8,128)} %par_cls_ref.1) | copy-start | bytes 12292
  32.5 5.0 %copy-start.8 = (s32[8,8]{1,0:T(8,128)S(1)}, s32[8,8]{1,0:T(8,128)}, u32[]{:S(2)}) copy-start(s32[8,8]{1,0:T(8,128)} %list_ref.1) | copy-start | bytes 772
  36.1 0.7 %copy-start.9 = (f32[256,256]{1,0:T(8,128)}, f32[256,256]{1,0:T(8,128)S(1)}, u32[]{:S(2)}) copy-start(f32[256,256]{1,0:T(8,128)S(1)} %get-tuple-element.9.partial_ref) | copy-start | bytes 786436
  36.8 0.7 %copy-start.11 = (bf16[8,128,128]{2,1,0:T(8,128)(2,1)}, bf16[8,128,128]{2,1,0:T(8,128)(2,1)S(1)}, u32[]{:S(2)}) copy-start(bf16[8,128,128]{2,1,0:T(8,128)(2,1)S(1)} %get-tuple-element.11.small_ref) | copy-start | bytes 786436
  37.5 4.2 %copy-start.5 = (bf16[8,256,256]{2,1,0:T(8,128)(2,1)S(1)}, bf16[8,256,256]{2,1,0:T(8,128)(2,1)}, u32[]{:S(2)}) copy-start(bf16[8,256,256]{2,1,0:T(8,128)(2,1)} %l2l_ref.1) | copy-start | bytes 3145732
  37.5 4.2 %copy-start.10 = (f32[256,256]{1,0:T(8,128)S(1)}, f32[256,256]{1,0:T(8,128)}, u32[]{:S(2)}) copy-start(f32[256,256]{1,0:T(8,128)} %copy-done.9) | copy-start | bytes 786436
  41.7 1.0 %copy-start.12 = (bf16[8,128,128]{2,1,0:T(8,128)(2,1)S(1)}, bf16[8,128,128]{2,1,0:T(8,128)(2,1)}, u32[]{:S(2)}) copy-start(bf16[8,128,128]{2,1,0:T(8,128)(2,1)} %copy-done.11) | copy-start | bytes 786436

commit v2 on v1

v2 whole, which is shorter than its diff:
```python
import jax
import jax.numpy as jnp
from jax import lax
from jax.experimental import pallas as pl
from jax.experimental.pallas import tpu as pltpu
from jax.sharding import PartitionSpec as P

F32 = jnp.float32
BF16 = jnp.bfloat16
I32 = jnp.int32

HALO_T = 4
SOFTENING = 0.05
VMEM_LIMIT = 10 * 1024 * 1024
PACK_VMEM = 60 * 1024 * 1024


def iota(shape, dim):
    return lax.broadcasted_iota(I32, shape, dim)


def dot(a, b):
    return jnp.dot(a, b, preferred_element_type=F32)


def dot_nt(a, b):
    return lax.dot_general(a, b, (((1,), (1,)), ((), ())), preferred_element_type=F32)


def dot_tn(a, b):
    return lax.dot_general(a, b, (((0,), (0,)), ((), ())), preferred_element_type=F32)


def pieces(x):
    high = x.astype(BF16).astype(F32)
    rest = x - high
    middle = rest.astype(BF16).astype(F32)
    return high, middle, rest - middle


def wide(value):
    return jnp.concatenate([value[0], value[1]], axis=1)


def every_eighth(ref, first, count):
    return wide([ref[half, pl.ds(first, count, stride=8), :] for half in range(2)])


def put_every_eighth(ref, first, count, value):
    for half in range(2):
        ref[half, pl.ds(first, count, stride=8), :] = value[:, 128 * half : 128 * half + 128]


def fetch(copies):
    for copy in copies:
        copy.start()
    return copies


def tile_rows(parts, first):
    left = jnp.concatenate([part[first : first + HALO_T] for part in parts[:6]], axis=0)
    right = jnp.concatenate([part[first : first + HALO_T] for part in parts[6:]], axis=0)
    return jnp.concatenate([jnp.concatenate([left, right], axis=1), jnp.zeros((8, 256), F32)], axis=0)


def pack_kernel(
    leaf_hbm, m2m_hbm, rows_hbm, count_hbm, points_hbm, charges_hbm, send_ref, parents_ref,
    leaf_ref, m2m_ref, rows_ref, count_ref, points_ref, charges_ref, leaf_s, parents_s, sems,
):
    me = lax.axis_index("gy")
    pairs = (
        (leaf_hbm, leaf_ref), (rows_hbm.at[me], rows_ref), (count_hbm, count_ref),
        (points_hbm, points_ref), (charges_hbm, charges_ref), (m2m_hbm, m2m_ref),
    )
    copies = fetch([pltpu.make_async_copy(a, b, sems.at[i]) for i, (a, b) in enumerate(pairs)])
    parents_s[:, 32:64, :] = jnp.zeros((2, 32, 128), F32)
    for copy in copies[:5]:
        copy.wait()
    leaf = leaf_ref[...]
    for half in range(2):
        leaf_s[half] = leaf[:, 128 * half : 128 * half + 128].astype(F32)
    table = rows_ref[...].astype(F32)
    live = iota((8, 16), 0) < count_ref[pl.ds(me, 1), :]
    table = jnp.where(live, table, -1.0).astype(BF16)
    repeat = (iota((128, 16), 0) // 8 == iota((128, 16), 1)).astype(F32).astype(BF16)
    spread = dot_nt(repeat, table)
    column = jnp.sum(
        jnp.where(iota((128, 8), 0) % 8 == iota((128, 8), 1), spread, 0.0), axis=1, keepdims=True
    )
    pick = (iota((128, 256), 1).astype(F32) == column).astype(F32).astype(BF16)
    sent = dot(pick, leaf)
    parts = [[], [], []]
    for axis in range(3):
        for kind, part in enumerate(pieces(points_ref[axis])):
            parts[kind].append(part)
    parts = parts[0] + parts[1] + parts[2] + list(pieces(charges_ref[...]))
    first = tile_rows(parts, 0)
    last = tile_rows(parts, 8 - HALO_T)
    copies[5].wait()
    parents = jnp.zeros((32, 256), F32)
    for c in range(8):
        parents += dot(every_eighth(leaf_s, c, 32).astype(BF16), m2m_ref[c])
    parents = parents.astype(BF16)
    parents_ref[...] = parents
    for half in range(2):
        parents_s[half, 0:32, :] = parents[:, 128 * half : 128 * half + 128].astype(F32)
    top = jnp.zeros((8, 256), F32)
    for c in range(8):
        top += dot(every_eighth(parents_s, c, 8).astype(BF16), m2m_ref[c])
    for p in range(16):
        tiles = jnp.where(me + 1 == p, last, jnp.where(me - 1 == p, first, 0.0))
        send_ref[p] = jnp.concatenate([sent[8 * p : 8 * p + 8], top, tiles], axis=0).astype(BF16)


def pack(leaf, m2m, rows, count, points, charges):
    return pl.pallas_call(
        pack_kernel,
        out_shape=(
            jax.ShapeDtypeStruct((16, 48, 256), BF16),
            jax.ShapeDtypeStruct((32, 256), BF16),
        ),
        in_specs=[pl.BlockSpec(memory_space=pltpu.HBM)] * 6,
        scratch_shapes=[
            pltpu.VMEM((256, 256), BF16),
            pltpu.VMEM((8, 256, 256), BF16),
            pltpu.VMEM((8, 16), I32),
            pltpu.VMEM((16, 16), I32),
            pltpu.VMEM((3, 8, 128), F32),
            pltpu.VMEM((8, 128), F32),
            pltpu.VMEM((2, 256, 128), F32),
            pltpu.VMEM((2, 64, 128), F32),
            pltpu.SemaphoreType.DMA((6,)),
        ],
        compiler_params=pltpu.CompilerParams(vmem_limit_bytes=PACK_VMEM),
        cost_estimate=pl.CostEstimate(flops=200_000_000, bytes_accessed=1_500_000, transcendentals=0),
        name="pack",
    )(leaf, m2m, rows, count, points, charges)


def fields(src_ref, val_ref, lanes, base, rows):
    at = iota((rows, 128), 0)
    even = jnp.zeros((rows, 128), I32)
    odd = jnp.zeros((rows, 128), I32)
    for first, last in ((0, 15), (15, 30), (30, 32)):
        word = jnp.zeros((rows, 128), I32)
        for j in range(first, last):
            hit = at == (src_ref[j : j + 1, lanes] - base)
            word += jnp.where(hit, val_ref[j : j + 1, lanes], 0)
        even += word & 0x0F0F0F0F
        odd += (word >> 4) & 0x0F0F0F0F
    return even, odd


def counts_of(even, odd, k):
    word = odd if k % 2 else even
    return ((word >> (8 * (k // 2))) & 0xFF).astype(F32).astype(BF16)


def field_of(cls):
    return jnp.where(cls >= 0, jnp.left_shift(1, 4 * jnp.maximum(cls, 0)), 0)


def lists_kernel(
    leaf_ref, m2l_ref, before_ref, parents_ref, after_ref, src_hbm, cls_hbm, par_src_hbm, par_cls_hbm, top_src_hbm, top_cls_hbm,
    partial_ref, far_ref, par_ref, top_ref,
    src_t, val_t, low_src, low_val, par_src_ref, par_cls_ref, top_src_ref, top_cls_ref, near_w, far_w, z_ref, small_w, par_z, sems,
):
    me = lax.axis_index("gy")
    device = lax.axis_index("gx") * 16 + me
    pairs = (
        (src_hbm, src_t), (cls_hbm, val_t), (par_src_hbm, par_src_ref), (par_cls_hbm, par_cls_ref),
        (top_src_hbm, top_src_ref), (top_cls_hbm, top_cls_ref),
    )
    copies = fetch([pltpu.make_async_copy(a, b, sems.at[i]) for i, (a, b) in enumerate(pairs)])
    leaf = leaf_ref[...]
    for k in range(8):
        z_ref[256 * k : 256 * k + 256, :] = dot(leaf, m2l_ref[k]).astype(BF16)
    bank = jnp.concatenate([before_ref[...], parents_ref[...], after_ref[...]], axis=0)
    for k in range(8):
        z = dot(bank, m2l_ref[k])
        par_z[128 * k : 128 * k + 128, :] = jnp.concatenate([z, jnp.zeros((32, 256), F32)], axis=0).astype(BF16)
    for copy in copies:
        copy.wait()
    src = src_t[...]
    src_t[...] = jnp.where(src >= 4096, src - (4096 - 256), src - 256 * me)
    val_t[...] = field_of(val_t[...])
    src = par_src_ref[...]
    place = (src // 32 - device + 16) // 16
    src = jnp.where(src >= 0, place * 32 + src % 32, -1)
    none = jnp.full((96, 32), -1, I32)
    src = jnp.concatenate([src, none], axis=0).T
    cls = jnp.concatenate([par_cls_ref[...], none], axis=0).T
    top = top_src_ref[...]
    top = jnp.where(top >= 0, (top // 4) * 8 + top % 4, -1)
    none = jnp.full((32, 32), -1, I32)
    low_src[...] = jnp.concatenate([src[:, 0:32], top, none], axis=1)
    low_val[...] = field_of(jnp.concatenate([cls[:, 0:32], top_cls_ref[...], none], axis=1))

    rows = 64

    def near_block(i, _):
        for half in range(2):
            lanes = slice(128 * half, 128 * half + 128)
            even, odd = fields(src_t, val_t, lanes, i * rows, rows)
            for k in range(8):
                near_w[pl.ds(pl.multiple_of(256 * k + i * rows, rows), rows), lanes] = counts_of(even, odd, k)
        return 0

    def far_block(i, _):
        for half in range(2):
            lanes = slice(128 * half, 128 * half + 128)
            even, odd = fields(src_t, val_t, lanes, 256 + i * rows, rows)
            for k in range(8):
                far_w[pl.ds(pl.multiple_of(128 * k + i * rows, rows), rows), lanes] = counts_of(even, odd, k)
        return 0

    def small_block(i, _):
        even, odd = fields(low_src, low_val, slice(0, 128), i * rows, rows)
        for k in range(8):
            small_w[pl.ds(pl.multiple_of(128 * k + i * rows, rows), rows), :] = counts_of(even, odd, k)
        return 0

    lax.fori_loop(0, 4, near_block, 0)
    lax.fori_loop(0, 2, far_block, 0)
    lax.fori_loop(0, 2, small_block, 0)
    partial_ref[...] = dot_tn(near_w[...], z_ref[...])
    for k in range(8):
        far_ref[:, 128 * k : 128 * k + 128] = far_w[128 * k : 128 * k + 128, :].T
    weights = small_w[...].T
    top_ref[...] = weights
    par_ref[...] = dot(weights[0:32], par_z[...])


def lists(leaf, m2l, before, parents, after, src, cls, par_src, par_cls, top_src, top_cls):
    vmem = pl.BlockSpec(memory_space=pltpu.VMEM)
    return pl.pallas_call(
        lists_kernel,
        out_shape=(
            jax.ShapeDtypeStruct((256, 256), F32),
            jax.ShapeDtypeStruct((256, 1024), BF16),
            jax.ShapeDtypeStruct((32, 256), F32),
            jax.ShapeDtypeStruct((128, 1024), BF16),
        ),
        in_specs=[vmem] * 5 + [pl.BlockSpec(memory_space=pltpu.HBM)] * 6,
        scratch_shapes=[
            pltpu.VMEM((32, 256), I32),
            pltpu.VMEM((32, 256), I32),
            pltpu.VMEM((32, 128), I32),
            pltpu.VMEM((32, 128), I32),
            pltpu.VMEM((32, 32), I32),
            pltpu.VMEM((32, 32), I32),
            pltpu.VMEM((32, 64), I32),
            pltpu.VMEM((32, 64), I32),
            pltpu.VMEM((2048, 256), BF16),
            pltpu.VMEM((1024, 256), BF16),
            pltpu.VMEM((2048, 256), BF16),
            pltpu.VMEM((1024, 128), BF16),
            pltpu.VMEM((1024, 256), BF16),
            pltpu.SemaphoreType.DMA((6,)),
        ],
        compiler_params=pltpu.CompilerParams(vmem_limit_bytes=VMEM_LIMIT),
        cost_estimate=pl.CostEstimate(flops=4_000_000_000, bytes_accessed=2_500_000, transcendentals=0),
        name="lists",
    )(leaf, m2l, before, parents, after, src, cls, par_src, par_cls, top_src, top_cls)


def near_kernel(
    list_ref, points_ref, charges_ref, recv_ref, edge_ref, out_ref, source_s, target_s, source_b, q_s, total_s
):
    me = lax.axis_index("gy")
    device = lax.axis_index("gx") * 16 + me
    source_s[...] = jnp.zeros_like(source_s)
    target_s[...] = jnp.zeros_like(target_s)

    def put(ref, first, count, row, value):
        ref[pl.ds(32 * first + row, count, stride=32), :] = value

    def put_source(first, count, xyz, q):
        for kind_row, kind in enumerate((0, 0, 1, 0, 2, 1)):
            for axis in range(3):
                put(source_s, first, count, 3 * kind_row + axis, xyz[kind][axis])
        norm = 0.0
        for axis in range(3):
            whole = xyz[0][axis] + xyz[1][axis] + xyz[2][axis]
            norm += whole * whole
        for i, part in enumerate(pieces(norm)):
            put(source_s, first, count, 18 + i, jnp.ones((count, 128), F32))
            put(source_s, first, count, 21 + i, part)
        q_s[first : first + count, :] = q
        return norm

    below = recv_ref[jnp.maximum(me - 1, 0), 16:48, :].astype(F32)
    above = recv_ref[jnp.minimum(me + 1, 15), 16:48, :].astype(F32)
    far = [edge_ref[axis] for axis in range(4)]
    for first, rows, start, end in ((0, below, 4, me == 0), (12, above, 0, me == 15)):
        parts = [rows[4 * (i % 6) : 4 * (i % 6) + 4, 128 * (i // 6) : 128 * (i // 6) + 128] for i in range(12)]
        other = [pieces(far[axis][start : start + 4]) for axis in range(3)]
        xyz = [[jnp.where(end, other[axis][kind], parts[3 * kind + axis]) for axis in range(3)] for kind in range(3)]
        put_source(first, 4, xyz, jnp.where(end, far[3][start : start + 4], parts[9] + parts[10] + parts[11]))
    split = [pieces(points_ref[axis]) for axis in range(3)]
    xyz = [[split[axis][kind] for axis in range(3)] for kind in range(3)]
    norm = put_source(4, 8, xyz, charges_ref[...])
    for kind_row, kind in enumerate((0, 1, 0, 2, 0, 1)):
        for axis in range(3):
            put(target_s, 0, 8, 3 * kind_row + axis, -2.0 * xyz[kind][axis])
    for i, part in enumerate(pieces(norm + SOFTENING * SOFTENING)):
        put(target_s, 0, 8, 18 + i, part)
        put(target_s, 0, 8, 21 + i, jnp.ones((8, 128), F32))
    for s in range(16):
        source_b[s] = source_s[32 * s : 32 * s + 32, :].astype(BF16)

    def tile(t, _):
        target = target_s[pl.ds(pl.multiple_of(32 * t, 32), 32), :].T.astype(BF16)
        total = jnp.zeros((128, 128), F32)
        for j in range(0, 8, 2):
            sources, weights = [], []
            for i in (j, j + 1):
                number = list_ref[t, i]
                place = jnp.clip(number - (device * 8 - HALO_T), 0, 15)
                sources.append(source_b[place])
                weights.append(q_s[pl.ds(place, 1), :] * jnp.where(number >= 0, 1.0, 0.0))
            square = dot(target, jnp.concatenate(sources, axis=1))
            total += weights[0] * lax.rsqrt(square[:, 0:128]) + weights[1] * lax.rsqrt(square[:, 128:256])
        out_ref[pl.ds(t, 1), :] = jnp.sum(total.T, axis=0, keepdims=True)
        return 0

    lax.fori_loop(0, 8, tile, 0)


def near(near_src, points, charges, recv, edge):
    vmem = pl.BlockSpec(memory_space=pltpu.VMEM)
    return pl.pallas_call(
        near_kernel,
        out_shape=jax.ShapeDtypeStruct((8, 128), F32),
        in_specs=[pl.BlockSpec(memory_space=pltpu.SMEM), vmem, vmem, vmem, vmem],
        scratch_shapes=[
            pltpu.VMEM((512, 128), F32),
            pltpu.VMEM((256, 128), F32),
            pltpu.VMEM((16, 32, 128), BF16),
            pltpu.VMEM((16, 128), F32),
            pltpu.VMEM((128, 128), F32),
        ],
        compiler_params=pltpu.CompilerParams(vmem_limit_bytes=VMEM_LIMIT),
        cost_estimate=pl.CostEstimate(flops=1_500_000_000, bytes_accessed=100_000, transcendentals=1_000_000),
        name="near",
    )(near_src, points, charges, recv, edge)


def down_kernel(
    recv_ref, partial_ref, far_ref, par_ref, top_ref, m2l_ref, l2l_ref,
    out_ref, far_z, top_z, parents_s, leaves_s,
):
    me = lax.axis_index("gy")
    recv = jnp.concatenate([recv_ref[s, 0:16, :] for s in range(16)], axis=0)
    for k in range(8):
        z = dot(recv, m2l_ref[k]).reshape(16, 16, 256)
        far_z[128 * k : 128 * k + 128, :] = z[:, :8].reshape(128, 256).astype(BF16)
        top_z[128 * k : 128 * k + 128, :] = z[:, 8:].reshape(128, 256).astype(BF16)
    top_local = dot(top_ref[...], top_z[...]).astype(BF16)
    own = (iota((8, 128), 1) == 32 + 4 * me + iota((8, 128), 0)) & (iota((8, 128), 0) < 4)
    top_local = dot(own.astype(F32).astype(BF16), top_local).astype(BF16)
    for c in range(8):
        put_every_eighth(parents_s, c, 4, dot(top_local, l2l_ref[c])[0:4])
    parent_local = (par_ref[...] + wide(parents_s[...])).astype(BF16)
    for c in range(8):
        put_every_eighth(leaves_s, c, 32, dot(parent_local, l2l_ref[c]))
    total = partial_ref[...] + dot(far_ref[...], far_z[...])
    out_ref[...] = (total + wide(leaves_s[...])).astype(BF16)


def down(recv, partial, far, par, top, m2l, l2l):
    return pl.pallas_call(
        down_kernel,
        out_shape=jax.ShapeDtypeStruct((256, 256), BF16),
        scratch_shapes=[
            pltpu.VMEM((1024, 256), BF16),
            pltpu.VMEM((1024, 256), BF16),
            pltpu.VMEM((2, 32, 128), F32),
            pltpu.VMEM((2, 256, 128), F32),
        ],
        compiler_params=pltpu.CompilerParams(vmem_limit_bytes=VMEM_LIMIT),
        cost_estimate=pl.CostEstimate(flops=1_500_000_000, bytes_accessed=3_500_000, transcendentals=0),
        name="down",
    )(recv, partial, far, par, top, m2l, l2l)


def shifted(block, axis, distance):
    size = lax.axis_size(axis)
    route = [(i, i + distance) for i in range(size) if 0 <= i + distance < size]
    return lax.ppermute(block, axis, route)


def across(block):
    rows, width = lax.axis_size("gx"), lax.axis_size("gy")
    ends = [(g * width + width - 1, (g + 1) * width) for g in range(rows - 1)]
    return lax.ppermute(block, ("gx", "gy"), ends + [(b, a) for a, b in ends])


def per_device(
    leaf_moments, leaf_src, leaf_cls, send_rows, send_count, par_src, par_cls, top_src, top_cls,
    points, charges, near_src, m2m_ops, m2l_ops, l2l_ops,
):
    points = points.transpose(1, 0, 2)
    edge = across(jnp.concatenate([points, charges[None]], axis=0))
    sent, parents = pack(
        leaf_moments, m2m_ops, send_rows[0].transpose(0, 2, 1), send_count[0], points, charges
    )
    before = shifted(parents, "gx", 1)
    after = shifted(parents, "gx", -1)
    recv = lax.all_to_all(sent, "gy", 0, 0, tiled=True)
    partial, far, par, top = lists(
        leaf_moments, m2l_ops, before, parents, after,
        leaf_src.T, leaf_cls.T, par_src, par_cls, top_src.T, top_cls.T,
    )
    leaf_local = down(recv, partial, far, par, top, m2l_ops, l2l_ops)
    near_total = near(near_src, points, charges, recv, edge)
    return leaf_local, near_total


def solution(mesh):
    both = P(("gx", "gy"))
    return jax.shard_map(
        per_device,
        mesh=mesh,
        in_specs=(both, both, both, P("gx"), P("gx"), both, both, P("gx"), P("gx"), both, both, both, P(), P(), P()),
        out_specs=(both, both),
        check_vma=False,
    )
```

time: 46.3 us -> 37.4 us (0.81)
  the two profiles are of different devices: /device:TPU:384 before, /device:TPU:385 now
where the time goes in v2:
time: 37.4 us; the launch traced here: 37.1 us
  starting transfers between devices  21.4 us (57%)
  Pallas kernels  14 us (37%)
  between operations  0.91 us (2%)
  local copies, waits for them, and re-layouts  0.78 us (2%)
    ppermute x1, starting transfers between devices, across(): return lax.ppermute(block, ('gx', 'gy'), ends + [(b, a) for a, b in ends])  9.36 us
    all_to_all x1, starting transfers between devices, per_device(): recv = lax.all_to_all(sent, 'gy', 0, 0, tiled=True)  6.9 us
    ppermute x2, starting transfers between devices, shifted(): return lax.ppermute(block, axis, route)  5.13 us
    pallas_call x1, Pallas kernels, lists(): pl.pallas_call(lists_kernel, out_shape=(jax.ShapeDtypeStruct((256, 256),...  4.4 us
    pallas_call x1, Pallas kernels, near(): pl.pallas_call(near_kernel, out_shape=jax.ShapeDtypeStruct((8, 128), F32)...  4.23 us
    pallas_call x1, Pallas kernels, pack(): pl.pallas_call(pack_kernel, out_shape=(jax.ShapeDtypeStruct((16, 48, 256)...  3 us
    pallas_call x1, Pallas kernels, down(): pl.pallas_call(down_kernel, out_shape=jax.ShapeDtypeStruct((256, 256), BF...  2.34 us
    unnamed x30, local copies, waits for them, and re-layouts  0.78 us
  transfers between devices with their start and end apart: 4, of which 0 were waited for; matrix products, arithmetic and copies ran while one was open for 0% of the time, Pallas kernels for 12%

profile of v2, /device:TPU:385, one launch (start us, length us, event | category | flops | bytes accessed | tf_op | source)
XLA Modules:
  0.0 37.1 jit_solution(4799503088468642103)
XLA Ops:
  0.6 0.0 copy-start.3
  0.6 3.0 %pack.1 = (bf16[16,48,256]{2,1,0:T(8,128)(2,1)}, bf16[32,256]{1,0:T(8,128)(2,1)}) custom-call(bf16[256,256]{1,0:T(8,128)(2,1)} %leaf_ref.1, bf16[8,256,256]{2,1,0:T(8,128)(2,1)} %m2m_hbm.1, s32[16,8,16]{2,1,0:T(8,128)} %bitcast.18, s32[16,16]{1,0:T(8,128)} %bitcast.19, f32[3,8,128]{2,1,0:T(8,128)} %bitcast.10, f32[8,128]{1,0:T(8,128)} %charges_ref.1), custom_call_target="tpu_custom_call" | custom-call | flops 200000000 | bytes 1500000 | tf_op jit(solution)/shard_map/pack/pallas_call | solution.py:116
  3.6 3.2 %collective-permute-start = (bf16[32,256]{1,0:T(8,128)(2,1)}, bf16[32,256]{1,0:T(8,128)(2,1)S(1)}, u32[]{:S(2)}, u32[]{:S(2)}) collective-permute-start(bf16[32,256]{1,0:T(8,128)(2,1)} %get-tuple-element.9.parents_ref), channel_id=1, source_target_pairs={{0,16},{16,32},{32,48},{48,64},{64,80},{80,96},{96,112},{112,128},... | collective-permute-start | bytes 49160 | tf_op jit(solution)/shard_map/ppermute | solution.py:390
  6.9 1.9 %collective-permute-start.1 = (bf16[32,256]{1,0:T(8,128)(2,1)}, bf16[32,256]{1,0:T(8,128)(2,1)S(1)}, u32[]{:S(2)}, u32[]{:S(2)}) collective-permute-start(bf16[32,256]{1,0:T(8,128)(2,1)} %get-tuple-element.9.parents_ref), channel_id=1, source_target_pairs={{16,0},{32,16},{48,32},{64,48},{80,64},{96,80},{112,96},{128,112},... | collective-permute-start | bytes 49160 | tf_op jit(solution)/shard_map/ppermute | solution.py:390
  8.8 0.0 copy-start.1
  8.8 0.0 copy-start.2
  8.8 0.0 copy-start
  8.8 0.0 copy-start.6
  8.8 0.0 copy-start.7
  8.9 0.0 copy-start.8
  8.9 0.0 copy-start.9
  8.9 0.0 copy-start.10
  8.9 0.0 copy-start.11
  8.9 6.9 %all-to-all-start = ((bf16[16,48,256]{2,1,0:T(8,128)(2,1)}), bf16[16,48,256]{2,1,0:T(8,128)(2,1)S(1)}, u32[]{:S(2)}, u32[]{:S(2)}) async-start(bf16[16,48,256]{2,1,0:T(8,128)(2,1)} %get-tuple-element.8), calls=%async_computation | async-start | bytes 786432 | tf_op jit(solution)/shard_map/all_to_all | solution.py:410
  15.8 0.0 copy-start.5
  15.8 0.0 copy-done.1
  15.8 0.0 copy-done.2
  15.9 9.4 %collective-permute-start.2 = (f32[4,8,128]{2,1,0:T(8,128)S(1)}, f32[4,8,128]{2,1,0:T(8,128)S(1)}, u32[]{:S(2)}, u32[]{:S(2)}) collective-permute-start(f32[4,8,128]{2,1,0:T(8,128)S(1)} %pad_maximum_fusion), channel_id=1, source_target_pairs={{15,16},{31,32},{47,48},{63,64},{79,80},{95,96},{111,112},{127,128... | collective-permute-start | bytes 49160 | tf_op jit(solution)/shard_map/ppermute | solution.py:396
  25.2 0.0 collective-permute-done.before_ref
  25.2 0.0 collective-permute-done.1.after_ref
  25.2 0.0 copy-done.3
  25.3 0.0 copy-done
  25.3 0.0 copy-done.6
  25.3 0.0 copy-done.7
  25.3 0.0 copy-done.8
  25.3 0.0 copy-done.9
  25.3 0.0 copy-done.10
  25.3 0.0 copy-done.11
  25.3 0.0 copy-done.5
  25.3 0.0 copy-start.12
  25.3 4.4 %lists.1 = (f32[256,256]{1,0:T(8,128)S(1)}, bf16[256,1024]{1,0:T(8,128)(2,1)S(1)}, f32[32,256]{1,0:T(8,128)S(1)}, bf16[128,1024]{1,0:T(8,128)(2,1)S(1)}) custom-call(bf16[256,256]{1,0:T(8,128)(2,1)S(1)} %copy-done, bf16[8,256,256]{2,1,0:T(8,128)(2,1)S(1)} %copy-done.3, bf16[32,256]{1,0:T(8,128)(2,1)S(1)} %collective-permute-done.before_ref, ...), custom_call_target="tpu_custom_call" | custom-call | flops 4000000000 | bytes 2500000 | tf_op jit(solution)/shard_map/lists/pallas_call | solution.py:236
  29.8 0.0 copy-start.13
  29.8 0.7 %copy-done.13 = bf16[128,1024]{1,0:T(8,128)(2,1)} copy-done((bf16[128,1024]{1,0:T(8,128)(2,1)}, bf16[128,1024]{1,0:T(8,128)(2,1)S(1)}, u32[]{:S(2)}) %copy-start.13) | copy-done | bytes 262168
  30.5 0.0 copy-start.4
  30.5 0.0 collective-permute-done.2.edge_ref
  30.5 0.0 all-to-all-done.recv_ref
  30.5 0.0 copy-done.12
  30.5 0.0 copy-start.14
  30.5 4.2 %near.1 = f32[8,128]{1,0:T(8,128)} custom-call(s32[8,8]{1,0:T(8,128)S(1)} %copy-done.12, f32[3,8,128]{2,1,0:T(8,128)S(1)} %bitcast.12, f32[8,128]{1,0:T(8,128)S(1)} %copy-done.2, bf16[16,48,256]{2,1,0:T(8,128)(2,1)S(1)} %all-to-all-done.recv_ref, f32[4,8,128]{2,1,0:T(8,128)S(1)} %collective-permute-done.2.edge_ref), custom_call_target="tpu_custom_call" | custom-call | flops 1500000000 | bytes 100000 | tf_op jit(solution)/shard_map/near/pallas_call | solution.py:332
  34.7 0.0 copy-done.4
  34.7 0.0 copy-done.14
  34.7 2.3 %down.1 = bf16[256,256]{1,0:T(8,128)(2,1)} custom-call(bf16[16,48,256]{2,1,0:T(8,128)(2,1)S(1)} %all-to-all-done.recv_ref, f32[256,256]{1,0:T(8,128)S(1)} %get-tuple-element.10.partial_ref, bf16[256,1024]{1,0:T(8,128)(2,1)S(1)} %get-tuple-element.11.far_ref, f32[32,256]{1,0:T(8,128)S(1)} %get-tuple-element.12.par_ref, bf16[128,1024]{1,0:T(8,128)(2,1)S(1)} %copy-done.14, ...), custom_call_target="tpu_custom_call" | custom-call | flops 1500000000 | bytes 3500000 | tf_op jit(solution)/shard_map/down/pallas_call | solution.py:372
  (1 shorter events, 0.0 us)
Async XLA Ops:
  0.6 24.6 %copy-start.3 = (bf16[8,256,256]{2,1,0:T(8,128)(2,1)S(1)}, bf16[8,256,256]{2,1,0:T(8,128)(2,1)}, u32[]{:S(2)}) copy-start(bf16[8,256,256]{2,1,0:T(8,128)(2,1)} %m2l_ref.3) | copy-start | bytes 3145732
  3.6 21.6 %collective-permute-start = (bf16[32,256]{1,0:T(8,128)(2,1)}, bf16[32,256]{1,0:T(8,128)(2,1)S(1)}, u32[]{:S(2)}, u32[]{:S(2)}) collective-permute-start(bf16[32,256]{1,0:T(8,128)(2,1)} %get-tuple-element.9.parents_ref), channel_id=1, source_target_pairs={{0,16},{16,32},{32,48},{48,64},{64,80},{80,96},{96,112},{112,128},... | collective-permute-start | bytes 49160 | tf_op jit(solution)/shard_map/ppermute | solution.py:390
  6.9 18.4 %collective-permute-start.1 = (bf16[32,256]{1,0:T(8,128)(2,1)}, bf16[32,256]{1,0:T(8,128)(2,1)S(1)}, u32[]{:S(2)}, u32[]{:S(2)}) collective-permute-start(bf16[32,256]{1,0:T(8,128)(2,1)} %get-tuple-element.9.parents_ref), channel_id=1, source_target_pairs={{16,0},{32,16},{48,32},{64,48},{80,64},{96,80},{112,96},{128,112},... | collective-permute-start | bytes 49160 | tf_op jit(solution)/shard_map/ppermute | solution.py:390
  8.8 7.0 %copy-start.1 = (f32[8,3,128]{2,0,1:T(8,128)S(1)}, f32[8,3,128]{2,0,1:T(8,128)}, u32[]{:S(2)}) copy-start(f32[8,3,128]{2,0,1:T(8,128)} %param.24) | copy-start | bytes 36868
  8.8 7.0 %copy-start.2 = (f32[8,128]{1,0:T(8,128)S(1)}, f32[8,128]{1,0:T(8,128)}, u32[]{:S(2)}) copy-start(f32[8,128]{1,0:T(8,128)} %charges_ref.1) | copy-start | bytes 12292
  8.8 16.4 %copy-start = (bf16[256,256]{1,0:T(8,128)(2,1)S(1)}, bf16[256,256]{1,0:T(8,128)(2,1)}, u32[]{:S(2)}) copy-start(bf16[256,256]{1,0:T(8,128)(2,1)} %leaf_ref.1) | copy-start | bytes 393220
  8.8 16.4 %copy-start.6 = (s32[256,32]{0,1:T(8,128)S(1)}, s32[256,32]{0,1:T(8,128)}, u32[]{:S(2)}) copy-start(s32[256,32]{0,1:T(8,128)} %param.17) | copy-start | bytes 98308
  8.8 16.4 %copy-start.7 = (s32[32,32]{1,0:T(8,128)S(1)}, s32[32,32]{1,0:T(8,128)}, u32[]{:S(2)}) copy-start(s32[32,32]{1,0:T(8,128)} %par_src_hbm.1) | copy-start | bytes 12292
  8.9 16.4 %copy-start.8 = (s32[32,32]{1,0:T(8,128)S(1)}, s32[32,32]{1,0:T(8,128)}, u32[]{:S(2)}) copy-start(s32[32,32]{1,0:T(8,128)} %par_cls_hbm.1) | copy-start | bytes 12292
  8.9 16.4 %copy-start.9 = (s32[64,32]{0,1:T(8,128)S(1)}, s32[64,32]{0,1:T(8,128)}, u32[]{:S(2)}) copy-start(s32[64,32]{0,1:T(8,128)} %param.22) | copy-start | bytes 24580
  8.9 16.4 %copy-start.10 = (s32[64,32]{0,1:T(8,128)S(1)}, s32[64,32]{0,1:T(8,128)}, u32[]{:S(2)}) copy-start(s32[64,32]{0,1:T(8,128)} %param.23) | copy-start | bytes 24580
  8.9 16.4 %copy-start.11 = (bf16[32,256]{1,0:T(8,128)(2,1)S(1)}, bf16[32,256]{1,0:T(8,128)(2,1)}, u32[]{:S(2)}) copy-start(bf16[32,256]{1,0:T(8,128)(2,1)} %get-tuple-element.9.parents_ref) | copy-start | bytes 49156
  8.9 21.6 %all-to-all-start = ((bf16[16,48,256]{2,1,0:T(8,128)(2,1)}), bf16[16,48,256]{2,1,0:T(8,128)(2,1)S(1)}, u32[]{:S(2)}, u32[]{:S(2)}) async-start(bf16[16,48,256]{2,1,0:T(8,128)(2,1)} %get-tuple-element.8), calls=%async_computation | async-start | bytes 786432 | tf_op jit(solution)/shard_map/all_to_all | solution.py:410
  15.8 9.5 %copy-start.5 = (s32[256,32]{0,1:T(8,128)S(1)}, s32[256,32]{0,1:T(8,128)}, u32[]{:S(2)}) copy-start(s32[256,32]{0,1:T(8,128)} %param.16) | copy-start | bytes 98308
  15.9 14.6 %collective-permute-start.2 = (f32[4,8,128]{2,1,0:T(8,128)S(1)}, f32[4,8,128]{2,1,0:T(8,128)S(1)}, u32[]{:S(2)}, u32[]{:S(2)}) collective-permute-start(f32[4,8,128]{2,1,0:T(8,128)S(1)} %pad_maximum_fusion), channel_id=1, source_target_pairs={{15,16},{31,32},{47,48},{63,64},{79,80},{95,96},{111,112},{127,128... | collective-permute-start | bytes 49160 | tf_op jit(solution)/shard_map/ppermute | solution.py:396
  25.3 5.1 %copy-start.12 = (s32[8,8]{1,0:T(8,128)S(1)}, s32[8,8]{1,0:T(8,128)}, u32[]{:S(2)}) copy-start(s32[8,8]{1,0:T(8,128)} %list_ref.1) | copy-start | bytes 772
  29.8 0.7 %copy-start.13 = (bf16[128,1024]{1,0:T(8,128)(2,1)}, bf16[128,1024]{1,0:T(8,128)(2,1)S(1)}, u32[]{:S(2)}) copy-start(bf16[128,1024]{1,0:T(8,128)(2,1)S(1)} %get-tuple-element.13.top_ref) | copy-start | bytes 786436
  30.5 4.3 %copy-start.4 = (bf16[8,256,256]{2,1,0:T(8,128)(2,1)S(1)}, bf16[8,256,256]{2,1,0:T(8,128)(2,1)}, u32[]{:S(2)}) copy-start(bf16[8,256,256]{2,1,0:T(8,128)(2,1)} %l2l_ref.1) | copy-start | bytes 3145732
  30.5 4.2 %copy-start.14 = (bf16[128,1024]{1,0:T(8,128)(2,1)S(1)}, bf16[128,1024]{1,0:T(8,128)(2,1)}, u32[]{:S(2)}) copy-start(bf16[128,1024]{1,0:T(8,128)(2,1)} %copy-done.13) | copy-start | bytes 786436

commit v3 on v2

v3 whole, which is shorter than its diff:
```python
import jax
import jax.numpy as jnp
from jax import lax
from jax.experimental import pallas as pl
from jax.experimental.pallas import tpu as pltpu
from jax.sharding import PartitionSpec as P

F32 = jnp.float32
BF16 = jnp.bfloat16
I32 = jnp.int32

HALO_T = 4
SOFTENING = 0.05
VMEM_LIMIT = 10 * 1024 * 1024
PACK_VMEM = 60 * 1024 * 1024


def iota(shape, dim):
    return lax.broadcasted_iota(I32, shape, dim)


def dot(a, b):
    return jnp.dot(a, b, preferred_element_type=F32)


def dot_nt(a, b):
    return lax.dot_general(a, b, (((1,), (1,)), ((), ())), preferred_element_type=F32)


def dot_tn(a, b):
    return lax.dot_general(a, b, (((0,), (0,)), ((), ())), preferred_element_type=F32)


def pieces(x):
    high = x.astype(BF16).astype(F32)
    rest = x - high
    middle = rest.astype(BF16).astype(F32)
    return high, middle, rest - middle


def wide(value):
    return jnp.concatenate([value[0], value[1]], axis=1)


def every_eighth(ref, first, count):
    return wide([ref[half, pl.ds(first, count, stride=8), :] for half in range(2)])


def put_every_eighth(ref, first, count, value):
    for half in range(2):
        ref[half, pl.ds(first, count, stride=8), :] = value[:, 128 * half : 128 * half + 128]


def fetch(copies):
    for copy in copies:
        copy.start()
    return copies


def tile_rows(parts, first):
    high = jnp.concatenate([part[0][first : first + HALO_T] for part in parts], axis=0)
    rest = jnp.concatenate([part[1][first : first + HALO_T] for part in parts], axis=0)
    return jnp.concatenate([high, rest], axis=1)


def pack_kernel(
    leaf_hbm, m2m_hbm, rows_hbm, count_hbm, points_hbm, charges_hbm, send_hbm, parents_hbm, edge_hbm,
    leaf_ref, m2m_ref, rows_ref, count_ref, points_ref, charges_ref, leaf_s, parents_s, send_ref, parents_ref, edge_ref, sems,
):
    me = lax.axis_index("gy")
    pairs = (
        (leaf_hbm, leaf_ref), (rows_hbm.at[me], rows_ref), (count_hbm, count_ref),
        (points_hbm, points_ref), (charges_hbm, charges_ref), (m2m_hbm, m2m_ref),
    )
    copies = fetch([pltpu.make_async_copy(a, b, sems.at[i]) for i, (a, b) in enumerate(pairs)])
    parents_s[:, 32:64, :] = jnp.zeros((2, 32, 128), F32)
    for copy in copies[:5]:
        copy.wait()
    leaf = leaf_ref[...]
    for half in range(2):
        leaf_s[half] = leaf[:, 128 * half : 128 * half + 128].astype(F32)
    table = rows_ref[...].astype(F32)
    live = iota((8, 16), 0) < count_ref[pl.ds(me, 1), :]
    table = jnp.where(live, table, -1.0).astype(BF16)
    repeat = (iota((128, 16), 0) // 8 == iota((128, 16), 1)).astype(F32).astype(BF16)
    spread = dot_nt(repeat, table)
    column = jnp.sum(
        jnp.where(iota((128, 8), 0) % 8 == iota((128, 8), 1), spread, 0.0), axis=1, keepdims=True
    )
    pick = (iota((128, 256), 1).astype(F32) == column).astype(F32).astype(BF16)
    sent = dot(pick, leaf)
    parts = [pieces(x) for x in (points_ref[0], points_ref[1], points_ref[2], charges_ref[...])]
    edge_ref[0:3] = points_ref[...]
    edge_ref[3] = charges_ref[...]
    first = tile_rows(parts, 0)
    last = tile_rows(parts, 8 - HALO_T)
    for p in range(16):
        tiles = jnp.where(me + 1 == p, last, jnp.where(me - 1 == p, first, 0.0))
        send_ref[p, 16:32, :] = tiles.astype(BF16)
    stores = fetch([
        pltpu.make_async_copy(edge_ref, edge_hbm, sems.at[6]),
        pltpu.make_async_copy(send_ref.at[:, 16:32, :], send_hbm.at[:, 16:32, :], sems.at[7]),
    ])
    copies[5].wait()
    operators = m2m_ref[...].reshape(2048, 256)
    children = jnp.concatenate([every_eighth(leaf_s, c, 32) for c in range(8)], axis=1)
    parents = dot(children.astype(BF16), operators).astype(BF16)
    parents_ref[...] = parents
    stores += fetch([pltpu.make_async_copy(parents_ref, parents_hbm, sems.at[8])])
    for half in range(2):
        parents_s[half, 0:32, :] = parents[:, 128 * half : 128 * half + 128].astype(F32)
    children = jnp.concatenate([every_eighth(parents_s, c, 8) for c in range(8)], axis=1)
    top = dot(children.astype(BF16), operators)
    for p in range(16):
        send_ref[p, 0:16, :] = jnp.concatenate([sent[8 * p : 8 * p + 8], top], axis=0).astype(BF16)
    stores += fetch([pltpu.make_async_copy(send_ref.at[:, 0:16, :], send_hbm.at[:, 0:16, :], sems.at[9])])
    for copy in stores:
        copy.wait()


def pack(leaf, m2m, rows, count, points, charges):
    return pl.pallas_call(
        pack_kernel,
        out_shape=(
            jax.ShapeDtypeStruct((16, 32, 256), BF16),
            jax.ShapeDtypeStruct((32, 256), BF16),
            jax.ShapeDtypeStruct((4, 8, 128), F32),
        ),
        in_specs=[pl.BlockSpec(memory_space=pltpu.HBM)] * 6,
        out_specs=[pl.BlockSpec(memory_space=pltpu.HBM)] * 3,
        scratch_shapes=[
            pltpu.VMEM((256, 256), BF16),
            pltpu.VMEM((8, 256, 256), BF16),
            pltpu.VMEM((8, 16), I32),
            pltpu.VMEM((16, 16), I32),
            pltpu.VMEM((3, 8, 128), F32),
            pltpu.VMEM((8, 128), F32),
            pltpu.VMEM((2, 256, 128), F32),
            pltpu.VMEM((2, 64, 128), F32),
            pltpu.VMEM((16, 32, 256), BF16),
            pltpu.VMEM((32, 256), BF16),
            pltpu.VMEM((4, 8, 128), F32),
            pltpu.SemaphoreType.DMA((10,)),
        ],
        compiler_params=pltpu.CompilerParams(vmem_limit_bytes=PACK_VMEM),
        cost_estimate=pl.CostEstimate(flops=200_000_000, bytes_accessed=1_500_000, transcendentals=0),
        name="pack",
    )(leaf, m2m, rows, count, points, charges)


def fields(src_ref, val_ref, lanes, base, rows):
    at = iota((rows, 128), 0)
    even = jnp.zeros((rows, 128), I32)
    odd = jnp.zeros((rows, 128), I32)
    for first, last in ((0, 15), (15, 30), (30, 32)):
        word = jnp.zeros((rows, 128), I32)
        for j in range(first, last):
            hit = at == (src_ref[j : j + 1, lanes] - base)
            word += jnp.where(hit, val_ref[j : j + 1, lanes], 0)
        even += word & 0x0F0F0F0F
        odd += (word >> 4) & 0x0F0F0F0F
    return even, odd


def counts_of(even, odd, k):
    word = odd if k % 2 else even
    return ((word >> (8 * (k // 2))) & 0xFF).astype(F32).astype(BF16)


def field_of(cls):
    return jnp.where(cls >= 0, jnp.left_shift(1, 4 * jnp.maximum(cls, 0)), 0)


def lists_kernel(
    leaf_ref, m2l_ref, before_ref, parents_ref, after_ref, edge_ref, src_hbm, cls_hbm, par_src_hbm, par_cls_hbm, top_src_hbm, top_cls_hbm,
    partial_ref, far_ref, par_ref, top_ref,
    src_t, val_t, low_src, low_val, par_src_ref, par_cls_ref, top_src_ref, top_cls_ref, near_w, far_w, z_ref, small_w, par_z, sems,
):
    me = lax.axis_index("gy")
    device = lax.axis_index("gx") * 16 + me
    pairs = (
        (src_hbm, src_t), (cls_hbm, val_t), (par_src_hbm, par_src_ref), (par_cls_hbm, par_cls_ref),
        (top_src_hbm, top_src_ref), (top_cls_hbm, top_cls_ref),
    )
    copies = fetch([pltpu.make_async_copy(a, b, sems.at[i]) for i, (a, b) in enumerate(pairs)])
    leaf = leaf_ref[...]
    for k in range(8):
        z_ref[256 * k : 256 * k + 256, :] = dot(leaf, m2l_ref[k]).astype(BF16)
    bank = jnp.concatenate([before_ref[...], parents_ref[...], after_ref[...]], axis=0)
    for k in range(8):
        z = dot(bank, m2l_ref[k])
        par_z[128 * k : 128 * k + 128, :] = jnp.concatenate([z, jnp.zeros((32, 256), F32)], axis=0).astype(BF16)
    for copy in copies:
        copy.wait()
    src = src_t[...]
    src_t[...] = jnp.where(src >= 4096, src - (4096 - 256), src - 256 * me)
    val_t[...] = field_of(val_t[...])
    src = par_src_ref[...]
    place = (src // 32 - device + 16) // 16
    src = jnp.where(src >= 0, place * 32 + src % 32, -1)
    none = jnp.full((96, 32), -1, I32)
    src = jnp.concatenate([src, none], axis=0).T
    cls = jnp.concatenate([par_cls_ref[...], none], axis=0).T
    top = top_src_ref[...]
    top = jnp.where(top >= 0, (top // 4) * 8 + top % 4, -1)
    none = jnp.full((32, 32), -1, I32)
    low_src[...] = jnp.concatenate([src[:, 0:32], top, none], axis=1)
    low_val[...] = field_of(jnp.concatenate([cls[:, 0:32], top_cls_ref[...], none], axis=1))

    rows = 64

    def near_block(i, _):
        for half in range(2):
            lanes = slice(128 * half, 128 * half + 128)
            even, odd = fields(src_t, val_t, lanes, i * rows, rows)
            for k in range(8):
                near_w[pl.ds(pl.multiple_of(256 * k + i * rows, rows), rows), lanes] = counts_of(even, odd, k)
        return 0

    def far_block(i, _):
        for half in range(2):
            lanes = slice(128 * half, 128 * half + 128)
            even, odd = fields(src_t, val_t, lanes, 256 + i * rows, rows)
            for k in range(8):
                far_w[pl.ds(pl.multiple_of(128 * k + i * rows, rows), rows), lanes] = counts_of(even, odd, k)
        return 0

    def small_block(i, _):
        even, odd = fields(low_src, low_val, slice(0, 128), i * rows, rows)
        for k in range(8):
            small_w[pl.ds(pl.multiple_of(128 * k + i * rows, rows), rows), :] = counts_of(even, odd, k)
        return 0

    lax.fori_loop(0, 4, near_block, 0)
    lax.fori_loop(0, 2, far_block, 0)
    lax.fori_loop(0, 2, small_block, 0)
    partial_ref[...] = dot_tn(near_w[...], z_ref[...])
    for k in range(8):
        far_ref[:, 128 * k : 128 * k + 128] = far_w[128 * k : 128 * k + 128, :].T
    weights = small_w[...].T
    own = (iota((8, 128), 1) == 32 + 4 * me + iota((8, 128), 0)) & (iota((8, 128), 0) < 4)
    own = dot(own.astype(F32).astype(BF16), weights)
    top_ref[...] = jnp.concatenate([own[:, 128 * k : 128 * k + 128] for k in range(8)], axis=0).astype(BF16)
    par_ref[...] = dot(weights[0:32], par_z[...])


def lists(leaf, m2l, before, parents, after, edge, src, cls, par_src, par_cls, top_src, top_cls):
    vmem = pl.BlockSpec(memory_space=pltpu.VMEM)
    return pl.pallas_call(
        lists_kernel,
        out_shape=(
            jax.ShapeDtypeStruct((256, 256), F32),
            jax.ShapeDtypeStruct((256, 1024), BF16),
            jax.ShapeDtypeStruct((32, 256), F32),
            jax.ShapeDtypeStruct((64, 128), BF16),
        ),
        in_specs=[vmem] * 6 + [pl.BlockSpec(memory_space=pltpu.HBM)] * 6,
        scratch_shapes=[
            pltpu.VMEM((32, 256), I32),
            pltpu.VMEM((32, 256), I32),
            pltpu.VMEM((32, 128), I32),
            pltpu.VMEM((32, 128), I32),
            pltpu.VMEM((32, 32), I32),
            pltpu.VMEM((32, 32), I32),
            pltpu.VMEM((32, 64), I32),
            pltpu.VMEM((32, 64), I32),
            pltpu.VMEM((2048, 256), BF16),
            pltpu.VMEM((1024, 256), BF16),
            pltpu.VMEM((2048, 256), BF16),
            pltpu.VMEM((1024, 128), BF16),
            pltpu.VMEM((1024, 256), BF16),
            pltpu.SemaphoreType.DMA((6,)),
        ],
        compiler_params=pltpu.CompilerParams(vmem_limit_bytes=VMEM_LIMIT),
        cost_estimate=pl.CostEstimate(flops=4_000_000_000, bytes_accessed=2_500_000, transcendentals=0),
        name="lists",
    )(leaf, m2l, before, parents, after, edge, src, cls, par_src, par_cls, top_src, top_cls)


def put_rows(ref, first, count, row, value):
    ref[pl.ds(32 * first + row, count, stride=32), :] = value


def put_source(ref, first, count, xyz):
    split = [pieces(x) for x in xyz]
    for row, kind in enumerate((0, 0, 1, 0, 2, 1)):
        for axis in range(3):
            put_rows(ref, first, count, 3 * row + axis, split[axis][kind])
    norm = xyz[0] * xyz[0] + xyz[1] * xyz[1] + xyz[2] * xyz[2]
    for i, part in enumerate(pieces(norm)):
        put_rows(ref, first, count, 18 + i, jnp.ones((count, 128), F32))
        put_rows(ref, first, count, 21 + i, part)


def put_target(ref, xyz):
    split = [pieces(-2.0 * x) for x in xyz]
    for row, kind in enumerate((0, 1, 0, 2, 0, 1)):
        for axis in range(3):
            put_rows(ref, 0, 8, 3 * row + axis, split[axis][kind])
    norm = xyz[0] * xyz[0] + xyz[1] * xyz[1] + xyz[2] * xyz[2] + SOFTENING * SOFTENING
    for i, part in enumerate(pieces(norm)):
        put_rows(ref, 0, 8, 18 + i, part)
        put_rows(ref, 0, 8, 21 + i, jnp.ones((8, 128), F32))


def clear_rows(ref, tiles):
    for s in range(tiles):
        ref[32 * s + 24 : 32 * s + 32, :] = jnp.zeros((8, 128), F32)


def side_by_side(ref):
    return jnp.concatenate([ref[32 * s : 32 * s + 32, :] for s in range(8)], axis=1).astype(BF16)


def near_sum(list_ref, target_of, sources, places, charges, total_s):
    device = lax.axis_index("gx") * 16 + lax.axis_index("gy")
    number = list_ref[...]
    place = jnp.where(number >= 0, number - (device * 8 - HALO_T), -1)
    weights = []
    for i, s in enumerate(places):
        times = jnp.sum((place == s).astype(F32), axis=1, keepdims=True)
        weights.append(times * charges[i : i + 1, :])
    for t in range(8):
        square = dot_tn(target_of(t), sources)
        total = weights[0][t : t + 1, :] * lax.rsqrt(square[:, 0:128])
        for i in range(1, 8):
            total += weights[i][t : t + 1, :] * lax.rsqrt(square[:, 128 * i : 128 * i + 128])
        total_s[128 * t : 128 * t + 128, :] = total
    ones = jnp.ones((8, 128), BF16)
    row = 0.0
    for part in pieces(total_s[...]):
        row += dot_nt(ones, part.astype(BF16))[0:1, :]
    return jnp.concatenate([row[:, 128 * t : 128 * t + 128] for t in range(8)], axis=0)


def own_kernel(
    after_ref, list_ref, points_ref, charges_ref, out_ref, target_ref, source_s, target_s, total_s
):
    xyz = [points_ref[axis] for axis in range(3)]
    clear_rows(source_s, 8)
    clear_rows(target_s, 8)
    put_source(source_s, 0, 8, xyz)
    put_target(target_s, xyz)
    for t in range(8):
        target_ref[t] = target_s[32 * t : 32 * t + 32, :].astype(BF16)
    own = range(HALO_T, HALO_T + 8)
    out_ref[...] = near_sum(
        list_ref, lambda t: target_ref[t], side_by_side(source_s), own, charges_ref[...], total_s
    )


def own_tiles(after, near_src, points, charges):
    return pl.pallas_call(
        own_kernel,
        out_shape=(
            jax.ShapeDtypeStruct((8, 128), F32),
            jax.ShapeDtypeStruct((8, 32, 128), BF16),
        ),
        scratch_shapes=[
            pltpu.VMEM((256, 128), F32),
            pltpu.VMEM((256, 128), F32),
            pltpu.VMEM((1024, 128), F32),
        ],
        compiler_params=pltpu.CompilerParams(vmem_limit_bytes=VMEM_LIMIT),
        cost_estimate=pl.CostEstimate(flops=2_000_000_000, bytes_accessed=100_000, transcendentals=1_000_000),
        name="own_tiles",
    )(after, near_src, points, charges)


def finish_kernel(
    list_ref, target_ref, near_ref, recv_ref, edge_ref, partial_ref, far_ref, par_ref, top_ref, m2l_ref, l2l_ref,
    local_ref, near_out_ref, source_s, total_s, far_z, parents_s, leaves_s,
):
    me = lax.axis_index("gy")
    rows = recv_ref[:, 0:16, :].astype(F32)
    leaf_rows = rows[:, 0:8].reshape(128, 256).astype(BF16)
    top_rows = rows[:, 8:16].reshape(128, 256).astype(BF16)
    buckets = dot(top_ref[...], top_rows).astype(BF16).astype(F32)
    buckets = jnp.concatenate([buckets[8 * k : 8 * k + 8] for k in range(8)], axis=1)
    top_local = dot(buckets.astype(BF16), m2l_ref[...].reshape(2048, 256)).astype(BF16)
    for c in range(8):
        put_every_eighth(parents_s, c, 4, dot(top_local, l2l_ref[c])[0:4])
    for k in range(8):
        far_z[128 * k : 128 * k + 128, :] = dot(leaf_rows, m2l_ref[k]).astype(BF16)
    parent_local = (par_ref[...] + wide(parents_s[...])).astype(BF16)
    for c in range(8):
        put_every_eighth(leaves_s, c, 32, dot(parent_local, l2l_ref[c]))
    total = partial_ref[...] + dot(far_ref[...], far_z[...])
    local_ref[...] = (total + wide(leaves_s[...])).astype(BF16)

    below = recv_ref[jnp.maximum(me - 1, 0), 16:32, :].astype(F32)
    above = recv_ref[jnp.minimum(me + 1, 15), 16:32, :].astype(F32)
    clear_rows(source_s, 8)
    charges = []
    for first, rows, start, end in ((0, below, 4, me == 0), (4, above, 0, me == 15)):
        rows = rows[:, 0:128] + rows[:, 128:256]
        xyzq = [
            jnp.where(end, edge_ref[axis, start : start + 4, :], rows[4 * axis : 4 * axis + 4]) for axis in range(4)
        ]
        put_source(source_s, first, 4, xyzq[0:3])
        charges.append(xyzq[3])
    halo = (0, 1, 2, 3, 12, 13, 14, 15)
    near_out_ref[...] = near_ref[...] + near_sum(
        list_ref, lambda t: target_ref[t], side_by_side(source_s), halo, jnp.concatenate(charges, axis=0), total_s
    )


def finish(near_src, targets, near, recv, edge, partial, far, par, top, m2l, l2l):
    return pl.pallas_call(
        finish_kernel,
        out_shape=(jax.ShapeDtypeStruct((256, 256), BF16), jax.ShapeDtypeStruct((8, 128), F32)),
        scratch_shapes=[
            pltpu.VMEM((256, 128), F32),
            pltpu.VMEM((1024, 128), F32),
            pltpu.VMEM((1024, 256), BF16),
            pltpu.VMEM((2, 32, 128), F32),
            pltpu.VMEM((2, 256, 128), F32),
        ],
        compiler_params=pltpu.CompilerParams(vmem_limit_bytes=VMEM_LIMIT),
        cost_estimate=pl.CostEstimate(flops=3_000_000_000, bytes_accessed=3_500_000, transcendentals=1_000_000),
        name="finish",
    )(near_src, targets, near, recv, edge, partial, far, par, top, m2l, l2l)


def shifted(block, axis, distance):
    size = lax.axis_size(axis)
    route = [(i, i + distance) for i in range(size) if 0 <= i + distance < size]
    return lax.ppermute(block, axis, route)


def across(block):
    rows, width = lax.axis_size("gx"), lax.axis_size("gy")
    ends = [(g * width + width - 1, (g + 1) * width) for g in range(rows - 1)]
    return lax.ppermute(block, ("gx", "gy"), ends + [(b, a) for a, b in ends])


def per_device(
    leaf_moments, leaf_src, leaf_cls, send_rows, send_count, par_src, par_cls, top_src, top_cls,
    points, charges, near_src, m2m_ops, m2l_ops, l2l_ops,
):
    points = points.transpose(1, 0, 2)
    sent, parents, edge = pack(
        leaf_moments, m2m_ops, send_rows[0].transpose(0, 2, 1), send_count[0], points, charges
    )
    edge = across(edge)
    before = shifted(parents, "gx", 1)
    after = shifted(parents, "gx", -1)
    recv = lax.all_to_all(sent, "gy", 0, 0, tiled=True)
    partial, far, par, top = lists(
        leaf_moments, m2l_ops, before, parents, after, edge,
        leaf_src.T, leaf_cls.T, par_src, par_cls, top_src.T, top_cls.T,
    )
    near_own, targets = own_tiles(par, near_src, points, charges)
    return finish(near_src, targets, near_own, recv, edge, partial, far, par, top, m2l_ops, l2l_ops)


def solution(mesh):
    both = P(("gx", "gy"))
    return jax.shard_map(
        per_device,
        mesh=mesh,
        in_specs=(both, both, both, P("gx"), P("gx"), both, both, P("gx"), P("gx"), both, both, both, P(), P(), P()),
        out_specs=(both, both),
        check_vma=False,
    )
```

time: 37.4 us -> 32.3 us (0.86)
  the two profiles are of different devices: /device:TPU:385 before, /device:TPU:225 now
where the time goes in v3:
time: 32.3 us; the launch traced here: 32 us
  starting transfers between devices  18.1 us (56%)
  Pallas kernels  11.1 us (34%)
  waiting for transfers between devices  1.77 us (5%)
  between operations  0.9 us (3%)
    ppermute x1, starting transfers between devices, across(): return lax.ppermute(block, ('gx', 'gy'), ends + [(b, a) for a, b in ends])  7.4 us
    ppermute x2, starting transfers between devices, shifted(): return lax.ppermute(block, axis, route)  6.77 us
    pallas_call x1, Pallas kernels, lists(): pl.pallas_call(lists_kernel, out_shape=(jax.ShapeDtypeStruct((256, 256),...  4.29 us
    all_to_all x1, starting transfers between devices, per_device(): recv = lax.all_to_all(sent, 'gy', 0, 0, tiled=True)  3.95 us
    pallas_call x1, Pallas kernels, pack(): pl.pallas_call(pack_kernel, out_shape=(jax.ShapeDtypeStruct((16, 32, 256)...  2.94 us
    pallas_call x1, Pallas kernels, finish(): pl.pallas_call(finish_kernel, out_shape=(jax.ShapeDtypeStruct((256, 256),...  2.75 us
    all_to_all x1, waiting for transfers between devices, per_device(): recv = lax.all_to_all(sent, 'gy', 0, 0, tiled=True)  1.76 us
    pallas_call x1, Pallas kernels, own_tiles(): pl.pallas_call(own_kernel, out_shape=(jax.ShapeDtypeStruct((8, 128), F32)...  1.1 us
  transfers between devices with their start and end apart: 4, of which 1 were waited for; matrix products, arithmetic and copies ran while one was open for 0% of the time, Pallas kernels for 17%

profile of v3, /device:TPU:225, one launch (start us, length us, event | category | flops | bytes accessed | tf_op | source)
XLA Modules:
  0.0 32.0 jit_solution(5719686957727229760)
XLA Ops:
  0.6 0.0 copy-start.3
  0.6 2.9 %pack.1 = (bf16[16,32,256]{2,1,0:T(8,128)(2,1)}, bf16[32,256]{1,0:T(8,128)(2,1)}, f32[4,8,128]{2,1,0:T(8,128)}) custom-call(bf16[256,256]{1,0:T(8,128)(2,1)} %leaf_ref.1, bf16[8,256,256]{2,1,0:T(8,128)(2,1)} %m2m_hbm.1, s32[16,8,16]{2,1,0:T(8,128)} %bitcast.15, s32[16,16]{1,0:T(8,128)} %bitcast.16, f32[3,8,128]{2,1,0:T(8,128)} %bitcast.9, f32[8,128]{1,0:T(8,128)} %charges_ref.1), custom_call_target="tpu_custom_call" | custom-call | flops 200000000 | bytes 1500000 | tf_op jit(solution)/shard_map/pack/pallas_call | solution.py:122
  3.6 7.4 %collective-permute-start.2 = (f32[4,8,128]{2,1,0:T(8,128)}, f32[4,8,128]{2,1,0:T(8,128)S(1)}, u32[]{:S(2)}, u32[]{:S(2)}) collective-permute-start(f32[4,8,128]{2,1,0:T(8,128)} %get-tuple-element.12), channel_id=1, source_target_pairs={{15,16},{31,32},{47,48},{63,64},{79,80},{95,96},{111,112},{127,128... | collective-permute-start | bytes 49160 | tf_op jit(solution)/shard_map/ppermute | solution.py:434
  11.0 1.9 %collective-permute-start.1 = (bf16[32,256]{1,0:T(8,128)(2,1)}, bf16[32,256]{1,0:T(8,128)(2,1)S(1)}, u32[]{:S(2)}, u32[]{:S(2)}) collective-permute-start(bf16[32,256]{1,0:T(8,128)(2,1)} %get-tuple-element.11.parents_ref), channel_id=1, source_target_pairs={{16,0},{32,16},{48,32},{64,48},{80,64},{96,80},{112,96},{128,112},... | collective-permute-start | bytes 49160 | tf_op jit(solution)/shard_map/ppermute | solution.py:428
  12.9 4.9 %collective-permute-start = (bf16[32,256]{1,0:T(8,128)(2,1)}, bf16[32,256]{1,0:T(8,128)(2,1)S(1)}, u32[]{:S(2)}, u32[]{:S(2)}) collective-permute-start(bf16[32,256]{1,0:T(8,128)(2,1)} %get-tuple-element.11.parents_ref), channel_id=1, source_target_pairs={{0,16},{16,32},{32,48},{48,64},{64,80},{80,96},{96,112},{112,128},... | collective-permute-start | bytes 49160 | tf_op jit(solution)/shard_map/ppermute | solution.py:428
  17.8 0.0 copy-start
  17.8 0.0 copy-start.5
  17.8 0.0 copy-start.6
  17.8 0.0 copy-start.7
  17.8 0.0 copy-start.8
  17.8 0.0 copy-start.9
  17.9 0.0 copy-start.10
  17.9 0.0 copy-start.11
  17.9 3.9 %all-to-all-start = ((bf16[16,32,256]{2,1,0:T(8,128)(2,1)}), bf16[16,32,256]{2,1,0:T(8,128)(2,1)S(1)}, u32[]{:S(2)}, u32[]{:S(2)}) async-start(bf16[16,32,256]{2,1,0:T(8,128)(2,1)} %get-tuple-element.16), calls=%async_computation | async-start | bytes 524288 | tf_op jit(solution)/shard_map/all_to_all | solution.py:448
  21.8 0.0 collective-permute-done.2.edge_ref
  21.8 0.0 collective-permute-done.1.after_ref
  21.9 0.0 collective-permute-done.before_ref
  21.9 0.0 copy-done.3
  21.9 0.0 copy-done
  21.9 0.0 copy-done.5
  21.9 0.0 copy-done.6
  21.9 0.0 copy-done.7
  21.9 0.0 copy-done.8
  21.9 0.0 copy-done.9
  21.9 0.0 copy-done.10
  21.9 0.0 copy-done.11
  22.0 0.0 copy-start.1
  22.0 0.0 copy-start.2
  22.0 0.0 copy-start.12
  22.0 4.3 %lists.1 = (f32[256,256]{1,0:T(8,128)S(1)}, bf16[256,1024]{1,0:T(8,128)(2,1)S(1)}, f32[32,256]{1,0:T(8,128)S(1)}, bf16[64,128]{1,0:T(8,128)(2,1)S(1)}) custom-call(bf16[256,256]{1,0:T(8,128)(2,1)S(1)} %copy-done, bf16[8,256,256]{2,1,0:T(8,128)(2,1)S(1)} %copy-done.3, bf16[32,256]{1,0:T(8,128)(2,1)S(1)} %collective-permute-done.before_ref, ...), custom_call_target="tpu_custom_call" | custom-call | flops 4000000000 | bytes 2500000 | tf_op jit(solution)/shard_map/lists/pallas_call | solution.py:249
  26.3 0.0 copy-done.1
  26.3 0.0 copy-done.2
  26.3 0.0 copy-done.12
  26.3 0.0 copy-start.4
  26.3 1.1 %own_tiles.1 = (f32[8,128]{1,0:T(8,128)S(1)}, bf16[8,32,128]{2,1,0:T(8,128)(2,1)S(1)}) custom-call(f32[32,256]{1,0:T(8,128)S(1)} %get-tuple-element.13.after_ref.par_ref, s32[8,8]{1,0:T(8,128)S(1)} %copy-done.12, f32[3,8,128]{2,1,0:T(8,128)S(1)} %bitcast.10, f32[8,128]{1,0:T(8,128)S(1)} %copy-done.2), custom_call_target="tpu_custom_call" | custom-call | flops 2000000000 | bytes 100000 | tf_op jit(solution)/shard_map/own_tiles/pallas_call | solution.py:353
  27.4 1.8 %all-to-all-done.recv_ref = bf16[16,32,256]{2,1,0:T(8,128)(2,1)S(1)} async-done(((bf16[16,32,256]{2,1,0:T(8,128)(2,1)}), bf16[16,32,256]{2,1,0:T(8,128)(2,1)S(1)}, u32[]{:S(2)}, u32[]{:S(2)}) %all-to-all-start) | async-done | bytes 262176 | tf_op jit(solution)/shard_map/all_to_all | solution.py:448
  29.2 0.0 copy-done.4
  29.2 2.7 %finish.1 = (bf16[256,256]{1,0:T(8,128)(2,1)}, f32[8,128]{1,0:T(8,128)}) custom-call(s32[8,8]{1,0:T(8,128)S(1)} %copy-done.12, bf16[8,32,128]{2,1,0:T(8,128)(2,1)S(1)} %get-tuple-element.14.target_ref, f32[8,128]{1,0:T(8,128)S(1)} %get-tuple-element.15.near_ref, bf16[16,32,256]{2,1,0:T(8,128)(2,1)S(1)} %all-to-all-done.recv_ref, ...), custom_call_target="tpu_custom_call" | custom-call | flops 3000000000 | bytes 3500000 | tf_op jit(solution)/shard_map/finish/pallas_call | solution.py:409
Async XLA Ops:
  0.6 21.2 %copy-start.3 = (bf16[8,256,256]{2,1,0:T(8,128)(2,1)S(1)}, bf16[8,256,256]{2,1,0:T(8,128)(2,1)}, u32[]{:S(2)}) copy-start(bf16[8,256,256]{2,1,0:T(8,128)(2,1)} %m2l_ref.3) | copy-start | bytes 3145732
  3.6 18.2 %collective-permute-start.2 = (f32[4,8,128]{2,1,0:T(8,128)}, f32[4,8,128]{2,1,0:T(8,128)S(1)}, u32[]{:S(2)}, u32[]{:S(2)}) collective-permute-start(f32[4,8,128]{2,1,0:T(8,128)} %get-tuple-element.12), channel_id=1, source_target_pairs={{15,16},{31,32},{47,48},{63,64},{79,80},{95,96},{111,112},{127,128... | collective-permute-start | bytes 49160 | tf_op jit(solution)/shard_map/ppermute | solution.py:434
  11.0 10.9 %collective-permute-start.1 = (bf16[32,256]{1,0:T(8,128)(2,1)}, bf16[32,256]{1,0:T(8,128)(2,1)S(1)}, u32[]{:S(2)}, u32[]{:S(2)}) collective-permute-start(bf16[32,256]{1,0:T(8,128)(2,1)} %get-tuple-element.11.parents_ref), channel_id=1, source_target_pairs={{16,0},{32,16},{48,32},{64,48},{80,64},{96,80},{112,96},{128,112},... | collective-permute-start | bytes 49160 | tf_op jit(solution)/shard_map/ppermute | solution.py:428
  12.9 8.9 %collective-permute-start = (bf16[32,256]{1,0:T(8,128)(2,1)}, bf16[32,256]{1,0:T(8,128)(2,1)S(1)}, u32[]{:S(2)}, u32[]{:S(2)}) collective-permute-start(bf16[32,256]{1,0:T(8,128)(2,1)} %get-tuple-element.11.parents_ref), channel_id=1, source_target_pairs={{0,16},{16,32},{32,48},{48,64},{64,80},{80,96},{96,112},{112,128},... | collective-permute-start | bytes 49160 | tf_op jit(solution)/shard_map/ppermute | solution.py:428
  17.8 4.1 %copy-start = (bf16[256,256]{1,0:T(8,128)(2,1)S(1)}, bf16[256,256]{1,0:T(8,128)(2,1)}, u32[]{:S(2)}) copy-start(bf16[256,256]{1,0:T(8,128)(2,1)} %leaf_ref.1) | copy-start | bytes 393220
  17.8 4.1 %copy-start.5 = (s32[256,32]{0,1:T(8,128)S(1)}, s32[256,32]{0,1:T(8,128)}, u32[]{:S(2)}) copy-start(s32[256,32]{0,1:T(8,128)} %param.16) | copy-start | bytes 98308
  17.8 4.1 %copy-start.6 = (s32[256,32]{0,1:T(8,128)S(1)}, s32[256,32]{0,1:T(8,128)}, u32[]{:S(2)}) copy-start(s32[256,32]{0,1:T(8,128)} %param.17) | copy-start | bytes 98308
  17.8 4.1 %copy-start.7 = (s32[32,32]{1,0:T(8,128)S(1)}, s32[32,32]{1,0:T(8,128)}, u32[]{:S(2)}) copy-start(s32[32,32]{1,0:T(8,128)} %par_src_hbm.1) | copy-start | bytes 12292
  17.8 4.1 %copy-start.8 = (s32[32,32]{1,0:T(8,128)S(1)}, s32[32,32]{1,0:T(8,128)}, u32[]{:S(2)}) copy-start(s32[32,32]{1,0:T(8,128)} %par_cls_hbm.1) | copy-start | bytes 12292
  17.8 4.1 %copy-start.9 = (s32[64,32]{0,1:T(8,128)S(1)}, s32[64,32]{0,1:T(8,128)}, u32[]{:S(2)}) copy-start(s32[64,32]{0,1:T(8,128)} %param.22) | copy-start | bytes 24580
  17.9 4.1 %copy-start.10 = (s32[64,32]{0,1:T(8,128)S(1)}, s32[64,32]{0,1:T(8,128)}, u32[]{:S(2)}) copy-start(s32[64,32]{0,1:T(8,128)} %param.23) | copy-start | bytes 24580
  17.9 4.1 %copy-start.11 = (bf16[32,256]{1,0:T(8,128)(2,1)S(1)}, bf16[32,256]{1,0:T(8,128)(2,1)}, u32[]{:S(2)}) copy-start(bf16[32,256]{1,0:T(8,128)(2,1)} %get-tuple-element.11.parents_ref) | copy-start | bytes 49156
  17.9 11.3 %all-to-all-start = ((bf16[16,32,256]{2,1,0:T(8,128)(2,1)}), bf16[16,32,256]{2,1,0:T(8,128)(2,1)S(1)}, u32[]{:S(2)}, u32[]{:S(2)}) async-start(bf16[16,32,256]{2,1,0:T(8,128)(2,1)} %get-tuple-element.16), calls=%async_computation | async-start | bytes 524288 | tf_op jit(solution)/shard_map/all_to_all | solution.py:448
  22.0 4.3 %copy-start.1 = (f32[8,3,128]{2,0,1:T(8,128)S(1)}, f32[8,3,128]{2,0,1:T(8,128)}, u32[]{:S(2)}) copy-start(f32[8,3,128]{2,0,1:T(8,128)} %param.24) | copy-start | bytes 36868
  22.0 4.3 %copy-start.2 = (f32[8,128]{1,0:T(8,128)S(1)}, f32[8,128]{1,0:T(8,128)}, u32[]{:S(2)}) copy-start(f32[8,128]{1,0:T(8,128)} %charges_ref.1) | copy-start | bytes 12292
  22.0 4.3 %copy-start.12 = (s32[8,8]{1,0:T(8,128)S(1)}, s32[8,8]{1,0:T(8,128)}, u32[]{:S(2)}) copy-start(s32[8,8]{1,0:T(8,128)} %list_ref.3) | copy-start | bytes 772
  26.3 2.9 %copy-start.4 = (bf16[8,256,256]{2,1,0:T(8,128)(2,1)S(1)}, bf16[8,256,256]{2,1,0:T(8,128)(2,1)}, u32[]{:S(2)}) copy-start(bf16[8,256,256]{2,1,0:T(8,128)(2,1)} %l2l_ref.1) | copy-start | bytes 3145732

commit v4 on v3

--- a/solution.py
+++ b/solution.py
@@ -12,7 +12,7 @@
 HALO_T = 4
 SOFTENING = 0.05
 VMEM_LIMIT = 10 * 1024 * 1024
-PACK_VMEM = 60 * 1024 * 1024
+PACK_VMEM = 10 * 1024 * 1024
 
 
 def iota(shape, dim):
@@ -64,8 +64,8 @@
 
 
 def pack_kernel(
-    leaf_hbm, m2m_hbm, rows_hbm, count_hbm, points_hbm, charges_hbm, send_hbm, parents_hbm, edge_hbm,
-    leaf_ref, m2m_ref, rows_ref, count_ref, points_ref, charges_ref, leaf_s, parents_s, send_ref, parents_ref, edge_ref, sems,
+    leaf_hbm, m2m_hbm, rows_hbm, count_hbm, points_hbm, charges_hbm, send_ref, parents_ref, edge_ref,
+    leaf_ref, m2m_ref, rows_ref, count_ref, points_ref, charges_ref, leaf_s, parents_s, sems,
 ):
     me = lax.axis_index("gy")
     pairs = (
@@ -97,25 +97,17 @@
     for p in range(16):
         tiles = jnp.where(me + 1 == p, last, jnp.where(me - 1 == p, first, 0.0))
         send_ref[p, 16:32, :] = tiles.astype(BF16)
-    stores = fetch([
-        pltpu.make_async_copy(edge_ref, edge_hbm, sems.at[6]),
-        pltpu.make_async_copy(send_ref.at[:, 16:32, :], send_hbm.at[:, 16:32, :], sems.at[7]),
-    ])
     copies[5].wait()
     operators = m2m_ref[...].reshape(2048, 256)
     children = jnp.concatenate([every_eighth(leaf_s, c, 32) for c in range(8)], axis=1)
     parents = dot(children.astype(BF16), operators).astype(BF16)
     parents_ref[...] = parents
-    stores += fetch([pltpu.make_async_copy(parents_ref, parents_hbm, sems.at[8])])
     for half in range(2):
         parents_s[half, 0:32, :] = parents[:, 128 * half : 128 * half + 128].astype(F32)
     children = jnp.concatenate([every_eighth(parents_s, c, 8) for c in range(8)], axis=1)
     top = dot(children.astype(BF16), operators)
     for p in range(16):
         send_ref[p, 0:16, :] = jnp.concatenate([sent[8 * p : 8 * p + 8], top], axis=0).astype(BF16)
-    stores += fetch([pltpu.make_async_copy(send_ref.at[:, 0:16, :], send_hbm.at[:, 0:16, :], sems.at[9])])
-    for copy in stores:
-        copy.wait()
 
 
 def pack(leaf, m2m, rows, count, points, charges):
@@ -127,7 +119,6 @@
             jax.ShapeDtypeStruct((4, 8, 128), F32),
         ),
         in_specs=[pl.BlockSpec(memory_space=pltpu.HBM)] * 6,
-        out_specs=[pl.BlockSpec(memory_space=pltpu.HBM)] * 3,
         scratch_shapes=[
             pltpu.VMEM((256, 256), BF16),
             pltpu.VMEM((8, 256, 256), BF16),
@@ -137,15 +128,12 @@
             pltpu.VMEM((8, 128), F32),
             pltpu.VMEM((2, 256, 128), F32),
             pltpu.VMEM((2, 64, 128), F32),
-            pltpu.VMEM((16, 32, 256), BF16),
-            pltpu.VMEM((32, 256), BF16),
-            pltpu.VMEM((4, 8, 128), F32),
-            pltpu.SemaphoreType.DMA((10,)),
+            pltpu.SemaphoreType.DMA((6,)),
         ],
         compiler_params=pltpu.CompilerParams(vmem_limit_bytes=PACK_VMEM),
         cost_estimate=pl.CostEstimate(flops=200_000_000, bytes_accessed=1_500_000, transcendentals=0),
         name="pack",
-    )(leaf, m2m, rows, count, points, charges)
+    )(*[pltpu.with_memory_space_constraint(x, pltpu.HBM) for x in (leaf, m2m, rows, count, points, charges)])
 
 
 def fields(src_ref, val_ref, lanes, base, rows):
@@ -172,9 +160,9 @@
 
 
 def lists_kernel(
-    leaf_ref, m2l_ref, before_ref, parents_ref, after_ref, edge_ref, src_hbm, cls_hbm, par_src_hbm, par_cls_hbm, top_src_hbm, top_cls_hbm,
-    partial_ref, far_ref, par_ref, top_ref,
-    src_t, val_t, low_src, low_val, par_src_ref, par_cls_ref, top_src_ref, top_cls_ref, near_w, far_w, z_ref, small_w, par_z, sems,
+    leaf_ref, m2l_ref, parents_ref, edge_ref, src_hbm, cls_hbm, par_src_hbm, par_cls_hbm, top_src_hbm, top_cls_hbm,
+    partial_ref, far_ref, par_ref, top_ref, parents_out,
+    src_t, val_t, low_src, low_val, par_src_ref, par_cls_ref, top_src_ref, top_cls_ref, near_w, far_w, z_ref, small_w, sems,
 ):
     me = lax.axis_index("gy")
     device = lax.axis_index("gx") * 16 + me
@@ -186,10 +174,7 @@
     leaf = leaf_ref[...]
     for k in range(8):
         z_ref[256 * k : 256 * k + 256, :] = dot(leaf, m2l_ref[k]).astype(BF16)
-    bank = jnp.concatenate([before_ref[...], parents_ref[...], after_ref[...]], axis=0)
-    for k in range(8):
-        z = dot(bank, m2l_ref[k])
-        par_z[128 * k : 128 * k + 128, :] = jnp.concatenate([z, jnp.zeros((32, 256), F32)], axis=0).astype(BF16)
+    parents_out[...] = parents_ref[...]
     for copy in copies:
         copy.wait()
     src = src_t[...]
@@ -241,20 +226,22 @@
     own = (iota((8, 128), 1) == 32 + 4 * me + iota((8, 128), 0)) & (iota((8, 128), 0) < 4)
     own = dot(own.astype(F32).astype(BF16), weights)
     top_ref[...] = jnp.concatenate([own[:, 128 * k : 128 * k + 128] for k in range(8)], axis=0).astype(BF16)
-    par_ref[...] = dot(weights[0:32], par_z[...])
-
-
-def lists(leaf, m2l, before, parents, after, edge, src, cls, par_src, par_cls, top_src, top_cls):
+    for k in range(8):
+        par_ref[32 * k : 32 * k + 32, :] = weights[0:32, 128 * k : 128 * k + 128]
+
+
+def lists(leaf, m2l, parents, edge, src, cls, par_src, par_cls, top_src, top_cls):
     vmem = pl.BlockSpec(memory_space=pltpu.VMEM)
     return pl.pallas_call(
         lists_kernel,
         out_shape=(
             jax.ShapeDtypeStruct((256, 256), F32),
             jax.ShapeDtypeStruct((256, 1024), BF16),
-            jax.ShapeDtypeStruct((32, 256), F32),
+            jax.ShapeDtypeStruct((256, 128), BF16),
             jax.ShapeDtypeStruct((64, 128), BF16),
+            jax.ShapeDtypeStruct((32, 256), BF16),
         ),
-        in_specs=[vmem] * 6 + [pl.BlockSpec(memory_space=pltpu.HBM)] * 6,
+        in_specs=[vmem] * 4 + [pl.BlockSpec(memory_space=pltpu.HBM)] * 6,
         scratch_shapes=[
             pltpu.VMEM((32, 256), I32),
             pltpu.VMEM((32, 256), I32),
@@ -268,13 +255,12 @@
             pltpu.VMEM((1024, 256), BF16),
             pltpu.VMEM((2048, 256), BF16),
             pltpu.VMEM((1024, 128), BF16),
-            pltpu.VMEM((1024, 256), BF16),
             pltpu.SemaphoreType.DMA((6,)),
         ],
         compiler_params=pltpu.CompilerParams(vmem_limit_bytes=VMEM_LIMIT),
         cost_estimate=pl.CostEstimate(flops=4_000_000_000, bytes_accessed=2_500_000, transcendentals=0),
         name="lists",
-    )(leaf, m2l, before, parents, after, edge, src, cls, par_src, par_cls, top_src, top_cls)
+    )(leaf, m2l, parents, edge, src, cls, par_src, par_cls, top_src, top_cls)
 
 
 def put_rows(ref, first, count, row, value):
@@ -368,8 +354,8 @@
 
 
 def finish_kernel(
-    list_ref, target_ref, near_ref, recv_ref, edge_ref, partial_ref, far_ref, par_ref, top_ref, m2l_ref, l2l_ref,
-    local_ref, near_out_ref, source_s, total_s, far_z, parents_s, leaves_s,
+    list_ref, target_ref, near_ref, recv_ref, edge_ref, partial_ref, far_ref, top_ref, m2l_ref, l2l_ref,
+    field_ref, from_top_ref, near_out_ref, source_s, total_s, far_z, parents_s,
 ):
     me = lax.axis_index("gy")
     rows = recv_ref[:, 0:16, :].astype(F32)
@@ -382,11 +368,8 @@
         put_every_eighth(parents_s, c, 4, dot(top_local, l2l_ref[c])[0:4])
     for k in range(8):
         far_z[128 * k : 128 * k + 128, :] = dot(leaf_rows, m2l_ref[k]).astype(BF16)
-    parent_local = (par_ref[...] + wide(parents_s[...])).astype(BF16)
-    for c in range(8):
-        put_every_eighth(leaves_s, c, 32, dot(parent_local, l2l_ref[c]))
-    total = partial_ref[...] + dot(far_ref[...], far_z[...])
-    local_ref[...] = (total + wide(leaves_s[...])).astype(BF16)
+    from_top_ref[...] = wide(parents_s[...])
+    field_ref[...] = partial_ref[...] + dot(far_ref[...], far_z[...])
 
     below = recv_ref[jnp.maximum(me - 1, 0), 16:32, :].astype(F32)
     above = recv_ref[jnp.minimum(me + 1, 15), 16:32, :].astype(F32)
@@ -405,21 +388,50 @@
     )
 
 
-def finish(near_src, targets, near, recv, edge, partial, far, par, top, m2l, l2l):
+def finish(near_src, targets, near, recv, edge, partial, far, top, m2l, l2l):
     return pl.pallas_call(
         finish_kernel,
-        out_shape=(jax.ShapeDtypeStruct((256, 256), BF16), jax.ShapeDtypeStruct((8, 128), F32)),
+        out_shape=(
+            jax.ShapeDtypeStruct((256, 256), F32),
+            jax.ShapeDtypeStruct((32, 256), F32),
+            jax.ShapeDtypeStruct((8, 128), F32),
+        ),
         scratch_shapes=[
             pltpu.VMEM((256, 128), F32),
             pltpu.VMEM((1024, 128), F32),
             pltpu.VMEM((1024, 256), BF16),
             pltpu.VMEM((2, 32, 128), F32),
-            pltpu.VMEM((2, 256, 128), F32),
         ],
         compiler_params=pltpu.CompilerParams(vmem_limit_bytes=VMEM_LIMIT),
         cost_estimate=pl.CostEstimate(flops=3_000_000_000, bytes_accessed=3_500_000, transcendentals=1_000_000),
         name="finish",
-    )(near_src, targets, near, recv, edge, partial, far, par, top, m2l, l2l)
+    )(near_src, targets, near, recv, edge, partial, far, top, m2l, l2l)
+
+
+def leaves_kernel(
+    before_ref, parents_ref, after_ref, par_ref, from_top_ref, field_ref, m2l_ref, l2l_ref, local_ref, leaves_s
+):
+    bank = jnp.concatenate(
+        [before_ref[...], parents_ref[...], after_ref[...], jnp.zeros((32, 256), BF16)], axis=0
+    )
+    buckets = dot(par_ref[...], bank).astype(BF16)
+    buckets = jnp.concatenate([buckets[32 * k : 32 * k + 32] for k in range(8)], axis=1)
+    field = dot(buckets, m2l_ref[...].reshape(2048, 256))
+    parent_local = (field + from_top_ref[...]).astype(BF16)
+    for c in range(8):
+        put_every_eighth(leaves_s, c, 32, dot(parent_local, l2l_ref[c]))
+    local_ref[...] = (field_ref[...] + wide(leaves_s[...])).astype(BF16)
+
+
+def leaves(before, parents, after, par, from_top, field, m2l, l2l):
+    return pl.pallas_call(
+        leaves_kernel,
+        out_shape=jax.ShapeDtypeStruct((256, 256), BF16),
+        scratch_shapes=[pltpu.VMEM((2, 256, 128), F32)],
+        compiler_params=pltpu.CompilerParams(vmem_limit_bytes=VMEM_LIMIT),
+        cost_estimate=pl.CostEstimate(flops=500_000_000, bytes_accessed=3_000_000, transcendentals=0),
+        name="leaves",
+    )(before, parents, after, par, from_top, field, m2l, l2l)
 
 
 def shifted(block, axis, distance):
@@ -443,15 +455,19 @@
         leaf_moments, m2m_ops, send_rows[0].transpose(0, 2, 1), send_count[0], points, charges
     )
     edge = across(edge)
+    recv = lax.all_to_all(sent, "gy", 0, 0, tiled=True)
+    partial, far, par, top, parents = lists(
+        leaf_moments, m2l_ops, parents, edge,
+        leaf_src.T, leaf_cls.T, par_src, par_cls, top_src.T, top_cls.T,
+    )
     before = shifted(parents, "gx", 1)
     after = shifted(parents, "gx", -1)
-    recv = lax.all_to_all(sent, "gy", 0, 0, tiled=True)
-    partial, far, par, top = lists(
-        leaf_moments, m2l_ops, before, parents, after, edge,
-        leaf_src.T, leaf_cls.T, par_src, par_cls, top_src.T, top_cls.T,
-    )
-    near_own, targets = own_tiles(par, near_src, points, charges)
-    return finish(near_src, targets, near_own, recv, edge, partial, far, par, top, m2l_ops, l2l_ops)
+    near_own, targets = own_tiles(top, near_src, points, charges)
+    field, from_top, near_total = finish(
+        near_src, targets, near_own, recv, edge, partial, far, top, m2l_ops, l2l_ops
+    )
+    leaf_local = leaves(before, parents, after, par, from_top, field, m2l_ops, l2l_ops)
+    return leaf_local, near_total
 
 
 def solution(mesh):

time: 32.3 us -> 32.8 us (1.015)
  the two profiles are of different devices: /device:TPU:225 before, /device:TPU:386 now
where the time goes in v4:
time: 32.8 us; the launch traced here: 32.4 us
  starting transfers between devices  19 us (58%)
  Pallas kernels  12.4 us (38%)
  between operations  0.86 us (3%)
    all_to_all x1, starting transfers between devices, per_device(): recv = lax.all_to_all(sent, 'gy', 0, 0, tiled=True)  11.6 us
    ppermute x2, starting transfers between devices, shifted(): return lax.ppermute(block, axis, route)  6.77 us
    pallas_call x1, Pallas kernels, lists(): pl.pallas_call(lists_kernel, out_shape=(jax.ShapeDtypeStruct((256, 256),...  4.23 us
    pallas_call x1, Pallas kernels, pack(): pl.pallas_call(pack_kernel, out_shape=(jax.ShapeDtypeStruct((16, 32, 256)...  2.95 us
    pallas_call x1, Pallas kernels, finish(): pl.pallas_call(finish_kernel, out_shape=(jax.ShapeDtypeStruct((256, 256),...  2.62 us
    pallas_call x1, Pallas kernels, leaves(): pl.pallas_call(leaves_kernel, out_shape=jax.ShapeDtypeStruct((256, 256),...  1.5 us
    pallas_call x1, Pallas kernels, own_tiles(): pl.pallas_call(own_kernel, out_shape=(jax.ShapeDtypeStruct((8, 128), F32)...  1.1 us
    ppermute x1, starting transfers between devices, across(): return lax.ppermute(block, ('gx', 'gy'), ends + [(b, a) for a, b in ends])  0.66 us
  transfers between devices with their start and end apart: 4, of which 0 were waited for; matrix products, arithmetic and copies ran while one was open for 0% of the time, Pallas kernels for 25%

profile of v4, /device:TPU:386, one launch (start us, length us, event | category | flops | bytes accessed | tf_op | source)
XLA Modules:
  0.0 32.4 jit_solution(5790689493152739263)
XLA Ops:
  0.6 0.0 copy-start
  0.6 3.0 %pack.1 = (bf16[16,32,256]{2,1,0:T(8,128)(2,1)}, bf16[32,256]{1,0:T(8,128)(2,1)S(1)}, f32[4,8,128]{2,1,0:T(8,128)S(1)}) custom-call(bf16[256,256]{1,0:T(8,128)(2,1)} %leaf_ref.1, bf16[8,256,256]{2,1,0:T(8,128)(2,1)} %m2m_hbm.1, s32[16,8,16]{2,1,0:T(8,128)} %bitcast.15, s32[16,16]{1,0:T(8,128)} %bitcast.16, f32[3,8,128]{2,1,0:T(8,128)} %bitcast.9, ...), custom_call_target="tpu_custom_call" | custom-call | flops 200000000 | bytes 1500000 | tf_op jit(solution)/shard_map/pack/pallas_call | solution.py:114
  3.6 0.7 %collective-permute-start = (f32[4,8,128]{2,1,0:T(8,128)S(1)}, f32[4,8,128]{2,1,0:T(8,128)S(1)}, u32[]{:S(2)}, u32[]{:S(2)}) collective-permute-start(f32[4,8,128]{2,1,0:T(8,128)S(1)} %get-tuple-element.16), channel_id=1, source_target_pairs={{15,16},{31,32},{47,48},{63,64},{79,80},{95,96},{111,112},{127,128... | collective-permute-start | bytes 49160 | tf_op jit(solution)/shard_map/ppermute | solution.py:446
  4.3 0.0 copy-start.2
  4.3 0.0 copy-start.5
  4.3 0.0 copy-start.6
  4.3 0.0 copy-start.7
  4.3 0.0 copy-start.8
  4.3 0.0 copy-start.9
  4.3 0.0 copy-start.10
  4.4 11.6 %all-to-all-start = ((bf16[16,32,256]{2,1,0:T(8,128)(2,1)}), bf16[16,32,256]{2,1,0:T(8,128)(2,1)S(1)}, u32[]{:S(2)}, u32[]{:S(2)}) async-start(bf16[16,32,256]{2,1,0:T(8,128)(2,1)} %get-tuple-element.22), calls=%async_computation | async-start | bytes 524288 | tf_op jit(solution)/shard_map/all_to_all | solution.py:458
  15.9 0.0 collective-permute-done.edge_ref
  15.9 0.0 copy-done
  15.9 0.0 copy-done.2
  15.9 0.0 copy-done.5
  16.0 0.0 copy-done.6
  16.0 0.0 copy-done.7
  16.0 0.0 copy-done.8
  16.0 0.0 copy-done.9
  16.0 0.0 copy-done.10
  16.0 0.0 copy-start.3
  16.0 0.0 copy-start.4
  16.0 0.0 copy-start.11
  16.0 4.2 %lists.1 = (f32[256,256]{1,0:T(8,128)S(1)}, bf16[256,1024]{1,0:T(8,128)(2,1)S(1)}, bf16[256,128]{1,0:T(8,128)(2,1)S(1)}, bf16[64,128]{1,0:T(8,128)(2,1)S(1)}, bf16[32,256]{1,0:T(8,128)(2,1)S(1)}) custom-call(bf16[256,256]{1,0:T(8,128)(2,1)S(1)} %copy-done.2, bf16[8,256,256]{2,1,0:T(8,128)(2,1)S(1)} %copy-done, ...), custom_call_target="tpu_custom_call" | custom-call | flops 4000000000 | bytes 2500000 | tf_op jit(solution)/shard_map/lists/pallas_call | solution.py:235
  20.3 1.9 %collective-permute-start.1 = (bf16[32,256]{1,0:T(8,128)(2,1)S(1)}, bf16[32,256]{1,0:T(8,128)(2,1)S(1)}, u32[]{:S(2)}, u32[]{:S(2)}) collective-permute-start(bf16[32,256]{1,0:T(8,128)(2,1)S(1)} %get-tuple-element.17.parents_ref), channel_id=1, source_target_pairs={{0,16},{16,32},{32,48},{48,64},{64,80},{80,96},{96,112},{112,128},... | collective-permute-start | bytes 49160 | tf_op jit(solution)/shard_map/ppermute | solution.py:440
  22.2 4.9 %collective-permute-start.2 = (bf16[32,256]{1,0:T(8,128)(2,1)S(1)}, bf16[32,256]{1,0:T(8,128)(2,1)S(1)}, u32[]{:S(2)}, u32[]{:S(2)}) collective-permute-start(bf16[32,256]{1,0:T(8,128)(2,1)S(1)} %get-tuple-element.17.parents_ref), channel_id=1, source_target_pairs={{16,0},{32,16},{48,32},{64,48},{80,64},{96,80},{112,96},{128,112},... | collective-permute-start | bytes 49160 | tf_op jit(solution)/shard_map/ppermute | solution.py:440
  27.1 0.0 copy-done.3
  27.1 0.0 copy-done.4
  27.1 0.0 copy-done.11
  27.1 0.0 copy-start.1
  27.1 1.1 %own_tiles.1 = (f32[8,128]{1,0:T(8,128)S(1)}, bf16[8,32,128]{2,1,0:T(8,128)(2,1)S(1)}) custom-call(bf16[64,128]{1,0:T(8,128)(2,1)S(1)} %get-tuple-element.19.after_ref.top_ref, s32[8,8]{1,0:T(8,128)S(1)} %copy-done.11, f32[3,8,128]{2,1,0:T(8,128)S(1)} %bitcast.10, f32[8,128]{1,0:T(8,128)S(1)} %copy-done.4), custom_call_target="tpu_custom_call" | custom-call | flops 2000000000 | bytes 100000 | tf_op jit(solution)/shard_map/own_tiles/pallas_call | solution.py:339
  28.2 0.0 all-to-all-done.recv_ref
  28.2 0.1 copy-done.1
  28.3 2.6 %finish.1 = (f32[256,256]{1,0:T(8,128)S(1)}, f32[32,256]{1,0:T(8,128)S(1)}, f32[8,128]{1,0:T(8,128)}) custom-call(s32[8,8]{1,0:T(8,128)S(1)} %copy-done.11, bf16[8,32,128]{2,1,0:T(8,128)(2,1)S(1)} %get-tuple-element.20.target_ref, f32[8,128]{1,0:T(8,128)S(1)} %get-tuple-element.21.near_ref, bf16[16,32,256]{2,1,0:T(8,128)(2,1)S(1)} %all-to-all-done.recv_ref, ...), custom_call_target="tpu_custom_call" | custom-call | flops 3000000000 | bytes 3500000 | tf_op jit(solution)/shard_map/finish/pallas_call | solution.py:392
  30.9 0.0 collective-permute-done.1.before_ref
  30.9 0.0 collective-permute-done.2.after_ref
  31.0 1.5 %leaves.1 = bf16[256,256]{1,0:T(8,128)(2,1)} custom-call(bf16[32,256]{1,0:T(8,128)(2,1)S(1)} %collective-permute-done.1.before_ref, bf16[32,256]{1,0:T(8,128)(2,1)S(1)} %get-tuple-element.17.parents_ref, bf16[32,256]{1,0:T(8,128)(2,1)S(1)} %collective-permute-done.2.after_ref, bf16[256,128]{1,0:T(8,128)(2,1)S(1)} %get-tuple-element.18.par_ref, ...), custom_call_target="tpu_custom_call" | custom-call | flops 500000000 | bytes 3000000 | tf_op jit(solution)/shard_map/leaves/pallas_call | solution.py:427
Async XLA Ops:
  0.6 15.3 %copy-start = (bf16[8,256,256]{2,1,0:T(8,128)(2,1)S(1)}, bf16[8,256,256]{2,1,0:T(8,128)(2,1)}, u32[]{:S(2)}) copy-start(bf16[8,256,256]{2,1,0:T(8,128)(2,1)} %m2l_ref.5) | copy-start | bytes 3145732
  3.6 12.3 %collective-permute-start = (f32[4,8,128]{2,1,0:T(8,128)S(1)}, f32[4,8,128]{2,1,0:T(8,128)S(1)}, u32[]{:S(2)}, u32[]{:S(2)}) collective-permute-start(f32[4,8,128]{2,1,0:T(8,128)S(1)} %get-tuple-element.16), channel_id=1, source_target_pairs={{15,16},{31,32},{47,48},{63,64},{79,80},{95,96},{111,112},{127,128... | collective-permute-start | bytes 49160 | tf_op jit(solution)/shard_map/ppermute | solution.py:446
  4.3 11.7 %copy-start.2 = (bf16[256,256]{1,0:T(8,128)(2,1)S(1)}, bf16[256,256]{1,0:T(8,128)(2,1)}, u32[]{:S(2)}) copy-start(bf16[256,256]{1,0:T(8,128)(2,1)} %leaf_ref.1) | copy-start | bytes 393220
  4.3 11.7 %copy-start.5 = (s32[256,32]{0,1:T(8,128)S(1)}, s32[256,32]{0,1:T(8,128)}, u32[]{:S(2)}) copy-start(s32[256,32]{0,1:T(8,128)} %param.16) | copy-start | bytes 98308
  4.3 11.7 %copy-start.6 = (s32[256,32]{0,1:T(8,128)S(1)}, s32[256,32]{0,1:T(8,128)}, u32[]{:S(2)}) copy-start(s32[256,32]{0,1:T(8,128)} %param.17) | copy-start | bytes 98308
  4.3 11.7 %copy-start.7 = (s32[32,32]{1,0:T(8,128)S(1)}, s32[32,32]{1,0:T(8,128)}, u32[]{:S(2)}) copy-start(s32[32,32]{1,0:T(8,128)} %par_src_hbm.1) | copy-start | bytes 12292
  4.3 11.7 %copy-start.8 = (s32[32,32]{1,0:T(8,128)S(1)}, s32[32,32]{1,0:T(8,128)}, u32[]{:S(2)}) copy-start(s32[32,32]{1,0:T(8,128)} %par_cls_hbm.1) | copy-start | bytes 12292
  4.3 11.7 %copy-start.9 = (s32[64,32]{0,1:T(8,128)S(1)}, s32[64,32]{0,1:T(8,128)}, u32[]{:S(2)}) copy-start(s32[64,32]{0,1:T(8,128)} %param.22) | copy-start | bytes 24580
  4.3 11.7 %copy-start.10 = (s32[64,32]{0,1:T(8,128)S(1)}, s32[64,32]{0,1:T(8,128)}, u32[]{:S(2)}) copy-start(s32[64,32]{0,1:T(8,128)} %param.23) | copy-start | bytes 24580
  4.4 23.9 %all-to-all-start = ((bf16[16,32,256]{2,1,0:T(8,128)(2,1)}), bf16[16,32,256]{2,1,0:T(8,128)(2,1)S(1)}, u32[]{:S(2)}, u32[]{:S(2)}) async-start(bf16[16,32,256]{2,1,0:T(8,128)(2,1)} %get-tuple-element.22), calls=%async_computation | async-start | bytes 524288 | tf_op jit(solution)/shard_map/all_to_all | solution.py:458
  16.0 11.1 %copy-start.3 = (f32[8,3,128]{2,0,1:T(8,128)S(1)}, f32[8,3,128]{2,0,1:T(8,128)}, u32[]{:S(2)}) copy-start(f32[8,3,128]{2,0,1:T(8,128)} %param.24) | copy-start | bytes 36868
  16.0 11.1 %copy-start.4 = (f32[8,128]{1,0:T(8,128)S(1)}, f32[8,128]{1,0:T(8,128)}, u32[]{:S(2)}) copy-start(f32[8,128]{1,0:T(8,128)} %charges_ref.1) | copy-start | bytes 12292
  16.0 11.1 %copy-start.11 = (s32[8,8]{1,0:T(8,128)S(1)}, s32[8,8]{1,0:T(8,128)}, u32[]{:S(2)}) copy-start(s32[8,8]{1,0:T(8,128)} %list_ref.3) | copy-start | bytes 772
  20.3 10.7 %collective-permute-start.1 = (bf16[32,256]{1,0:T(8,128)(2,1)S(1)}, bf16[32,256]{1,0:T(8,128)(2,1)S(1)}, u32[]{:S(2)}, u32[]{:S(2)}) collective-permute-start(bf16[32,256]{1,0:T(8,128)(2,1)S(1)} %get-tuple-element.17.parents_ref), channel_id=1, source_target_pairs={{0,16},{16,32},{32,48},{48,64},{64,80},{80,96},{96,112},{112,128},... | collective-permute-start | bytes 49160 | tf_op jit(solution)/shard_map/ppermute | solution.py:440
  22.2 8.7 %collective-permute-start.2 = (bf16[32,256]{1,0:T(8,128)(2,1)S(1)}, bf16[32,256]{1,0:T(8,128)(2,1)S(1)}, u32[]{:S(2)}, u32[]{:S(2)}) collective-permute-start(bf16[32,256]{1,0:T(8,128)(2,1)S(1)} %get-tuple-element.17.parents_ref), channel_id=1, source_target_pairs={{16,0},{32,16},{48,32},{64,48},{80,64},{96,80},{112,96},{128,112},... | collective-permute-start | bytes 49160 | tf_op jit(solution)/shard_map/ppermute | solution.py:440
  27.1 1.2 %copy-start.1 = (bf16[8,256,256]{2,1,0:T(8,128)(2,1)S(1)}, bf16[8,256,256]{2,1,0:T(8,128)(2,1)}, u32[]{:S(2)}) copy-start(bf16[8,256,256]{2,1,0:T(8,128)(2,1)} %l2l_ref.3) | copy-start | bytes 3145732

commit v5 on v3

--- a/solution.py
+++ b/solution.py
@@ -12,7 +12,6 @@
 HALO_T = 4
 SOFTENING = 0.05
 VMEM_LIMIT = 10 * 1024 * 1024
-PACK_VMEM = 60 * 1024 * 1024
 
 
 def iota(shape, dim):
@@ -64,8 +63,8 @@
 
 
 def pack_kernel(
-    leaf_hbm, m2m_hbm, rows_hbm, count_hbm, points_hbm, charges_hbm, send_hbm, parents_hbm, edge_hbm,
-    leaf_ref, m2m_ref, rows_ref, count_ref, points_ref, charges_ref, leaf_s, parents_s, send_ref, parents_ref, edge_ref, sems,
+    leaf_hbm, m2m_hbm, rows_hbm, count_hbm, points_hbm, charges_hbm, send_ref, up_ref, down_ref,
+    leaf_ref, m2m_ref, rows_ref, count_ref, points_ref, charges_ref, leaf_s, parents_s, sems,
 ):
     me = lax.axis_index("gy")
     pairs = (
@@ -90,32 +89,25 @@
     pick = (iota((128, 256), 1).astype(F32) == column).astype(F32).astype(BF16)
     sent = dot(pick, leaf)
     parts = [pieces(x) for x in (points_ref[0], points_ref[1], points_ref[2], charges_ref[...])]
-    edge_ref[0:3] = points_ref[...]
-    edge_ref[3] = charges_ref[...]
     first = tile_rows(parts, 0)
     last = tile_rows(parts, 8 - HALO_T)
     for p in range(16):
         tiles = jnp.where(me + 1 == p, last, jnp.where(me - 1 == p, first, 0.0))
         send_ref[p, 16:32, :] = tiles.astype(BF16)
-    stores = fetch([
-        pltpu.make_async_copy(edge_ref, edge_hbm, sems.at[6]),
-        pltpu.make_async_copy(send_ref.at[:, 16:32, :], send_hbm.at[:, 16:32, :], sems.at[7]),
-    ])
+    up_ref[32:48, :] = last.astype(BF16)
+    down_ref[32:48, :] = first.astype(BF16)
     copies[5].wait()
     operators = m2m_ref[...].reshape(2048, 256)
     children = jnp.concatenate([every_eighth(leaf_s, c, 32) for c in range(8)], axis=1)
     parents = dot(children.astype(BF16), operators).astype(BF16)
-    parents_ref[...] = parents
-    stores += fetch([pltpu.make_async_copy(parents_ref, parents_hbm, sems.at[8])])
+    up_ref[0:32, :] = parents
+    down_ref[0:32, :] = parents
     for half in range(2):
         parents_s[half, 0:32, :] = parents[:, 128 * half : 128 * half + 128].astype(F32)
     children = jnp.concatenate([every_eighth(parents_s, c, 8) for c in range(8)], axis=1)
     top = dot(children.astype(BF16), operators)
     for p in range(16):
         send_ref[p, 0:16, :] = jnp.concatenate([sent[8 * p : 8 * p + 8], top], axis=0).astype(BF16)
-    stores += fetch([pltpu.make_async_copy(send_ref.at[:, 0:16, :], send_hbm.at[:, 0:16, :], sems.at[9])])
-    for copy in stores:
-        copy.wait()
 
 
 def pack(leaf, m2m, rows, count, points, charges):
@@ -123,11 +115,10 @@
         pack_kernel,
         out_shape=(
             jax.ShapeDtypeStruct((16, 32, 256), BF16),
-            jax.ShapeDtypeStruct((32, 256), BF16),
-            jax.ShapeDtypeStruct((4, 8, 128), F32),
+            jax.ShapeDtypeStruct((48, 256), BF16),
+            jax.ShapeDtypeStruct((48, 256), BF16),
         ),
         in_specs=[pl.BlockSpec(memory_space=pltpu.HBM)] * 6,
-        out_specs=[pl.BlockSpec(memory_space=pltpu.HBM)] * 3,
         scratch_shapes=[
             pltpu.VMEM((256, 256), BF16),
             pltpu.VMEM((8, 256, 256), BF16),
@@ -137,15 +128,34 @@
             pltpu.VMEM((8, 128), F32),
             pltpu.VMEM((2, 256, 128), F32),
             pltpu.VMEM((2, 64, 128), F32),
-            pltpu.VMEM((16, 32, 256), BF16),
-            pltpu.VMEM((32, 256), BF16),
-            pltpu.VMEM((4, 8, 128), F32),
-            pltpu.SemaphoreType.DMA((10,)),
+            pltpu.SemaphoreType.DMA((6,)),
         ],
-        compiler_params=pltpu.CompilerParams(vmem_limit_bytes=PACK_VMEM),
+        compiler_params=pltpu.CompilerParams(vmem_limit_bytes=VMEM_LIMIT),
         cost_estimate=pl.CostEstimate(flops=200_000_000, bytes_accessed=1_500_000, transcendentals=0),
         name="pack",
-    )(leaf, m2m, rows, count, points, charges)
+    )(*[pltpu.with_memory_space_constraint(x, pltpu.HBM) for x in (leaf, m2m, rows, count, points, charges)])
+
+
+def ends_kernel(send_ref, before_ref, after_ref, out_ref):
+    me = lax.axis_index("gy")
+    out_ref[...] = send_ref[...]
+
+    @pl.when(me == 15)
+    def _():
+        out_ref[0, 16:32, :] = before_ref[32:48, :]
+
+    @pl.when(me == 0)
+    def _():
+        out_ref[15, 16:32, :] = after_ref[32:48, :]
+
+
+def with_ends(send, before, after):
+    return pl.pallas_call(
+        ends_kernel,
+        out_shape=jax.ShapeDtypeStruct((16, 32, 256), BF16),
+        compiler_params=pltpu.CompilerParams(vmem_limit_bytes=VMEM_LIMIT),
+        name="with_ends",
+    )(send, before, after)
 
 
 def fields(src_ref, val_ref, lanes, base, rows):
@@ -172,7 +182,7 @@
 
 
 def lists_kernel(
-    leaf_ref, m2l_ref, before_ref, parents_ref, after_ref, edge_ref, src_hbm, cls_hbm, par_src_hbm, par_cls_hbm, top_src_hbm, top_cls_hbm,
+    leaf_ref, m2l_ref, before_ref, parents_ref, after_ref, src_hbm, cls_hbm, par_src_hbm, par_cls_hbm, top_src_hbm, top_cls_hbm,
     partial_ref, far_ref, par_ref, top_ref,
     src_t, val_t, low_src, low_val, par_src_ref, par_cls_ref, top_src_ref, top_cls_ref, near_w, far_w, z_ref, small_w, par_z, sems,
 ):
@@ -186,7 +196,7 @@
     leaf = leaf_ref[...]
     for k in range(8):
         z_ref[256 * k : 256 * k + 256, :] = dot(leaf, m2l_ref[k]).astype(BF16)
-    bank = jnp.concatenate([before_ref[...], parents_ref[...], after_ref[...]], axis=0)
+    bank = jnp.concatenate([before_ref[0:32, :], parents_ref[0:32, :], after_ref[0:32, :]], axis=0)
     for k in range(8):
         z = dot(bank, m2l_ref[k])
         par_z[128 * k : 128 * k + 128, :] = jnp.concatenate([z, jnp.zeros((32, 256), F32)], axis=0).astype(BF16)
@@ -244,7 +254,7 @@
     par_ref[...] = dot(weights[0:32], par_z[...])
 
 
-def lists(leaf, m2l, before, parents, after, edge, src, cls, par_src, par_cls, top_src, top_cls):
+def lists(leaf, m2l, before, parents, after, src, cls, par_src, par_cls, top_src, top_cls):
     vmem = pl.BlockSpec(memory_space=pltpu.VMEM)
     return pl.pallas_call(
         lists_kernel,
@@ -254,7 +264,7 @@
             jax.ShapeDtypeStruct((32, 256), F32),
             jax.ShapeDtypeStruct((64, 128), BF16),
         ),
-        in_specs=[vmem] * 6 + [pl.BlockSpec(memory_space=pltpu.HBM)] * 6,
+        in_specs=[vmem] * 5 + [pl.BlockSpec(memory_space=pltpu.HBM)] * 6,
         scratch_shapes=[
             pltpu.VMEM((32, 256), I32),
             pltpu.VMEM((32, 256), I32),
@@ -274,7 +284,7 @@
         compiler_params=pltpu.CompilerParams(vmem_limit_bytes=VMEM_LIMIT),
         cost_estimate=pl.CostEstimate(flops=4_000_000_000, bytes_accessed=2_500_000, transcendentals=0),
         name="lists",
-    )(leaf, m2l, before, parents, after, edge, src, cls, par_src, par_cls, top_src, top_cls)
+    )(leaf, m2l, before, parents, after, src, cls, par_src, par_cls, top_src, top_cls)
 
 
 def put_rows(ref, first, count, row, value):
@@ -310,6 +320,12 @@
 
 def side_by_side(ref):
     return jnp.concatenate([ref[32 * s : 32 * s + 32, :] for s in range(8)], axis=1).astype(BF16)
+
+
+def tiles_of(rows):
+    rows = rows.astype(F32)
+    rows = rows[:, 0:128] + rows[:, 128:256]
+    return [rows[4 * i : 4 * i + 4] for i in range(4)]
 
 
 def near_sum(list_ref, target_of, sources, places, charges, total_s):
@@ -368,7 +384,7 @@
 
 
 def finish_kernel(
-    list_ref, target_ref, near_ref, recv_ref, edge_ref, partial_ref, far_ref, par_ref, top_ref, m2l_ref, l2l_ref,
+    list_ref, target_ref, near_ref, recv_ref, partial_ref, far_ref, par_ref, top_ref, m2l_ref, l2l_ref,
     local_ref, near_out_ref, source_s, total_s, far_z, parents_s, leaves_s,
 ):
     me = lax.axis_index("gy")
@@ -388,24 +404,19 @@
     total = partial_ref[...] + dot(far_ref[...], far_z[...])
     local_ref[...] = (total + wide(leaves_s[...])).astype(BF16)
 
-    below = recv_ref[jnp.maximum(me - 1, 0), 16:32, :].astype(F32)
-    above = recv_ref[jnp.minimum(me + 1, 15), 16:32, :].astype(F32)
+    below = tiles_of(recv_ref[(me + 15) % 16, 16:32, :])
+    above = tiles_of(recv_ref[(me + 1) % 16, 16:32, :])
     clear_rows(source_s, 8)
-    charges = []
-    for first, rows, start, end in ((0, below, 4, me == 0), (4, above, 0, me == 15)):
-        rows = rows[:, 0:128] + rows[:, 128:256]
-        xyzq = [
-            jnp.where(end, edge_ref[axis, start : start + 4, :], rows[4 * axis : 4 * axis + 4]) for axis in range(4)
-        ]
-        put_source(source_s, first, 4, xyzq[0:3])
-        charges.append(xyzq[3])
+    put_source(source_s, 0, 4, below[0:3])
+    put_source(source_s, 4, 4, above[0:3])
+    charges = [below[3], above[3]]
     halo = (0, 1, 2, 3, 12, 13, 14, 15)
     near_out_ref[...] = near_ref[...] + near_sum(
         list_ref, lambda t: target_ref[t], side_by_side(source_s), halo, jnp.concatenate(charges, axis=0), total_s
     )
 
 
-def finish(near_src, targets, near, recv, edge, partial, far, par, top, m2l, l2l):
+def finish(near_src, targets, near, recv, partial, far, par, top, m2l, l2l):
     return pl.pallas_call(
         finish_kernel,
         out_shape=(jax.ShapeDtypeStruct((256, 256), BF16), jax.ShapeDtypeStruct((8, 128), F32)),
@@ -419,19 +430,13 @@
         compiler_params=pltpu.CompilerParams(vmem_limit_bytes=VMEM_LIMIT),
         cost_estimate=pl.CostEstimate(flops=3_000_000_000, bytes_accessed=3_500_000, transcendentals=1_000_000),
         name="finish",
-    )(near_src, targets, near, recv, edge, partial, far, par, top, m2l, l2l)
+    )(near_src, targets, near, recv, partial, far, par, top, m2l, l2l)
 
 
 def shifted(block, axis, distance):
     size = lax.axis_size(axis)
     route = [(i, i + distance) for i in range(size) if 0 <= i + distance < size]
     return lax.ppermute(block, axis, route)
-
-
-def across(block):
-    rows, width = lax.axis_size("gx"), lax.axis_size("gy")
-    ends = [(g * width + width - 1, (g + 1) * width) for g in range(rows - 1)]
-    return lax.ppermute(block, ("gx", "gy"), ends + [(b, a) for a, b in ends])
 
 
 def per_device(
@@ -439,19 +444,18 @@
     points, charges, near_src, m2m_ops, m2l_ops, l2l_ops,
 ):
     points = points.transpose(1, 0, 2)
-    sent, parents, edge = pack(
+    sent, up, down = pack(
         leaf_moments, m2m_ops, send_rows[0].transpose(0, 2, 1), send_count[0], points, charges
     )
-    edge = across(edge)
-    before = shifted(parents, "gx", 1)
-    after = shifted(parents, "gx", -1)
-    recv = lax.all_to_all(sent, "gy", 0, 0, tiled=True)
+    before = shifted(up, "gx", 1)
+    after = shifted(down, "gx", -1)
+    recv = lax.all_to_all(with_ends(sent, before, after), "gy", 0, 0, tiled=True)
     partial, far, par, top = lists(
-        leaf_moments, m2l_ops, before, parents, after, edge,
+        leaf_moments, m2l_ops, before, up, after,
         leaf_src.T, leaf_cls.T, par_src, par_cls, top_src.T, top_cls.T,
     )
     near_own, targets = own_tiles(par, near_src, points, charges)
-    return finish(near_src, targets, near_own, recv, edge, partial, far, par, top, m2l_ops, l2l_ops)
+    return finish(near_src, targets, near_own, recv, partial, far, par, top, m2l_ops, l2l_ops)
 
 
 def solution(mesh):

time: 32.3 us -> 32.3 us (level)
  the two profiles are of different devices: /device:TPU:225 before, /device:TPU:384 now
where the time goes in v5:
time: 32.3 us; the launch traced here: 32 us
  starting transfers between devices  12.7 us (39%)
  Pallas kernels  11.1 us (34%)
  waiting for transfers between devices  7.32 us (23%)
  between operations  0.84 us (3%)
    all_to_all x1, starting transfers between devices, per_device(): lax.all_to_all(with_ends(sent, before, after), 'gy', 0, 0, tiled=True)  7.18 us
    ppermute x2, starting transfers between devices, shifted(): return lax.ppermute(block, axis, route)  5.49 us
    ppermute x2, waiting for transfers between devices, shifted(): return lax.ppermute(block, axis, route)  4.42 us
    pallas_call x1, Pallas kernels, lists(): pl.pallas_call(lists_kernel, out_shape=(jax.ShapeDtypeStruct((256, 256),...  4.29 us
    all_to_all x1, waiting for transfers between devices, per_device(): lax.all_to_all(with_ends(sent, before, after), 'gy', 0, 0, tiled=True)  2.9 us
    pallas_call x1, Pallas kernels, finish(): pl.pallas_call(finish_kernel, out_shape=(jax.ShapeDtypeStruct((256, 256),...  2.75 us
    pallas_call x1, Pallas kernels, pack(): pl.pallas_call(pack_kernel, out_shape=(jax.ShapeDtypeStruct((16, 32, 256)...  2.26 us
    pallas_call x1, Pallas kernels, own_tiles(): pl.pallas_call(own_kernel, out_shape=(jax.ShapeDtypeStruct((8, 128), F32)...  1.11 us
  transfers between devices with their start and end apart: 3, of which 2 were waited for; matrix products, arithmetic and copies ran while one was open for 0% of the time, Pallas kernels for 17%

profile of v5, /device:TPU:384, one launch (start us, length us, event | category | flops | bytes accessed | tf_op | source)
XLA Modules:
  0.0 32.0 jit_solution(17796738459910410247)
XLA Ops:
  0.6 0.0 copy-start.3
  0.6 2.3 %pack.1 = (bf16[16,32,256]{2,1,0:T(8,128)(2,1)S(1)}, bf16[48,256]{1,0:T(8,128)(2,1)S(1)}, bf16[48,256]{1,0:T(8,128)(2,1)S(1)}) custom-call(bf16[256,256]{1,0:T(8,128)(2,1)} %leaf_ref.1, bf16[8,256,256]{2,1,0:T(8,128)(2,1)} %m2m_hbm.1, s32[16,8,16]{2,1,0:T(8,128)} %bitcast.15, s32[16,16]{1,0:T(8,128)} %bitcast.16, f32[3,8,128]{2,1,0:T(8,128)} %bitcast.9, ...), custom_call_target="tpu_custom_call" | custom-call | flops 200000000 | bytes 1500000 | tf_op jit(solution)/shard_map/pack/pallas_call | solution.py:114
  2.9 3.6 %collective-permute-start.1 = (bf16[48,256]{1,0:T(8,128)(2,1)S(1)}, bf16[48,256]{1,0:T(8,128)(2,1)S(1)}, u32[]{:S(2)}, u32[]{:S(2)}) collective-permute-start(bf16[48,256]{1,0:T(8,128)(2,1)S(1)} %get-tuple-element.12), channel_id=1, source_target_pairs={{16,0},{32,16},{48,32},{64,48},{80,64},{96,80},{112,96},{128,112},... | collective-permute-start | bytes 73736 | tf_op jit(solution)/shard_map/ppermute | solution.py:439
  6.5 1.9 %collective-permute-start = (bf16[48,256]{1,0:T(8,128)(2,1)S(1)}, bf16[48,256]{1,0:T(8,128)(2,1)S(1)}, u32[]{:S(2)}, u32[]{:S(2)}) collective-permute-start(bf16[48,256]{1,0:T(8,128)(2,1)S(1)} %get-tuple-element.11.parents_ref), channel_id=1, source_target_pairs={{0,16},{16,32},{32,48},{48,64},{64,80},{80,96},{96,112},{112,128},... | collective-permute-start | bytes 73736 | tf_op jit(solution)/shard_map/ppermute | solution.py:439
  8.4 0.0 collective-permute-done.1.after_ref
  8.4 4.4 %collective-permute-done.before_ref = bf16[48,256]{1,0:T(8,128)(2,1)S(1)} collective-permute-done((bf16[48,256]{1,0:T(8,128)(2,1)S(1)}, bf16[48,256]{1,0:T(8,128)(2,1)S(1)}, u32[]{:S(2)}, u32[]{:S(2)}) %collective-permute-start) | collective-permute-done | bytes 24608 | tf_op jit(solution)/shard_map/ppermute | solution.py:439
  12.8 0.7 %with_ends.1 = bf16[16,32,256]{2,1,0:T(8,128)(2,1)} custom-call(bf16[16,32,256]{2,1,0:T(8,128)(2,1)S(1)} %get-tuple-element.16.send_ref, bf16[48,256]{1,0:T(8,128)(2,1)S(1)} %collective-permute-done.before_ref, bf16[48,256]{1,0:T(8,128)(2,1)S(1)} %collective-permute-done.1.after_ref), custom_call_target="tpu_custom_call" | custom-call | tf_op jit(solution)/shard_map/with_ends/pallas_call | solution.py:153
  13.6 0.0 copy-start
  13.6 0.0 copy-start.5
  13.6 0.0 copy-start.6
  13.6 0.0 copy-start.7
  13.6 0.0 copy-start.8
  13.6 0.0 copy-start.9
  13.6 0.0 copy-start.10
  13.6 7.2 %all-to-all-start = ((bf16[16,32,256]{2,1,0:T(8,128)(2,1)}), bf16[16,32,256]{2,1,0:T(8,128)(2,1)S(1)}, u32[]{:S(2)}, u32[]{:S(2)}) async-start(bf16[16,32,256]{2,1,0:T(8,128)(2,1)} %with_ends.1), calls=%async_computation | async-start | bytes 524288 | tf_op jit(solution)/shard_map/all_to_all | solution.py:452
  20.8 0.0 copy-done.3
  20.8 0.0 copy-done
  20.8 0.0 copy-done.5
  20.8 0.0 copy-done.6
  20.8 0.0 copy-done.7
  20.8 0.0 copy-done.8
  20.9 0.0 copy-done.9
  20.9 0.0 copy-done.10
  20.9 0.0 copy-start.1
  20.9 0.0 copy-start.2
  20.9 0.0 copy-start.11
  20.9 4.3 %lists.1 = (f32[256,256]{1,0:T(8,128)S(1)}, bf16[256,1024]{1,0:T(8,128)(2,1)S(1)}, f32[32,256]{1,0:T(8,128)S(1)}, bf16[64,128]{1,0:T(8,128)(2,1)S(1)}) custom-call(bf16[256,256]{1,0:T(8,128)(2,1)S(1)} %copy-done, bf16[8,256,256]{2,1,0:T(8,128)(2,1)S(1)} %copy-done.3, bf16[48,256]{1,0:T(8,128)(2,1)S(1)} %collective-permute-done.before_ref, ...), custom_call_target="tpu_custom_call" | custom-call | flops 4000000000 | bytes 2500000 | tf_op jit(solution)/shard_map/lists/pallas_call | solution.py:259
  25.2 0.0 copy-done.1
  25.2 0.0 copy-done.2
  25.2 0.0 copy-done.11
  25.2 0.0 copy-start.4
  25.3 1.1 %own_tiles.1 = (f32[8,128]{1,0:T(8,128)S(1)}, bf16[8,32,128]{2,1,0:T(8,128)(2,1)S(1)}) custom-call(f32[32,256]{1,0:T(8,128)S(1)} %get-tuple-element.13.after_ref.par_ref, s32[8,8]{1,0:T(8,128)S(1)} %copy-done.11, f32[3,8,128]{2,1,0:T(8,128)S(1)} %bitcast.10, f32[8,128]{1,0:T(8,128)S(1)} %copy-done.2), custom_call_target="tpu_custom_call" | custom-call | flops 2000000000 | bytes 100000 | tf_op jit(solution)/shard_map/own_tiles/pallas_call | solution.py:369
  26.4 2.9 %all-to-all-done.recv_ref = bf16[16,32,256]{2,1,0:T(8,128)(2,1)S(1)} async-done(((bf16[16,32,256]{2,1,0:T(8,128)(2,1)}), bf16[16,32,256]{2,1,0:T(8,128)(2,1)S(1)}, u32[]{:S(2)}, u32[]{:S(2)}) %all-to-all-start) | async-done | bytes 262176 | tf_op jit(solution)/shard_map/all_to_all | solution.py:452
  29.3 0.0 copy-done.4
  29.3 2.8 %finish.1 = (bf16[256,256]{1,0:T(8,128)(2,1)}, f32[8,128]{1,0:T(8,128)}) custom-call(s32[8,8]{1,0:T(8,128)S(1)} %copy-done.11, bf16[8,32,128]{2,1,0:T(8,128)(2,1)S(1)} %get-tuple-element.14.target_ref, f32[8,128]{1,0:T(8,128)S(1)} %get-tuple-element.15.near_ref, bf16[16,32,256]{2,1,0:T(8,128)(2,1)S(1)} %all-to-all-done.recv_ref, ...), custom_call_target="tpu_custom_call" | custom-call | flops 3000000000 | bytes 3500000 | tf_op jit(solution)/shard_map/finish/pallas_call | solution.py:420
Async XLA Ops:
  0.6 20.2 %copy-start.3 = (bf16[8,256,256]{2,1,0:T(8,128)(2,1)S(1)}, bf16[8,256,256]{2,1,0:T(8,128)(2,1)}, u32[]{:S(2)}) copy-start(bf16[8,256,256]{2,1,0:T(8,128)(2,1)} %m2l_ref.3) | copy-start | bytes 3145732
  2.9 5.5 %collective-permute-start.1 = (bf16[48,256]{1,0:T(8,128)(2,1)S(1)}, bf16[48,256]{1,0:T(8,128)(2,1)S(1)}, u32[]{:S(2)}, u32[]{:S(2)}) collective-permute-start(bf16[48,256]{1,0:T(8,128)(2,1)S(1)} %get-tuple-element.12), channel_id=1, source_target_pairs={{16,0},{32,16},{48,32},{64,48},{80,64},{96,80},{112,96},{128,112},... | collective-permute-start | bytes 73736 | tf_op jit(solution)/shard_map/ppermute | solution.py:439
  6.5 6.4 %collective-permute-start = (bf16[48,256]{1,0:T(8,128)(2,1)S(1)}, bf16[48,256]{1,0:T(8,128)(2,1)S(1)}, u32[]{:S(2)}, u32[]{:S(2)}) collective-permute-start(bf16[48,256]{1,0:T(8,128)(2,1)S(1)} %get-tuple-element.11.parents_ref), channel_id=1, source_target_pairs={{0,16},{16,32},{32,48},{48,64},{64,80},{80,96},{96,112},{112,128},... | collective-permute-start | bytes 73736 | tf_op jit(solution)/shard_map/ppermute | solution.py:439
  13.6 7.2 %copy-start = (bf16[256,256]{1,0:T(8,128)(2,1)S(1)}, bf16[256,256]{1,0:T(8,128)(2,1)}, u32[]{:S(2)}) copy-start(bf16[256,256]{1,0:T(8,128)(2,1)} %leaf_ref.1) | copy-start | bytes 393220
  13.6 7.3 %copy-start.5 = (s32[256,32]{0,1:T(8,128)S(1)}, s32[256,32]{0,1:T(8,128)}, u32[]{:S(2)}) copy-start(s32[256,32]{0,1:T(8,128)} %param.16) | copy-start | bytes 98308
  13.6 7.3 %copy-start.6 = (s32[256,32]{0,1:T(8,128)S(1)}, s32[256,32]{0,1:T(8,128)}, u32[]{:S(2)}) copy-start(s32[256,32]{0,1:T(8,128)} %param.17) | copy-start | bytes 98308
  13.6 7.3 %copy-start.7 = (s32[32,32]{1,0:T(8,128)S(1)}, s32[32,32]{1,0:T(8,128)}, u32[]{:S(2)}) copy-start(s32[32,32]{1,0:T(8,128)} %par_src_hbm.1) | copy-start | bytes 12292
  13.6 7.3 %copy-start.8 = (s32[32,32]{1,0:T(8,128)S(1)}, s32[32,32]{1,0:T(8,128)}, u32[]{:S(2)}) copy-start(s32[32,32]{1,0:T(8,128)} %par_cls_hbm.1) | copy-start | bytes 12292
  13.6 7.3 %copy-start.9 = (s32[64,32]{0,1:T(8,128)S(1)}, s32[64,32]{0,1:T(8,128)}, u32[]{:S(2)}) copy-start(s32[64,32]{0,1:T(8,128)} %param.22) | copy-start | bytes 24580
  13.6 7.3 %copy-start.10 = (s32[64,32]{0,1:T(8,128)S(1)}, s32[64,32]{0,1:T(8,128)}, u32[]{:S(2)}) copy-start(s32[64,32]{0,1:T(8,128)} %param.23) | copy-start | bytes 24580
  13.6 15.7 %all-to-all-start = ((bf16[16,32,256]{2,1,0:T(8,128)(2,1)}), bf16[16,32,256]{2,1,0:T(8,128)(2,1)S(1)}, u32[]{:S(2)}, u32[]{:S(2)}) async-start(bf16[16,32,256]{2,1,0:T(8,128)(2,1)} %with_ends.1), calls=%async_computation | async-start | bytes 524288 | tf_op jit(solution)/shard_map/all_to_all | solution.py:452
  20.9 4.3 %copy-start.1 = (f32[8,3,128]{2,0,1:T(8,128)S(1)}, f32[8,3,128]{2,0,1:T(8,128)}, u32[]{:S(2)}) copy-start(f32[8,3,128]{2,0,1:T(8,128)} %param.24) | copy-start | bytes 36868
  20.9 4.3 %copy-start.2 = (f32[8,128]{1,0:T(8,128)S(1)}, f32[8,128]{1,0:T(8,128)}, u32[]{:S(2)}) copy-start(f32[8,128]{1,0:T(8,128)} %charges_ref.1) | copy-start | bytes 12292
  20.9 4.3 %copy-start.11 = (s32[8,8]{1,0:T(8,128)S(1)}, s32[8,8]{1,0:T(8,128)}, u32[]{:S(2)}) copy-start(s32[8,8]{1,0:T(8,128)} %list_ref.3) | copy-start | bytes 772
  25.2 4.0 %copy-start.4 = (bf16[8,256,256]{2,1,0:T(8,128)(2,1)S(1)}, bf16[8,256,256]{2,1,0:T(8,128)(2,1)}, u32[]{:S(2)}) copy-start(bf16[8,256,256]{2,1,0:T(8,128)(2,1)} %l2l_ref.1) | copy-start | bytes 3145732

commit v6 on v5

--- a/solution.py
+++ b/solution.py
@@ -63,8 +63,8 @@
 
 
 def pack_kernel(
-    leaf_hbm, m2m_hbm, rows_hbm, count_hbm, points_hbm, charges_hbm, send_ref, up_ref, down_ref,
-    leaf_ref, m2m_ref, rows_ref, count_ref, points_ref, charges_ref, leaf_s, parents_s, sems,
+    leaf_hbm, m2m_hbm, rows_hbm, count_hbm, points_hbm, charges_hbm, send_ref, up_ref, down_ref, m2m_ref,
+    leaf_ref, rows_ref, count_ref, points_ref, charges_ref, leaf_s, sems,
 ):
     me = lax.axis_index("gy")
     pairs = (
@@ -72,7 +72,6 @@
         (points_hbm, points_ref), (charges_hbm, charges_ref), (m2m_hbm, m2m_ref),
     )
     copies = fetch([pltpu.make_async_copy(a, b, sems.at[i]) for i, (a, b) in enumerate(pairs)])
-    parents_s[:, 32:64, :] = jnp.zeros((2, 32, 128), F32)
     for copy in copies[:5]:
         copy.wait()
     leaf = leaf_ref[...]
@@ -93,7 +92,8 @@
     last = tile_rows(parts, 8 - HALO_T)
     for p in range(16):
         tiles = jnp.where(me + 1 == p, last, jnp.where(me - 1 == p, first, 0.0))
-        send_ref[p, 16:32, :] = tiles.astype(BF16)
+        rows = jnp.concatenate([sent[8 * p : 8 * p + 8], jnp.zeros((8, 256), F32), tiles], axis=0)
+        send_ref[p] = rows.astype(BF16)
     up_ref[32:48, :] = last.astype(BF16)
     down_ref[32:48, :] = first.astype(BF16)
     copies[5].wait()
@@ -102,12 +102,6 @@
     parents = dot(children.astype(BF16), operators).astype(BF16)
     up_ref[0:32, :] = parents
     down_ref[0:32, :] = parents
-    for half in range(2):
-        parents_s[half, 0:32, :] = parents[:, 128 * half : 128 * half + 128].astype(F32)
-    children = jnp.concatenate([every_eighth(parents_s, c, 8) for c in range(8)], axis=1)
-    top = dot(children.astype(BF16), operators)
-    for p in range(16):
-        send_ref[p, 0:16, :] = jnp.concatenate([sent[8 * p : 8 * p + 8], top], axis=0).astype(BF16)
 
 
 def pack(leaf, m2m, rows, count, points, charges):
@@ -117,17 +111,16 @@
             jax.ShapeDtypeStruct((16, 32, 256), BF16),
             jax.ShapeDtypeStruct((48, 256), BF16),
             jax.ShapeDtypeStruct((48, 256), BF16),
+            jax.ShapeDtypeStruct((8, 256, 256), BF16),
         ),
         in_specs=[pl.BlockSpec(memory_space=pltpu.HBM)] * 6,
         scratch_shapes=[
             pltpu.VMEM((256, 256), BF16),
-            pltpu.VMEM((8, 256, 256), BF16),
             pltpu.VMEM((8, 16), I32),
             pltpu.VMEM((16, 16), I32),
             pltpu.VMEM((3, 8, 128), F32),
             pltpu.VMEM((8, 128), F32),
             pltpu.VMEM((2, 256, 128), F32),
-            pltpu.VMEM((2, 64, 128), F32),
             pltpu.SemaphoreType.DMA((6,)),
         ],
         compiler_params=pltpu.CompilerParams(vmem_limit_bytes=VMEM_LIMIT),
@@ -136,9 +129,31 @@
     )(*[pltpu.with_memory_space_constraint(x, pltpu.HBM) for x in (leaf, m2m, rows, count, points, charges)])
 
 
-def ends_kernel(send_ref, before_ref, after_ref, out_ref):
+def tops_kernel(up_ref, m2m_ref, top_ref, parents_s):
+    parents = up_ref[0:32, :].astype(F32)
+    for half in range(2):
+        parents_s[half, 0:32, :] = parents[:, 128 * half : 128 * half + 128]
+        parents_s[half, 32:64, :] = jnp.zeros((32, 128), F32)
+    children = jnp.concatenate([every_eighth(parents_s, c, 8) for c in range(8)], axis=1)
+    top_ref[...] = dot(children.astype(BF16), m2m_ref[...].reshape(2048, 256))
+
+
+def tops(up, m2m):
+    return pl.pallas_call(
+        tops_kernel,
+        out_shape=jax.ShapeDtypeStruct((8, 256), F32),
+        scratch_shapes=[pltpu.VMEM((2, 64, 128), F32)],
+        compiler_params=pltpu.CompilerParams(vmem_limit_bytes=VMEM_LIMIT),
+        cost_estimate=pl.CostEstimate(flops=100_000_000, bytes_accessed=1_100_000, transcendentals=0),
+        name="tops",
+    )(up, m2m)
+
+
+def ends_kernel(send_ref, top_ref, before_ref, after_ref, out_ref):
     me = lax.axis_index("gy")
-    out_ref[...] = send_ref[...]
+    top = jnp.concatenate([jnp.zeros((8, 256), F32), top_ref[...], jnp.zeros((16, 256), F32)], axis=0).astype(BF16)
+    for p in range(16):
+        out_ref[p] = send_ref[p] + top
 
     @pl.when(me == 15)
     def _():
@@ -149,13 +164,13 @@
         out_ref[15, 16:32, :] = after_ref[32:48, :]
 
 
-def with_ends(send, before, after):
+def with_ends(send, top, before, after):
     return pl.pallas_call(
         ends_kernel,
         out_shape=jax.ShapeDtypeStruct((16, 32, 256), BF16),
         compiler_params=pltpu.CompilerParams(vmem_limit_bytes=VMEM_LIMIT),
         name="with_ends",
-    )(send, before, after)
+    )(send, top, before, after)
 
 
 def fields(src_ref, val_ref, lanes, base, rows):
@@ -444,12 +459,12 @@
     points, charges, near_src, m2m_ops, m2l_ops, l2l_ops,
 ):
     points = points.transpose(1, 0, 2)
-    sent, up, down = pack(
+    sent, up, down, m2m = pack(
         leaf_moments, m2m_ops, send_rows[0].transpose(0, 2, 1), send_count[0], points, charges
     )
     before = shifted(up, "gx", 1)
     after = shifted(down, "gx", -1)
-    recv = lax.all_to_all(with_ends(sent, before, after), "gy", 0, 0, tiled=True)
+    recv = lax.all_to_all(with_ends(sent, tops(up, m2m), before, after), "gy", 0, 0, tiled=True)
     partial, far, par, top = lists(
         leaf_moments, m2l_ops, before, up, after,
         leaf_src.T, leaf_cls.T, par_src, par_cls, top_src.T, top_cls.T,

time: 32.3 us -> 31.8 us (0.985)
    pallas_call x1, Pallas kernels: 2.26 us -> 1.75 us  [pack(): pl.pallas_call(pack_kernel, out_shape=(jax.ShapeDtypeStruct((16, 32, 256)...]
  transfers between devices with their start and end apart: 3 -> 3, of which waited for: 2 -> 2; matrix products, arithmetic and copies ran while one was open for 0% -> 0% of each run, Pallas kernels for 17% -> 18%
where the time goes in v6:
time: 31.8 us; the launch traced here: 31.5 us
  starting transfers between devices  12.7 us (40%)
  Pallas kernels  10.9 us (34%)
  waiting for transfers between devices  7.07 us (22%)
  between operations  0.83 us (3%)
    all_to_all x1, starting transfers between devices, per_device(): lax.all_to_all(with_ends(sent, tops(up, m2m), before, after), 'gy', 0, 0,...  7.18 us
    ppermute x2, starting transfers between devices, shifted(): return lax.ppermute(block, axis, route)  5.49 us
    pallas_call x1, Pallas kernels, lists(): pl.pallas_call(lists_kernel, out_shape=(jax.ShapeDtypeStruct((256, 256),...  4.3 us
    ppermute x2, waiting for transfers between devices, shifted(): return lax.ppermute(block, axis, route)  4.17 us
    all_to_all x1, waiting for transfers between devices, per_device(): lax.all_to_all(with_ends(sent, tops(up, m2m), before, after), 'gy', 0, 0,...  2.9 us
    pallas_call x1, Pallas kernels, finish(): pl.pallas_call(finish_kernel, out_shape=(jax.ShapeDtypeStruct((256, 256),...  2.77 us
    pallas_call x1, Pallas kernels, pack(): pl.pallas_call(pack_kernel, out_shape=(jax.ShapeDtypeStruct((16, 32, 256)...  1.75 us
    pallas_call x1, Pallas kernels, own_tiles(): pl.pallas_call(own_kernel, out_shape=(jax.ShapeDtypeStruct((8, 128), F32)...  1.1 us
  transfers between devices with their start and end apart: 3, of which 2 were waited for; matrix products, arithmetic and copies ran while one was open for 0% of the time, Pallas kernels for 18%

profile of v6, /device:TPU:384, one launch (start us, length us, event | category | flops | bytes accessed | tf_op | source)
XLA Modules:
  0.0 31.5 jit_solution(1214887974976031010)
XLA Ops:
  0.6 1.7 %pack.1 = (bf16[16,32,256]{2,1,0:T(8,128)(2,1)S(1)}, bf16[48,256]{1,0:T(8,128)(2,1)S(1)}, bf16[48,256]{1,0:T(8,128)(2,1)S(1)}, bf16[8,256,256]{2,1,0:T(8,128)(2,1)S(1)}) custom-call(bf16[256,256]{1,0:T(8,128)(2,1)} %leaf_ref.1, bf16[8,256,256]{2,1,0:T(8,128)(2,1)} %m2m_hbm.1, s32[16,8,16]{2,1,0:T(8,128)} %bitcast.15, s32[16,16]{1,0:T(8,128)} %bitcast.16, ...), custom_call_target="tpu_custom_call" | custom-call | flops 200000000 | bytes 1500000 | tf_op jit(solution)/shard_map/pack/pallas_call | solution.py:108
  2.4 3.6 %collective-permute-start.1 = (bf16[48,256]{1,0:T(8,128)(2,1)S(1)}, bf16[48,256]{1,0:T(8,128)(2,1)S(1)}, u32[]{:S(2)}, u32[]{:S(2)}) collective-permute-start(bf16[48,256]{1,0:T(8,128)(2,1)S(1)} %get-tuple-element.13), channel_id=1, source_target_pairs={{16,0},{32,16},{48,32},{64,48},{80,64},{96,80},{112,96},{128,112},... | collective-permute-start | bytes 73736 | tf_op jit(solution)/shard_map/ppermute | solution.py:454
  6.0 1.9 %collective-permute-start = (bf16[48,256]{1,0:T(8,128)(2,1)S(1)}, bf16[48,256]{1,0:T(8,128)(2,1)S(1)}, u32[]{:S(2)}, u32[]{:S(2)}) collective-permute-start(bf16[48,256]{1,0:T(8,128)(2,1)S(1)} %get-tuple-element.12.parents_ref.up_ref), channel_id=1, source_target_pairs={{0,16},{16,32},{32,48},{48,64},{64,80},{80,96},{96,112},{112,128},... | collective-permute-start | bytes 73736 | tf_op jit(solution)/shard_map/ppermute | solution.py:454
  7.9 0.0 copy-start.3
  7.9 0.2 tops.1.top_ref
  8.1 0.0 collective-permute-done.1.after_ref
  8.2 4.2 %collective-permute-done.before_ref = bf16[48,256]{1,0:T(8,128)(2,1)S(1)} collective-permute-done((bf16[48,256]{1,0:T(8,128)(2,1)S(1)}, bf16[48,256]{1,0:T(8,128)(2,1)S(1)}, u32[]{:S(2)}, u32[]{:S(2)}) %collective-permute-start) | collective-permute-done | bytes 24608 | tf_op jit(solution)/shard_map/ppermute | solution.py:454
  12.3 0.7 %with_ends.1 = bf16[16,32,256]{2,1,0:T(8,128)(2,1)} custom-call(bf16[16,32,256]{2,1,0:T(8,128)(2,1)S(1)} %get-tuple-element.17.send_ref, f32[8,256]{1,0:T(8,128)S(1)} %tops.1.top_ref, bf16[48,256]{1,0:T(8,128)(2,1)S(1)} %collective-permute-done.before_ref, bf16[48,256]{1,0:T(8,128)(2,1)S(1)} %collective-permute-done.1.after_ref), custom_call_target="tpu_custom_call" | custom-call | tf_op jit(solution)/shard_map/with_ends/pallas_call | solution.py:168
  13.0 0.0 copy-start
  13.0 0.0 copy-start.5
  13.0 0.0 copy-start.6
  13.1 0.0 copy-start.7
  13.1 0.0 copy-start.8
  13.1 0.0 copy-start.9
  13.1 0.0 copy-start.10
  13.1 7.2 %all-to-all-start = ((bf16[16,32,256]{2,1,0:T(8,128)(2,1)}), bf16[16,32,256]{2,1,0:T(8,128)(2,1)S(1)}, u32[]{:S(2)}, u32[]{:S(2)}) async-start(bf16[16,32,256]{2,1,0:T(8,128)(2,1)} %with_ends.1), calls=%async_computation | async-start | bytes 524288 | tf_op jit(solution)/shard_map/all_to_all | solution.py:467
  20.3 0.0 copy-done.3
  20.3 0.0 copy-done
  20.3 0.0 copy-done.5
  20.3 0.0 copy-done.6
  20.3 0.0 copy-done.7
  20.3 0.0 copy-done.8
  20.3 0.0 copy-done.9
  20.3 0.0 copy-done.10
  20.4 0.0 copy-start.1
  20.4 0.0 copy-start.2
  20.4 0.0 copy-start.11
  20.4 4.3 %lists.1 = (f32[256,256]{1,0:T(8,128)S(1)}, bf16[256,1024]{1,0:T(8,128)(2,1)S(1)}, f32[32,256]{1,0:T(8,128)S(1)}, bf16[64,128]{1,0:T(8,128)(2,1)S(1)}) custom-call(bf16[256,256]{1,0:T(8,128)(2,1)S(1)} %copy-done, bf16[8,256,256]{2,1,0:T(8,128)(2,1)S(1)} %copy-done.3, bf16[48,256]{1,0:T(8,128)(2,1)S(1)} %collective-permute-done.before_ref, ...), custom_call_target="tpu_custom_call" | custom-call | flops 4000000000 | bytes 2500000 | tf_op jit(solution)/shard_map/lists/pallas_call | solution.py:274
  24.7 0.0 copy-done.1
  24.7 0.0 copy-done.2
  24.7 0.0 copy-done.11
  24.7 0.0 copy-start.4
  24.7 1.1 %own_tiles.1 = (f32[8,128]{1,0:T(8,128)S(1)}, bf16[8,32,128]{2,1,0:T(8,128)(2,1)S(1)}) custom-call(f32[32,256]{1,0:T(8,128)S(1)} %get-tuple-element.14.after_ref.par_ref, s32[8,8]{1,0:T(8,128)S(1)} %copy-done.11, f32[3,8,128]{2,1,0:T(8,128)S(1)} %bitcast.10, f32[8,128]{1,0:T(8,128)S(1)} %copy-done.2), custom_call_target="tpu_custom_call" | custom-call | flops 2000000000 | bytes 100000 | tf_op jit(solution)/shard_map/own_tiles/pallas_call | solution.py:384
  25.8 2.9 %all-to-all-done.recv_ref = bf16[16,32,256]{2,1,0:T(8,128)(2,1)S(1)} async-done(((bf16[16,32,256]{2,1,0:T(8,128)(2,1)}), bf16[16,32,256]{2,1,0:T(8,128)(2,1)S(1)}, u32[]{:S(2)}, u32[]{:S(2)}) %all-to-all-start) | async-done | bytes 262176 | tf_op jit(solution)/shard_map/all_to_all | solution.py:467
  28.7 0.0 copy-done.4
  28.8 2.8 %finish.1 = (bf16[256,256]{1,0:T(8,128)(2,1)}, f32[8,128]{1,0:T(8,128)}) custom-call(s32[8,8]{1,0:T(8,128)S(1)} %copy-done.11, bf16[8,32,128]{2,1,0:T(8,128)(2,1)S(1)} %get-tuple-element.15.target_ref, f32[8,128]{1,0:T(8,128)S(1)} %get-tuple-element.16.near_ref, bf16[16,32,256]{2,1,0:T(8,128)(2,1)S(1)} %all-to-all-done.recv_ref, ...), custom_call_target="tpu_custom_call" | custom-call | flops 3000000000 | bytes 3500000 | tf_op jit(solution)/shard_map/finish/pallas_call | solution.py:435
Async XLA Ops:
  2.4 5.8 %collective-permute-start.1 = (bf16[48,256]{1,0:T(8,128)(2,1)S(1)}, bf16[48,256]{1,0:T(8,128)(2,1)S(1)}, u32[]{:S(2)}, u32[]{:S(2)}) collective-permute-start(bf16[48,256]{1,0:T(8,128)(2,1)S(1)} %get-tuple-element.13), channel_id=1, source_target_pairs={{16,0},{32,16},{48,32},{64,48},{80,64},{96,80},{112,96},{128,112},... | collective-permute-start | bytes 73736 | tf_op jit(solution)/shard_map/ppermute | solution.py:454
  6.0 6.4 %collective-permute-start = (bf16[48,256]{1,0:T(8,128)(2,1)S(1)}, bf16[48,256]{1,0:T(8,128)(2,1)S(1)}, u32[]{:S(2)}, u32[]{:S(2)}) collective-permute-start(bf16[48,256]{1,0:T(8,128)(2,1)S(1)} %get-tuple-element.12.parents_ref.up_ref), channel_id=1, source_target_pairs={{0,16},{16,32},{32,48},{48,64},{64,80},{80,96},{96,112},{112,128},... | collective-permute-start | bytes 73736 | tf_op jit(solution)/shard_map/ppermute | solution.py:454
  7.9 12.4 %copy-start.3 = (bf16[8,256,256]{2,1,0:T(8,128)(2,1)S(1)}, bf16[8,256,256]{2,1,0:T(8,128)(2,1)}, u32[]{:S(2)}) copy-start(bf16[8,256,256]{2,1,0:T(8,128)(2,1)} %m2l_ref.3) | copy-start | bytes 3145732
  13.0 7.2 %copy-start = (bf16[256,256]{1,0:T(8,128)(2,1)S(1)}, bf16[256,256]{1,0:T(8,128)(2,1)}, u32[]{:S(2)}) copy-start(bf16[256,256]{1,0:T(8,128)(2,1)} %leaf_ref.1) | copy-start | bytes 393220
  13.0 7.3 %copy-start.5 = (s32[256,32]{0,1:T(8,128)S(1)}, s32[256,32]{0,1:T(8,128)}, u32[]{:S(2)}) copy-start(s32[256,32]{0,1:T(8,128)} %param.16) | copy-start | bytes 98308
  13.0 7.3 %copy-start.6 = (s32[256,32]{0,1:T(8,128)S(1)}, s32[256,32]{0,1:T(8,128)}, u32[]{:S(2)}) copy-start(s32[256,32]{0,1:T(8,128)} %param.17) | copy-start | bytes 98308
  13.1 7.3 %copy-start.7 = (s32[32,32]{1,0:T(8,128)S(1)}, s32[32,32]{1,0:T(8,128)}, u32[]{:S(2)}) copy-start(s32[32,32]{1,0:T(8,128)} %par_src_hbm.1) | copy-start | bytes 12292
  13.1 7.3 %copy-start.8 = (s32[32,32]{1,0:T(8,128)S(1)}, s32[32,32]{1,0:T(8,128)}, u32[]{:S(2)}) copy-start(s32[32,32]{1,0:T(8,128)} %par_cls_hbm.1) | copy-start | bytes 12292
  13.1 7.3 %copy-start.9 = (s32[64,32]{0,1:T(8,128)S(1)}, s32[64,32]{0,1:T(8,128)}, u32[]{:S(2)}) copy-start(s32[64,32]{0,1:T(8,128)} %param.22) | copy-start | bytes 24580
  13.1 7.3 %copy-start.10 = (s32[64,32]{0,1:T(8,128)S(1)}, s32[64,32]{0,1:T(8,128)}, u32[]{:S(2)}) copy-start(s32[64,32]{0,1:T(8,128)} %param.23) | copy-start | bytes 24580
  13.1 15.7 %all-to-all-start = ((bf16[16,32,256]{2,1,0:T(8,128)(2,1)}), bf16[16,32,256]{2,1,0:T(8,128)(2,1)S(1)}, u32[]{:S(2)}, u32[]{:S(2)}) async-start(bf16[16,32,256]{2,1,0:T(8,128)(2,1)} %with_ends.1), calls=%async_computation | async-start | bytes 524288 | tf_op jit(solution)/shard_map/all_to_all | solution.py:467
  20.4 4.3 %copy-start.1 = (f32[8,3,128]{2,0,1:T(8,128)S(1)}, f32[8,3,128]{2,0,1:T(8,128)}, u32[]{:S(2)}) copy-start(f32[8,3,128]{2,0,1:T(8,128)} %param.24) | copy-start | bytes 36868
  20.4 4.3 %copy-start.2 = (f32[8,128]{1,0:T(8,128)S(1)}, f32[8,128]{1,0:T(8,128)}, u32[]{:S(2)}) copy-start(f32[8,128]{1,0:T(8,128)} %charges_ref.1) | copy-start | bytes 12292
  20.4 4.3 %copy-start.11 = (s32[8,8]{1,0:T(8,128)S(1)}, s32[8,8]{1,0:T(8,128)}, u32[]{:S(2)}) copy-start(s32[8,8]{1,0:T(8,128)} %list_ref.3) | copy-start | bytes 772
  24.7 4.0 %copy-start.4 = (bf16[8,256,256]{2,1,0:T(8,128)(2,1)S(1)}, bf16[8,256,256]{2,1,0:T(8,128)(2,1)}, u32[]{:S(2)}) copy-start(bf16[8,256,256]{2,1,0:T(8,128)(2,1)} %l2l_ref.1) | copy-start | bytes 3145732

commit v7 on v6

--- a/solution.py
+++ b/solution.py
@@ -413,7 +413,7 @@
         put_every_eighth(parents_s, c, 4, dot(top_local, l2l_ref[c])[0:4])
     for k in range(8):
         far_z[128 * k : 128 * k + 128, :] = dot(leaf_rows, m2l_ref[k]).astype(BF16)
-    parent_local = (par_ref[...] + wide(parents_s[...])).astype(BF16)
+    parent_local = (par_ref[...] + wide(parents_s[:, 0:32, :])).astype(BF16)
     for c in range(8):
         put_every_eighth(leaves_s, c, 32, dot(parent_local, l2l_ref[c]))
     total = partial_ref[...] + dot(far_ref[...], far_z[...])
@@ -436,10 +436,10 @@
         finish_kernel,
         out_shape=(jax.ShapeDtypeStruct((256, 256), BF16), jax.ShapeDtypeStruct((8, 128), F32)),
         scratch_shapes=[
-            pltpu.VMEM((256, 128), F32),
+            pltpu.VMEM((384, 128), F32),
             pltpu.VMEM((1024, 128), F32),
             pltpu.VMEM((1024, 256), BF16),
-            pltpu.VMEM((2, 32, 128), F32),
+            pltpu.VMEM((2, 64, 128), F32),
             pltpu.VMEM((2, 256, 128), F32),
         ],
         compiler_params=pltpu.CompilerParams(vmem_limit_bytes=VMEM_LIMIT),

time: 31.8 us -> 31.8 us (level)
  no operation moved by 1% of the time
where the time goes in v7:
time: 31.8 us; the launch traced here: 31.5 us
  starting transfers between devices  12.7 us (40%)
  Pallas kernels  10.9 us (34%)
  waiting for transfers between devices  7.07 us (22%)
  between operations  0.83 us (3%)
    all_to_all x1, starting transfers between devices, per_device(): lax.all_to_all(with_ends(sent, tops(up, m2m), before, after), 'gy', 0, 0,...  7.18 us
    ppermute x2, starting transfers between devices, shifted(): return lax.ppermute(block, axis, route)  5.49 us
    pallas_call x1, Pallas kernels, lists(): pl.pallas_call(lists_kernel, out_shape=(jax.ShapeDtypeStruct((256, 256),...  4.3 us
    ppermute x2, waiting for transfers between devices, shifted(): return lax.ppermute(block, axis, route)  4.17 us
    all_to_all x1, waiting for transfers between devices, per_device(): lax.all_to_all(with_ends(sent, tops(up, m2m), before, after), 'gy', 0, 0,...  2.9 us
    pallas_call x1, Pallas kernels, finish(): pl.pallas_call(finish_kernel, out_shape=(jax.ShapeDtypeStruct((256, 256),...  2.77 us
    pallas_call x1, Pallas kernels, pack(): pl.pallas_call(pack_kernel, out_shape=(jax.ShapeDtypeStruct((16, 32, 256)...  1.75 us
    pallas_call x1, Pallas kernels, own_tiles(): pl.pallas_call(own_kernel, out_shape=(jax.ShapeDtypeStruct((8, 128), F32)...  1.1 us
  transfers between devices with their start and end apart: 3, of which 2 were waited for; matrix products, arithmetic and copies ran while one was open for 0% of the time, Pallas kernels for 18%

profile of v7, /device:TPU:384, one launch (start us, length us, event | category | flops | bytes accessed | tf_op | source)
XLA Modules:
  0.0 31.5 jit_solution(3040908462199471006)
XLA Ops:
  0.6 1.7 %pack.1 = (bf16[16,32,256]{2,1,0:T(8,128)(2,1)S(1)}, bf16[48,256]{1,0:T(8,128)(2,1)S(1)}, bf16[48,256]{1,0:T(8,128)(2,1)S(1)}, bf16[8,256,256]{2,1,0:T(8,128)(2,1)S(1)}) custom-call(bf16[256,256]{1,0:T(8,128)(2,1)} %leaf_ref.1, bf16[8,256,256]{2,1,0:T(8,128)(2,1)} %m2m_hbm.1, s32[16,8,16]{2,1,0:T(8,128)} %bitcast.15, s32[16,16]{1,0:T(8,128)} %bitcast.16, ...), custom_call_target="tpu_custom_call" | custom-call | flops 200000000 | bytes 1500000 | tf_op jit(solution)/shard_map/pack/pallas_call | solution.py:108
  2.4 3.6 %collective-permute-start.1 = (bf16[48,256]{1,0:T(8,128)(2,1)S(1)}, bf16[48,256]{1,0:T(8,128)(2,1)S(1)}, u32[]{:S(2)}, u32[]{:S(2)}) collective-permute-start(bf16[48,256]{1,0:T(8,128)(2,1)S(1)} %get-tuple-element.13), channel_id=1, source_target_pairs={{16,0},{32,16},{48,32},{64,48},{80,64},{96,80},{112,96},{128,112},... | collective-permute-start | bytes 73736 | tf_op jit(solution)/shard_map/ppermute | solution.py:454
  6.0 1.9 %collective-permute-start = (bf16[48,256]{1,0:T(8,128)(2,1)S(1)}, bf16[48,256]{1,0:T(8,128)(2,1)S(1)}, u32[]{:S(2)}, u32[]{:S(2)}) collective-permute-start(bf16[48,256]{1,0:T(8,128)(2,1)S(1)} %get-tuple-element.12.parents_ref.up_ref), channel_id=1, source_target_pairs={{0,16},{16,32},{32,48},{48,64},{64,80},{80,96},{96,112},{112,128},... | collective-permute-start | bytes 73736 | tf_op jit(solution)/shard_map/ppermute | solution.py:454
  7.9 0.0 copy-start.3
  7.9 0.2 tops.1.top_ref
  8.1 0.0 collective-permute-done.1.after_ref
  8.2 4.2 %collective-permute-done.before_ref = bf16[48,256]{1,0:T(8,128)(2,1)S(1)} collective-permute-done((bf16[48,256]{1,0:T(8,128)(2,1)S(1)}, bf16[48,256]{1,0:T(8,128)(2,1)S(1)}, u32[]{:S(2)}, u32[]{:S(2)}) %collective-permute-start) | collective-permute-done | bytes 24608 | tf_op jit(solution)/shard_map/ppermute | solution.py:454
  12.3 0.7 %with_ends.1 = bf16[16,32,256]{2,1,0:T(8,128)(2,1)} custom-call(bf16[16,32,256]{2,1,0:T(8,128)(2,1)S(1)} %get-tuple-element.17.send_ref, f32[8,256]{1,0:T(8,128)S(1)} %tops.1.top_ref, bf16[48,256]{1,0:T(8,128)(2,1)S(1)} %collective-permute-done.before_ref, bf16[48,256]{1,0:T(8,128)(2,1)S(1)} %collective-permute-done.1.after_ref), custom_call_target="tpu_custom_call" | custom-call | tf_op jit(solution)/shard_map/with_ends/pallas_call | solution.py:168
  13.0 0.0 copy-start
  13.0 0.0 copy-start.5
  13.0 0.0 copy-start.6
  13.1 0.0 copy-start.7
  13.1 0.0 copy-start.8
  13.1 0.0 copy-start.9
  13.1 0.0 copy-start.10
  13.1 7.2 %all-to-all-start = ((bf16[16,32,256]{2,1,0:T(8,128)(2,1)}), bf16[16,32,256]{2,1,0:T(8,128)(2,1)S(1)}, u32[]{:S(2)}, u32[]{:S(2)}) async-start(bf16[16,32,256]{2,1,0:T(8,128)(2,1)} %with_ends.1), calls=%async_computation | async-start | bytes 524288 | tf_op jit(solution)/shard_map/all_to_all | solution.py:467
  20.3 0.0 copy-done.3
  20.3 0.0 copy-done
  20.3 0.0 copy-done.5
  20.3 0.0 copy-done.6
  20.3 0.0 copy-done.7
  20.3 0.0 copy-done.8
  20.3 0.0 copy-done.9
  20.3 0.0 copy-done.10
  20.4 0.0 copy-start.1
  20.4 0.0 copy-start.2
  20.4 0.0 copy-start.11
  20.4 4.3 %lists.1 = (f32[256,256]{1,0:T(8,128)S(1)}, bf16[256,1024]{1,0:T(8,128)(2,1)S(1)}, f32[32,256]{1,0:T(8,128)S(1)}, bf16[64,128]{1,0:T(8,128)(2,1)S(1)}) custom-call(bf16[256,256]{1,0:T(8,128)(2,1)S(1)} %copy-done, bf16[8,256,256]{2,1,0:T(8,128)(2,1)S(1)} %copy-done.3, bf16[48,256]{1,0:T(8,128)(2,1)S(1)} %collective-permute-done.before_ref, ...), custom_call_target="tpu_custom_call" | custom-call | flops 4000000000 | bytes 2500000 | tf_op jit(solution)/shard_map/lists/pallas_call | solution.py:274
  24.7 0.0 copy-done.1
  24.7 0.0 copy-done.2
  24.7 0.0 copy-done.11
  24.7 0.0 copy-start.4
  24.7 1.1 %own_tiles.1 = (f32[8,128]{1,0:T(8,128)S(1)}, bf16[8,32,128]{2,1,0:T(8,128)(2,1)S(1)}) custom-call(f32[32,256]{1,0:T(8,128)S(1)} %get-tuple-element.14.after_ref.par_ref, s32[8,8]{1,0:T(8,128)S(1)} %copy-done.11, f32[3,8,128]{2,1,0:T(8,128)S(1)} %bitcast.10, f32[8,128]{1,0:T(8,128)S(1)} %copy-done.2), custom_call_target="tpu_custom_call" | custom-call | flops 2000000000 | bytes 100000 | tf_op jit(solution)/shard_map/own_tiles/pallas_call | solution.py:384
  25.8 2.9 %all-to-all-done.recv_ref = bf16[16,32,256]{2,1,0:T(8,128)(2,1)S(1)} async-done(((bf16[16,32,256]{2,1,0:T(8,128)(2,1)}), bf16[16,32,256]{2,1,0:T(8,128)(2,1)S(1)}, u32[]{:S(2)}, u32[]{:S(2)}) %all-to-all-start) | async-done | bytes 262176 | tf_op jit(solution)/shard_map/all_to_all | solution.py:467
  28.7 0.0 copy-done.4
  28.8 2.8 %finish.1 = (bf16[256,256]{1,0:T(8,128)(2,1)}, f32[8,128]{1,0:T(8,128)}) custom-call(s32[8,8]{1,0:T(8,128)S(1)} %copy-done.11, bf16[8,32,128]{2,1,0:T(8,128)(2,1)S(1)} %get-tuple-element.15.target_ref, f32[8,128]{1,0:T(8,128)S(1)} %get-tuple-element.16.near_ref, bf16[16,32,256]{2,1,0:T(8,128)(2,1)S(1)} %all-to-all-done.recv_ref, ...), custom_call_target="tpu_custom_call" | custom-call | flops 3000000000 | bytes 3500000 | tf_op jit(solution)/shard_map/finish/pallas_call | solution.py:435
Async XLA Ops:
  2.4 5.8 %collective-permute-start.1 = (bf16[48,256]{1,0:T(8,128)(2,1)S(1)}, bf16[48,256]{1,0:T(8,128)(2,1)S(1)}, u32[]{:S(2)}, u32[]{:S(2)}) collective-permute-start(bf16[48,256]{1,0:T(8,128)(2,1)S(1)} %get-tuple-element.13), channel_id=1, source_target_pairs={{16,0},{32,16},{48,32},{64,48},{80,64},{96,80},{112,96},{128,112},... | collective-permute-start | bytes 73736 | tf_op jit(solution)/shard_map/ppermute | solution.py:454
  6.0 6.4 %collective-permute-start = (bf16[48,256]{1,0:T(8,128)(2,1)S(1)}, bf16[48,256]{1,0:T(8,128)(2,1)S(1)}, u32[]{:S(2)}, u32[]{:S(2)}) collective-permute-start(bf16[48,256]{1,0:T(8,128)(2,1)S(1)} %get-tuple-element.12.parents_ref.up_ref), channel_id=1, source_target_pairs={{0,16},{16,32},{32,48},{48,64},{64,80},{80,96},{96,112},{112,128},... | collective-permute-start | bytes 73736 | tf_op jit(solution)/shard_map/ppermute | solution.py:454
  7.9 12.4 %copy-start.3 = (bf16[8,256,256]{2,1,0:T(8,128)(2,1)S(1)}, bf16[8,256,256]{2,1,0:T(8,128)(2,1)}, u32[]{:S(2)}) copy-start(bf16[8,256,256]{2,1,0:T(8,128)(2,1)} %m2l_ref.3) | copy-start | bytes 3145732
  13.0 7.2 %copy-start = (bf16[256,256]{1,0:T(8,128)(2,1)S(1)}, bf16[256,256]{1,0:T(8,128)(2,1)}, u32[]{:S(2)}) copy-start(bf16[256,256]{1,0:T(8,128)(2,1)} %leaf_ref.1) | copy-start | bytes 393220
  13.0 7.3 %copy-start.5 = (s32[256,32]{0,1:T(8,128)S(1)}, s32[256,32]{0,1:T(8,128)}, u32[]{:S(2)}) copy-start(s32[256,32]{0,1:T(8,128)} %param.16) | copy-start | bytes 98308
  13.0 7.3 %copy-start.6 = (s32[256,32]{0,1:T(8,128)S(1)}, s32[256,32]{0,1:T(8,128)}, u32[]{:S(2)}) copy-start(s32[256,32]{0,1:T(8,128)} %param.17) | copy-start | bytes 98308
  13.1 7.3 %copy-start.7 = (s32[32,32]{1,0:T(8,128)S(1)}, s32[32,32]{1,0:T(8,128)}, u32[]{:S(2)}) copy-start(s32[32,32]{1,0:T(8,128)} %par_src_hbm.1) | copy-start | bytes 12292
  13.1 7.3 %copy-start.8 = (s32[32,32]{1,0:T(8,128)S(1)}, s32[32,32]{1,0:T(8,128)}, u32[]{:S(2)}) copy-start(s32[32,32]{1,0:T(8,128)} %par_cls_hbm.1) | copy-start | bytes 12292
  13.1 7.3 %copy-start.9 = (s32[64,32]{0,1:T(8,128)S(1)}, s32[64,32]{0,1:T(8,128)}, u32[]{:S(2)}) copy-start(s32[64,32]{0,1:T(8,128)} %param.22) | copy-start | bytes 24580
  13.1 7.3 %copy-start.10 = (s32[64,32]{0,1:T(8,128)S(1)}, s32[64,32]{0,1:T(8,128)}, u32[]{:S(2)}) copy-start(s32[64,32]{0,1:T(8,128)} %param.23) | copy-start | bytes 24580
  13.1 15.7 %all-to-all-start = ((bf16[16,32,256]{2,1,0:T(8,128)(2,1)}), bf16[16,32,256]{2,1,0:T(8,128)(2,1)S(1)}, u32[]{:S(2)}, u32[]{:S(2)}) async-start(bf16[16,32,256]{2,1,0:T(8,128)(2,1)} %with_ends.1), calls=%async_computation | async-start | bytes 524288 | tf_op jit(solution)/shard_map/all_to_all | solution.py:467
  20.4 4.3 %copy-start.1 = (f32[8,3,128]{2,0,1:T(8,128)S(1)}, f32[8,3,128]{2,0,1:T(8,128)}, u32[]{:S(2)}) copy-start(f32[8,3,128]{2,0,1:T(8,128)} %param.24) | copy-start | bytes 36868
  20.4 4.3 %copy-start.2 = (f32[8,128]{1,0:T(8,128)S(1)}, f32[8,128]{1,0:T(8,128)}, u32[]{:S(2)}) copy-start(f32[8,128]{1,0:T(8,128)} %charges_ref.1) | copy-start | bytes 12292
  20.4 4.3 %copy-start.11 = (s32[8,8]{1,0:T(8,128)S(1)}, s32[8,8]{1,0:T(8,128)}, u32[]{:S(2)}) copy-start(s32[8,8]{1,0:T(8,128)} %list_ref.3) | copy-start | bytes 772
  24.7 4.0 %copy-start.4 = (bf16[8,256,256]{2,1,0:T(8,128)(2,1)S(1)}, bf16[8,256,256]{2,1,0:T(8,128)(2,1)}, u32[]{:S(2)}) copy-start(bf16[8,256,256]{2,1,0:T(8,128)(2,1)} %l2l_ref.1) | copy-start | bytes 3145732
